TPU v7x, 128 devices: a whole 4x4x4 slice. The times are simulated.
128 devices in a mesh: wide: 32 (over y, z, core), narrow: 4 (over x).
Axes of the slice: x: 4, y: 4, z: 4, core: 2. Of those that a mesh axis runs over, the one named last changes fastest.
Arguments:
- tokens: bfloat16 [4096, 2048], P('wide', 'narrow'), may hold values from -6 to 6
- ln_gain: float32 [2048], P('narrow'), may hold values from 0.5 to 1.5
- ln_bias: float32 [2048], P('narrow'), may hold values from -4 to 4
- w_query: bfloat16 [2048, 2048], P('narrow', 'wide'), may hold values from -0.125 to 0.125
- b_query: bfloat16 [2048], P('wide'), may hold values from -4 to 4
- w_key: bfloat16 [2048, 2048], P('narrow', 'wide'), may hold values from -0.125 to 0.125
- b_key: bfloat16 [2048], P('wide'), may hold values from -4 to 4
- w_value: bfloat16 [2048, 2048], P('narrow', 'wide'), may hold values from -0.125 to 0.125
- b_value: bfloat16 [2048], P('wide'), may hold values from -4 to 4
- w_out: bfloat16 [2048, 2048], P('wide', 'narrow'), may hold values from -0.75 to 0.75
- b_out: bfloat16 [2048], P('narrow'), may hold values from -4 to 4
- w_fc1: bfloat16 [2048, 8192], P('narrow', 'wide'), may hold values from -0.125 to 0.125
- b_fc1: bfloat16 [8192], P('wide'), may hold values from -4 to 4
- w_fc2: bfloat16 [8192, 2048], P('wide', 'narrow'), may hold values from -0.0625 to 0.0625
- b_fc2: bfloat16 [2048], P('narrow'), may hold values from -4 to 4
- cotangent: bfloat16 [4096, 2048], P('wide', 'narrow'), may hold values from -6 to 6
- lengths: int32 [2], replicated, may hold values from 1024 to 2048, as said below
- dealing: int32 [32], replicated, may hold values from 0 to 31, as said below
Outputs:
- block_output: bfloat16 [4096, 2048], P('wide', 'narrow')
- input_grad: float32 [4096, 2048], P('wide', 'narrow')
- grad_ln_gain: float32 [2048], P('narrow')
- grad_ln_bias: float32 [2048], P('narrow')
- grad_w_query: float32 [2048, 2048], P('narrow', 'wide')
- grad_b_query: float32 [2048], P('wide')
- grad_w_key: float32 [2048, 2048], P('narrow', 'wide')
- grad_b_key: float32 [2048], P('wide')
- grad_w_value: float32 [2048, 2048], P('narrow', 'wide')
- grad_b_value: float32 [2048], P('wide')
- grad_w_out: float32 [2048, 2048], P('wide', 'narrow')
- grad_b_out: float32 [2048], P('narrow')
- grad_w_fc1: float32 [2048, 8192], P('narrow', 'wide')
- grad_b_fc1: float32 [8192], P('wide')
- grad_w_fc2: float32 [8192, 2048], P('wide', 'narrow')
- grad_b_fc2: float32 [2048], P('narrow')
Inputs may be any that keep to these rules, and one draw needn't show every extreme that they name: `lengths`: each sequence holds at least 1024 tokens; one sequence holds exactly 2048. `dealing`: a permutation of the 32 logical blocks.
All inputs are finite; a program needn't handle non-finite values.
Results may differ from a plain program's by a relative error of at most 0.015.
Values may be sent and summed in bfloat16 or wider, within the bound.
A program may use at most 128 MiB of HBM per device.

v0:
```python
import jax
import jax.numpy as jnp
from jax import lax
from jax.sharding import PartitionSpec as P

D = 2048
HEAD_DIM = 64
ROT = 32
BLOCK = 128
MAXLEN = 2048


epsilon = 1e-05


def rotate(matrix, position, direction):
    halfway = ROT // 2
    inverse_freq = 10000.0 ** (-(jnp.arange(halfway, dtype=jnp.float32) * 2.0 / ROT))
    angles = position.astype(jnp.float32)[:, None] * inverse_freq[None, :]
    cosine = jnp.cos(angles)[:, None, :]
    sine_part = direction * jnp.sin(angles)[:, None, :]
    first_half = matrix[..., :halfway]
    second = matrix[..., halfway:ROT]
    return jnp.concatenate(
        [
            first_half * cosine - second * sine_part,
            second * cosine + first_half * sine_part,
            matrix[..., ROT:],
        ],
        -1,
    )


def block_layout(lengths, dealing):
    per_seq = MAXLEN // BLOCK
    logical = jnp.repeat(dealing, BLOCK)
    offsets = jnp.tile(jnp.arange(BLOCK, dtype=jnp.int32), dealing.shape[0])
    sequence = logical // per_seq
    position = logical % per_seq * BLOCK + offsets
    numbers = jnp.arange(lengths.shape[0], dtype=jnp.int32)
    limits = jnp.sum(jnp.where(sequence[:, None] == numbers[None, :], lengths[None, :], 0), 1)
    return (sequence, position, position < limits)


def smooth(values):
    return jax.nn.gelu(values, approximate=True)


def on_device(
    tokens,
    ln_gain,
    ln_bias,
    w_query,
    b_query,
    w_key,
    b_key,
    w_value,
    b_value,
    w_out,
    b_out,
    w_fc1,
    b_fc1,
    w_fc2,
    b_fc2,
    cotangent,
    lengths,
    dealing,
):
    local_rows = tokens.shape[0]
    total_rows = dealing.shape[0] * BLOCK
    quarter = total_rows // lax.axis_size("narrow")
    head_cols = w_query.shape[1]
    heads_here = head_cols // HEAD_DIM
    scale = HEAD_DIM ** (-0.5)
    block_rows = min(512, quarter)
    block_count = quarter // block_rows
    sequence, position, valid = block_layout(lengths, dealing)
    wide_start = lax.axis_index("wide") * local_rows
    narrow_start = lax.axis_index("narrow") * quarter
    valid_local = lax.dynamic_slice_in_dim(valid, wide_start, local_rows)
    query_seq = lax.dynamic_slice_in_dim(sequence, narrow_start, quarter)
    query_pos = lax.dynamic_slice_in_dim(position, narrow_start, quarter)
    inputs = tokens.astype(jnp.float32)
    row_sums = lax.psum((jnp.sum(inputs, 1), jnp.sum(inputs * inputs, 1)), "narrow")
    row_mean = row_sums[0] / D
    row_var = row_sums[1] / D - row_mean * row_mean
    inv_std = lax.rsqrt(row_var + epsilon)
    normed = (inputs - row_mean[:, None]) * inv_std[:, None]
    ln_low = (normed * ln_gain + ln_bias).astype(jnp.bfloat16)
    ln_all = lax.all_gather(ln_low, "wide", axis=0, tiled=True)
    w_in = jnp.concatenate([w_query, w_key, w_value, w_fc1], 1)
    b_in = jnp.concatenate([b_query, b_key, b_value, b_fc1]).astype(jnp.float32)
    partial_in = jnp.dot(ln_all, w_in, preferred_element_type=jnp.float32)
    summed = lax.psum(partial_in, "narrow") + b_in
    mine = lax.dynamic_slice_in_dim(summed, narrow_start, quarter, 0)
    key_lin = summed[:, head_cols : 2 * head_cols].reshape(total_rows, heads_here, HEAD_DIM)
    key_all = rotate(key_lin, position, 1.0).reshape(total_rows, head_cols).astype(jnp.bfloat16)
    value_all = summed[:, 2 * head_cols : 3 * head_cols].astype(jnp.bfloat16)
    keys_three = key_all.reshape(total_rows, heads_here, HEAD_DIM)
    values_three = value_all.reshape(total_rows, heads_here, HEAD_DIM)
    query_low = rotate(
        mine[:, :head_cols].reshape(quarter, heads_here, HEAD_DIM), query_pos, 1.0
    ).astype(jnp.bfloat16)
    query_blocks = query_low.reshape(block_count, block_rows, heads_here, HEAD_DIM)
    seq_blocks = query_seq.reshape(block_count, block_rows)
    pos_blocks = query_pos.reshape(block_count, block_rows)

    def allowed(rows_seq, rows_pos):
        same = rows_seq[:, None] == sequence[None, :]
        return same & (position[None, :] <= rows_pos[:, None]) & valid[None, :]

    def block_scores(query_blk, blk_seq, blk_pos):
        raw_scores = jnp.einsum(
            "qhd,khd->hqk", query_blk, keys_three, preferred_element_type=jnp.float32
        )
        return jnp.where(allowed(blk_seq, blk_pos)[None], raw_scores * scale, -1e30)

    def attend(args):
        query_blk, blk_seq, blk_pos = args
        scores = block_scores(query_blk, blk_seq, blk_pos)
        maxima = jnp.max(scores, -1, keepdims=True)
        expo = jnp.exp(scores - maxima)
        totals = jnp.sum(expo, -1, keepdims=True)
        probs = (expo / totals).astype(jnp.bfloat16)
        attended = jnp.einsum(
            "hqk,khd->qhd", probs, values_three, preferred_element_type=jnp.float32
        )
        return (attended, (maxima + jnp.log(totals))[..., 0])

    attended, log_totals = lax.map(attend, (query_blocks, seq_blocks, pos_blocks))
    attended_low = attended.reshape(quarter, head_cols).astype(jnp.bfloat16)
    units = mine[:, 3 * head_cols :]
    hidden, gelu_back = jax.vjp(smooth, units)
    hidden_low = hidden.astype(jnp.bfloat16)
    mixed = jnp.concatenate([attended_low, hidden_low], 1)
    mixed_all = lax.all_gather(mixed, "narrow", axis=0, tiled=True)
    w_mix = jnp.concatenate([w_out, w_fc2], 0)
    rows = mixed_all
    branch_sum = lax.psum_scatter(
        jnp.dot(rows, w_mix, preferred_element_type=jnp.float32).astype(jnp.bfloat16),
        "wide",
        scatter_dimension=0,
        tiled=True,
    ).astype(jnp.float32)
    out_bias = b_out.astype(jnp.float32) + b_fc2.astype(jnp.float32)
    result = inputs + valid_local[:, None].astype(jnp.float32) * (branch_sum + out_bias)
    cot_masked = jnp.where(valid_local[:, None], cotangent, jnp.zeros_like(cotangent))
    cot_all = lax.all_gather(cot_masked, "wide", axis=0, tiled=True)
    grad_mix = lax.dot_general(
        mixed_all, cot_all, (((0,), (0,)), ((), ())), preferred_element_type=jnp.float32
    )
    grad_b_out = jnp.sum(cot_all, 0, dtype=jnp.float32)
    rows = cot_all
    grad_mixed = lax.psum_scatter(
        lax.dot_general(rows, w_mix, (((1,), (1,)), ((), ())), preferred_element_type=jnp.float32),
        "narrow",
        scatter_dimension=0,
        tiled=True,
    )
    grad_att = (
        grad_mixed[:, :head_cols]
        .astype(jnp.bfloat16)
        .reshape(block_count, block_rows, heads_here, HEAD_DIM)
    )
    grad_units = gelu_back(grad_mixed[:, head_cols:])[0].astype(jnp.bfloat16)

    def attend_back(carry, args):
        key_acc, value_acc = carry
        query_blk, blk_seq, blk_pos, blk_lse, grad_blk = args
        scores = block_scores(query_blk, blk_seq, blk_pos)
        probs = jnp.exp(scores - blk_lse[..., None])
        probs_low = probs.astype(jnp.bfloat16)
        grad_probs = jnp.einsum(
            "qhd,khd->hqk", grad_blk, values_three, preferred_element_type=jnp.float32
        )
        inner = jnp.sum(probs * grad_probs, -1, keepdims=True)
        grad_raw = (probs * (grad_probs - inner) * scale).astype(jnp.bfloat16)
        grad_query = jnp.einsum(
            "hqk,khd->qhd", grad_raw, keys_three, preferred_element_type=jnp.float32
        )
        key_acc = key_acc + jnp.einsum(
            "hqk,qhd->khd", grad_raw, query_blk, preferred_element_type=jnp.float32
        )
        value_acc = value_acc + jnp.einsum(
            "hqk,qhd->khd", probs_low, grad_blk, preferred_element_type=jnp.float32
        )
        return ((key_acc, value_acc), grad_query)

    zeros_acc = jnp.zeros((total_rows, heads_here, HEAD_DIM), jnp.float32)
    (key_part, value_part), grad_query = lax.scan(
        attend_back,
        (zeros_acc, zeros_acc),
        (query_blocks, seq_blocks, pos_blocks, log_totals, grad_att),
    )
    key_grad, value_grad = (
        lax.psum_scatter(
            key_part.reshape(total_rows, head_cols), "narrow", scatter_dimension=0, tiled=True
        ),
        lax.psum_scatter(
            value_part.reshape(total_rows, head_cols), "narrow", scatter_dimension=0, tiled=True
        ),
    )
    grad_q = (
        rotate(grad_query.reshape(quarter, heads_here, HEAD_DIM), query_pos, -1.0)
        .reshape(quarter, head_cols)
        .astype(jnp.bfloat16)
    )
    grad_k = (
        rotate(key_grad.reshape(quarter, heads_here, HEAD_DIM), query_pos, -1.0)
        .reshape(quarter, head_cols)
        .astype(jnp.bfloat16)
    )
    grad_v = value_grad.astype(jnp.bfloat16)
    grad_pre = jnp.concatenate([grad_q, grad_k, grad_v, grad_units], 1)
    pre_all = lax.all_gather(grad_pre, "narrow", axis=0, tiled=True)
    grad_w_in = lax.dot_general(
        ln_all, pre_all, (((0,), (0,)), ((), ())), preferred_element_type=jnp.float32
    )
    grad_b_in = jnp.sum(pre_all, 0, dtype=jnp.float32)
    rows = pre_all
    grad_ln = lax.psum_scatter(
        lax.dot_general(
            rows, w_in, (((1,), (1,)), ((), ())), preferred_element_type=jnp.float32
        ).astype(jnp.bfloat16),
        "wide",
        scatter_dimension=0,
        tiled=True,
    ).astype(jnp.float32)
    grad_normed = grad_ln * ln_gain
    back_sums = lax.psum((jnp.sum(grad_normed, 1), jnp.sum(grad_normed * normed, 1)), "narrow")
    correction = grad_normed - back_sums[0][:, None] / D - normed * back_sums[1][:, None] / D
    input_grad = cotangent.astype(jnp.float32) + inv_std[:, None] * correction
    gain_sums = lax.psum((jnp.sum(grad_ln * normed, 0), jnp.sum(grad_ln, 0)), "wide")
    cols_two = 2 * head_cols
    cols_three = 3 * head_cols
    return (
        result.astype(jnp.bfloat16),
        input_grad,
        gain_sums[0],
        gain_sums[1],
        grad_w_in[:, :head_cols],
        grad_b_in[:head_cols],
        grad_w_in[:, head_cols:cols_two],
        grad_b_in[head_cols:cols_two],
        grad_w_in[:, cols_two:cols_three],
        grad_b_in[cols_two:cols_three],
        grad_mix[:head_cols],
        grad_b_out,
        grad_w_in[:, cols_three:],
        grad_b_in[cols_three:],
        grad_mix[head_cols:],
        grad_b_out,
    )


def solution(mesh):
    placed = (
        P("wide", "narrow"),
        P("narrow"),
        P("narrow"),
        P("narrow", "wide"),
        P("wide"),
        P("narrow", "wide"),
        P("wide"),
        P("narrow", "wide"),
        P("wide"),
        P("wide", "narrow"),
        P("narrow"),
        P("narrow", "wide"),
        P("wide"),
        P("wide", "narrow"),
        P("narrow"),
        P("wide", "narrow"),
        P(),
        P(),
    )
    return jax.shard_map(
        on_device,
        mesh=mesh,
        in_specs=placed,
        out_specs=(
            P("wide", "narrow"),
            P("wide", "narrow"),
            P("narrow"),
            P("narrow"),
            P("narrow", "wide"),
            P("wide"),
            P("narrow", "wide"),
            P("wide"),
            P("narrow", "wide"),
            P("wide"),
            P("wide", "narrow"),
            P("narrow"),
            P("narrow", "wide"),
            P("wide"),
            P("wide", "narrow"),
            P("narrow"),
        ),
        check_vma=False,
    )
```

profile of v0, /device:TPU:1, one launch (start us, length us, event | category | flops | bytes accessed | tf_op | source)
XLA Modules:
  0.0 695.0 jit_solution(1381232683055143270)
XLA Ops:
  7.2 1.0 convert_reduce_fusion.2
  8.2 9.3 %all-reduce.2 = (f32[128]{0:T(128)S(1)}, f32[128]{0:T(128)S(1)}) all-reduce(f32[128]{0:T(128)S(1)} %get-tuple-element.421, f32[128]{0:T(128)S(1)} %get-tuple-element.420), channel_id=1, replica_groups=mesh['wide'=32,'narrow'=4] {'narrow'}, use_global_device_ids=true, to_apply=%region_4.5 | all-reduce | flops 256 | bytes 2048 | tf_op jit(solution)/shard_map/psum | solution.py:84
  18.1 1.7 fusion.86
  22.0 1.6 broadcast_select_fusion
  23.7 1.0 copy.60
  24.7 1.0 copy.59
  25.7 1.0 copy.58
  26.7 42.3 %all-gather.5.cloned.1.call-done = bf16[4096,512]{1,0:T(8,128)(2,1)} async-done(((bf16[128,512]{1,0:T(8,128)(2,1)}), bf16[4096,512]{1,0:T(8,128)(2,1)}) %all-gather.5.cloned.1.call-update) | async-done | bytes 4194320 | tf_op jit(solution)/shard_map/all_gather | solution.py:90
  69.0 7.4 %fusion.118 = f32[4096,448]{0,1:T(8,128)} fusion(bf16[4096,512]{1,0:T(8,128)(2,1)} %all-gather.5.cloned.1.call-done, bf16[512,256]{1,0:T(8,128)(2,1)} %param.33, bf16[512,64]{1,0:T(8,128)(2,1)S(1)} %copy.60, bf16[512,64]{1,0:T(8,128)(2,1)S(1)} %copy.59, bf16[512,64]{1,0:T(8,128)(2,1)S(1)} %copy.58), kind=kOutput, calls=%fused_computation.186 | convolution fusion | flops 1880883200 | bytes 11993088 | tf_op jit(solution)/shard_map/dot_general | solution.py:93
  77.6 40.0 %all-gather.9.cloned.1.call-done = bf16[4096,512]{1,0:T(8,128)(2,1)} async-done(((bf16[128,512]{1,0:T(8,128)(2,1)}), bf16[4096,512]{1,0:T(8,128)(2,1)}) %all-gather.9.cloned.1.call-update) | async-done | bytes 4194320 | tf_op jit(solution)/shard_map/all_gather | solution.py:148
  117.6 6.1 fusion.137
  123.7 138.9 %all-reduce.5.cloned.1.call-done = f32[4096,448]{0,1:T(8,128)} async-done(((f32[4096,448]{0,1:T(8,128)}), f32[4096,448]{0,1:T(8,128)}) %all-reduce.5.cloned.1.call-update) | async-done | bytes 7340048 | tf_op jit(solution)/shard_map/psum | solution.py:94
  262.7 4.2 broadcast_add_fusion
  267.5 1.1 fusion.78
  268.7 1.2 copy-done.5
  269.9 12.8 %while.31 = (s32[]{:T(128)}, bf16[2,512,1,64]{1,3,2,0:T(8,128)(2,1)S(1)}, f32[2,1,512]{2,1,0:T(1,128)S(1)}, s32[2,512]{1,0:T(2,128)S(1)}, s32[2,512]{1,0:T(2,128...) while((s32[]{:T(128)}, ...), condition=%wide.region_9.10_spmd.clone.clone, body=%wide.region_6.9_spmd.clone.clone.sunk | while | flops 562122240 | bytes 26513668 | solution.py:130
  270.1 2.9 fusion.168
  273.0 1.3 fusion.169
  274.3 2.0 fusion.170
  276.5 2.9 fusion.168
  279.4 1.3 fusion.169
  280.7 2.0 fusion.170
  283.4 37.0 %reduce-scatter.8.cloned.1.call-done = f32[1024,320]{0,1:T(8,128)} async-done(((f32[4096,320]{0,1:T(8,128)}), f32[1024,320]{0,1:T(8,128)}) %reduce-scatter.8.cloned.1.call-update) | async-done | bytes 1310736 | tf_op jit(solution)/shard_map/reduce_scatter | solution.py:154
  320.4 1.0 slice.167
  321.5 61.5 %while.32 = (s32[]{:T(128)}, f32[4096,1,64]{0,2,1:T(8,128)S(1)}, f32[4096,1,64]{0,2,1:T(8,128)S(1)}, f32[2,512,1,64]{1,0,3,2:T(2,128)}, bf16[2,512,1,64]{1,3,2,0...) while((s32[]{:T(128)}, f32[4096,1,64]{0,2,1:T(8,128)S(1)}, ...), condition=%wide.region_14.15_spmd.clone.clone.clone, body=%wide.region_12.14_spmd.clone.clone.clone.sunk | while | flops 1372671488 | bytes 120039840 | solution.py:190
  321.7 1.3 fusion.179
  323.1 6.3 multiply_reduce_fusion.2
  329.4 10.2 %multiply_convert_fusion.3 = bf16[512,4096]{1,0:T(8,128)(2,1)} fusion(f32[512,4096]{1,0:T(8,128)} %get-tuple-element.679, f32[512,4096]{1,0:T(8,128)} %copy-done.1, f32[512]{0:T(512)S(1)} %get-tuple-element.680), kind=kLoop, calls=%fused_computation.37.clone.1 | loop fusion | flops 8388608 | bytes 20973568 | tf_op jit(solution)/shard_map/while/body/eval_jaxpr/convert_element_type | solution.py:177
  339.6 3.1 fusion.180
  342.8 4.5 fusion.181
  347.3 1.4 convolution_bitcast_fusion.4
  348.9 3.5 dynamic_update_slice.25
  352.3 1.3 fusion.179
  353.8 6.3 multiply_reduce_fusion.2
  360.1 10.2 %multiply_convert_fusion.3 = bf16[512,4096]{1,0:T(8,128)(2,1)} fusion(f32[512,4096]{1,0:T(8,128)} %get-tuple-element.679, f32[512,4096]{1,0:T(8,128)} %copy-done.1, f32[512]{0:T(512)S(1)} %get-tuple-element.680), kind=kLoop, calls=%fused_computation.37.clone.1 | loop fusion | flops 8388608 | bytes 20973568 | tf_op jit(solution)/shard_map/while/body/eval_jaxpr/convert_element_type | solution.py:177
  370.3 3.1 fusion.180
  373.4 4.5 fusion.181
  378.0 1.4 convolution_bitcast_fusion.4
  379.5 3.5 dynamic_update_slice.25
  383.0 1.0 copy-done.2
  384.6 1.2 reshape.588
  385.9 2.4 fusion.64
  388.3 17.7 %reduce-scatter.10.cloned.1.call-done = f32[1024,64]{0,1:T(8,128)} async-done(((f32[4096,64]{0,1:T(8,128)}), f32[1024,64]{0,1:T(8,128)}) %reduce-scatter.10.cloned.1.call-update) | async-done | bytes 262160 | tf_op jit(solution)/shard_map/reduce_scatter | solution.py:196
  406.0 0.9 slice.168
  406.9 1.2 fusion.104
  408.2 23.5 %reduce-scatter.12.cloned.1.call-done = f32[1024,64]{0,1:T(8,128)} async-done(((f32[4096,64]{0,1:T(8,128)}), f32[1024,64]{0,1:T(8,128)}) %reduce-scatter.12.cloned.1.call-update) | async-done | bytes 262160 | tf_op jit(solution)/shard_map/reduce_scatter | solution.py:199
  431.7 1.0 convert_element_type.131
  432.6 1.1 pad_maximum_fusion
  434.0 0.9 pad_maximum_fusion.1
  435.1 43.7 %all-gather.11.cloned.1.call-done = bf16[4096,448]{0,1:T(8,128)(2,1)} async-done(((bf16[1024,448]{0,1:T(8,128)(2,1)}), bf16[4096,448]{0,1:T(8,128)(2,1)}) %all-gather.11.cloned.1.call-update) | async-done | bytes 3670032 | tf_op jit(solution)/shard_map/all_gather | solution.py:215
  478.8 6.6 convolution_convert_fusion
  485.5 30.4 %all-gather.7.cloned.1.call-done = bf16[4096,320]{0,1:T(8,128)(2,1)} async-done(((bf16[1024,320]{0,1:T(8,128)(2,1)}), bf16[4096,320]{0,1:T(8,128)(2,1)}) %all-gather.7.cloned.1.call-update) | async-done | bytes 2621456 | tf_op jit(solution)/shard_map/all_gather | solution.py:136
  515.9 6.2 convolution_convert_fusion.1
  522.8 3.0 convert_reduce_fusion
  526.3 3.4 fusion.138
  531.2 2.0 fusion.139
  533.3 1.0 copy.67
  534.3 2.7 convert_reduce_fusion.1
  539.0 61.3 %reduce-scatter.14.cloned.1.call-done = bf16[128,512]{1,0:T(8,128)(2,1)} async-done(((bf16[4096,512]{1,0:T(8,128)(2,1)}), bf16[128,512]{1,0:T(8,128)(2,1)}) %reduce-scatter.14.cloned.1.call-update) | async-done | bytes 131088 | tf_op jit(solution)/shard_map/reduce_scatter | solution.py:221
  600.3 1.1 fusion.81
  601.4 8.4 %all-reduce.1 = (f32[128]{0:T(128)S(1)}, f32[128]{0:T(128)S(1)}) all-reduce(f32[128]{0:T(128)S(1)} %get-tuple-element.417, f32[128]{0:T(128)S(1)} %get-tuple-element.418), channel_id=1, replica_groups=mesh['wide'=32,'narrow'=4] {'narrow'}, use_global_device_ids=true, to_apply=%region_21.22 | all-reduce | flops 256 | bytes 2048 | tf_op jit(solution)/shard_map/psum | solution.py:230
  609.8 67.2 %all-reduce = (f32[512]{0:T(512)}, f32[512]{0:T(512)}) all-reduce(f32[512]{0:T(512)S(1)} %get-tuple-element.416, f32[512]{0:T(512)S(1)} %get-tuple-element.419), channel_id=1, replica_groups=mesh['wide'=32,'narrow'=4] {'wide'}, use_global_device_ids=true, to_apply=%region_23.24 | all-reduce | flops 1024 | bytes 8192 | tf_op jit(solution)/shard_map/psum | solution.py:233
  677.0 8.7 %reduce-scatter.6.cloned.1.call-done = bf16[128,512]{1,0:T(8,128)(2,1)} async-done(((bf16[4096,512]{1,0:T(8,128)(2,1)}), bf16[128,512]{1,0:T(8,128)(2,1)}) %reduce-scatter.6.cloned.1.call-update) | async-done | bytes 131088 | tf_op jit(solution)/shard_map/reduce_scatter | solution.py:139
  685.7 1.9 fusion.75
  (171 shorter events, 12.6 us)
Async XLA Ops:
  7.2 61.9 %all-gather.5.cloned.1.call-start = ((), (), s32[]{:S(2)}) async-start(), calls=%async_computation.5 | async-start | bytes 4325376 | tf_op jit(solution)/shard_map/all_gather | solution.py:90
  17.6 0.5 copy-start.27
  17.6 0.5 copy-start.29
  19.8 97.8 %all-gather.9.cloned.1.call-start = ((), (), s32[]{:S(2)}) async-start(), calls=%async_computation.9 | async-start | bytes 4325376 | tf_op jit(solution)/shard_map/all_gather | solution.py:148
  21.4 55.1 %copy-start.32 = (pred[4096]{0:T(1024)(128)(4,1)}, pred[4096]{0:T(1024)(128)(4,1)S(1)}, u32[]{:S(2)}) copy-start(pred[4096]{0:T(1024)(128)(4,1)S(1)} %lt.24) | copy-start | bytes 12292
  23.7 239.0 %all-reduce.5.cloned.1.call-start = ((), (), s32[]{:S(2)}) async-start(), calls=%async_computation.6 | async-start | bytes 14680064 | tf_op jit(solution)/shard_map/psum | solution.py:94
  24.7 51.8 %copy-start.9 = (bf16[512,64]{1,0:T(8,128)(2,1)}, bf16[512,64]{1,0:T(8,128)(2,1)S(1)}, u32[]{:S(2)}) copy-start(bf16[512,64]{1,0:T(8,128)(2,1)S(1)} %copy.60) | copy-start | bytes 196612
  25.7 50.8 %copy-start.11 = (bf16[512,64]{1,0:T(8,128)(2,1)}, bf16[512,64]{1,0:T(8,128)(2,1)S(1)}, u32[]{:S(2)}) copy-start(bf16[512,64]{1,0:T(8,128)(2,1)S(1)} %copy.59) | copy-start | bytes 196612
  26.7 49.8 %copy-start.13 = (bf16[512,64]{1,0:T(8,128)(2,1)}, bf16[512,64]{1,0:T(8,128)(2,1)S(1)}, u32[]{:S(2)}) copy-start(bf16[512,64]{1,0:T(8,128)(2,1)S(1)} %copy.58) | copy-start | bytes 196612
  76.5 0.7 copy-start.40
  76.5 0.7 copy-start.41
  76.5 0.7 copy-start.42
  76.5 0.7 copy-start.43
  76.5 0.9 copy-start.22
  76.6 1.0 copy-start.19
  76.6 243.8 %reduce-scatter.8.cloned.1.call-start = ((), (), s32[]{:S(2)}) async-start(), calls=%async_computation.10 | async-start | bytes 6553600 | tf_op jit(solution)/shard_map/reduce_scatter | solution.py:154
  76.8 190.4 %copy-start.24 = (f32[1024]{0:T(1024)}, f32[1024]{0:T(1024)S(1)}, u32[]{:S(2)}) copy-start(f32[1024]{0:T(1024)S(1)} %get-tuple-element.478) | copy-start | bytes 12292
  77.2 190.3 %copy-start.35 = (f32[16]{0:T(128)}, f32[16]{0:T(128)S(1)}, u32[]{:S(2)}) copy-start(f32[16]{0:T(128)S(1)} %negate_power_fusion) | copy-start | bytes 196
  77.6 46.1 %copy-start.16 = (bf16[320,512]{1,0:T(8,128)(2,1)}, bf16[320,512]{1,0:T(8,128)(2,1)S(1)}, u32[]{:S(2)}) copy-start(bf16[320,512]{1,0:T(8,128)(2,1)S(1)} %constant_dynamic-update-slice_fusion.1) | copy-start | bytes 983044
  123.7 282.3 %reduce-scatter.10.cloned.1.call-start = ((), (), s32[]{:S(2)}) async-start(), calls=%async_computation.11 | async-start | bytes 1310720 | tf_op jit(solution)/shard_map/reduce_scatter | solution.py:196
  266.9 3.0 copy-start.5
  266.9 3.0 copy-start.23
  266.9 3.0 copy-start.33
  282.8 0.7 copy-start.20
  321.7 1.4 copy-start.34
  323.0 6.5 copy-start.1
  342.8 4.6 copy-start
  352.3 1.4 copy-start.34
  353.6 6.5 copy-start.1
  373.4 4.6 copy-start
  383.0 1.0 copy-start.2
  383.0 1.3 copy-start.3
  383.0 23.9 %copy-start.25 = (f32[1024]{0:T(1024)S(1)}, f32[1024]{0:T(1024)}, u32[]{:S(2)}) copy-start(f32[1024]{0:T(1024)} %copy-done.24) | copy-start | bytes 12292
  383.0 23.9 %copy-start.36 = (f32[16]{0:T(128)S(1)}, f32[16]{0:T(128)}, u32[]{:S(2)}) copy-start(f32[16]{0:T(128)} %copy-done.35) | copy-start | bytes 196
  384.0 47.7 %reduce-scatter.12.cloned.1.call-start = ((), (), s32[]{:S(2)}) async-start(), calls=%async_computation.12 | async-start | bytes 1310720 | tf_op jit(solution)/shard_map/reduce_scatter | solution.py:199
  384.6 49.2 %copy-start.21 = (bf16[2,512,1,64]{1,3,2,0:T(8,128)(2,1)S(1)}, bf16[2,512,1,64]{1,3,2,0:T(8,128)(2,1)}, u32[]{:S(2)}) copy-start(bf16[2,512,1,64]{1,3,2,0:T(8,128)(2,1)} %copy-done.20) | copy-start | bytes 393220
  384.6 94.2 %all-gather.11.cloned.1.call-start = ((), (), s32[]{:S(2)}) async-start(), calls=%async_computation.13 | async-start | bytes 4587520 | tf_op jit(solution)/shard_map/all_gather | solution.py:215
  385.9 92.9 %copy-start.10 = (bf16[512,64]{1,0:T(8,128)(2,1)S(1)}, bf16[512,64]{1,0:T(8,128)(2,1)}, u32[]{:S(2)}) copy-start(bf16[512,64]{1,0:T(8,128)(2,1)} %copy-done.9) | copy-start | bytes 196612
  385.9 92.9 %copy-start.12 = (bf16[512,64]{1,0:T(8,128)(2,1)S(1)}, bf16[512,64]{1,0:T(8,128)(2,1)}, u32[]{:S(2)}) copy-start(bf16[512,64]{1,0:T(8,128)(2,1)} %copy-done.11) | copy-start | bytes 196612
  385.9 92.9 %copy-start.14 = (bf16[512,64]{1,0:T(8,128)(2,1)S(1)}, bf16[512,64]{1,0:T(8,128)(2,1)}, u32[]{:S(2)}) copy-start(bf16[512,64]{1,0:T(8,128)(2,1)} %copy-done.13) | copy-start | bytes 196612
  385.9 92.9 %copy-start.18 = (bf16[512,256]{1,0:T(8,128)(2,1)S(1)}, bf16[512,256]{1,0:T(8,128)(2,1)}, u32[]{:S(2)}) copy-start(bf16[512,256]{1,0:T(8,128)(2,1)} %param.33) | copy-start | bytes 786436
  433.7 82.2 %all-gather.7.cloned.1.call-start = ((), (), s32[]{:S(2)}) async-start(), calls=%async_computation.7 | async-start | bytes 3276800 | tf_op jit(solution)/shard_map/all_gather | solution.py:136
  434.9 165.4 %reduce-scatter.14.cloned.1.call-start = ((), (), s32[]{:S(2)}) async-start(), calls=%async_computation.14 | async-start | bytes 4325376 | tf_op jit(solution)/shard_map/reduce_scatter | solution.py:221
  485.4 30.5 %copy-start.17 = (bf16[320,512]{1,0:T(8,128)(2,1)S(1)}, bf16[320,512]{1,0:T(8,128)(2,1)}, u32[]{:S(2)}) copy-start(bf16[320,512]{1,0:T(8,128)(2,1)} %copy-done.16) | copy-start | bytes 983044
  485.4 200.2 %reduce-scatter.6.cloned.1.call-start = ((), (), s32[]{:S(2)}) async-start(), calls=%async_computation.8 | async-start | bytes 4325376 | tf_op jit(solution)/shard_map/reduce_scatter | solution.py:139
  522.1 0.7 copy-start.38
  522.1 0.7 copy-start.39
  522.8 3.4 copy-start.4
  526.3 161.3 %copy-start.31 = (f32[512]{0:T(512)}, f32[512]{0:T(512)S(1)}, u32[]{:S(2)}) copy-start(f32[512]{0:T(512)S(1)} %convert_reduce_fusion) | copy-start | bytes 6148
  526.3 4.9 copy-start.6
  526.3 4.9 copy-start.7
  533.2 67.1 %copy-start.8 = (bf16[128,512]{1,0:T(8,128)(2,1)S(1)}, bf16[128,512]{1,0:T(8,128)(2,1)}, u32[]{:S(2)}) copy-start(bf16[128,512]{1,0:T(8,128)(2,1)} %param.22) | copy-start | bytes 393220
  533.2 67.1 %copy-start.26 = (f32[512]{0:T(512)S(1)}, f32[512]{0:T(512)}, u32[]{:S(2)}) copy-start(f32[512]{0:T(512)} %param.23) | copy-start | bytes 6148
  533.2 67.1 %copy-start.28 = (f32[128]{0:T(128)S(1)}, f32[128]{0:T(128)}, u32[]{:S(2)}) copy-start(f32[128]{0:T(128)} %copy-done.27) | copy-start | bytes 1540
  533.3 67.1 %copy-start.30 = (f32[128]{0:T(128)S(1)}, f32[128]{0:T(128)}, u32[]{:S(2)}) copy-start(f32[128]{0:T(128)} %copy-done.29) | copy-start | bytes 1540
  533.3 152.4 %copy-start.15 = (bf16[128,512]{1,0:T(8,128)(2,1)S(1)}, bf16[128,512]{1,0:T(8,128)(2,1)}, u32[]{:S(2)}) copy-start(bf16[128,512]{1,0:T(8,128)(2,1)} %param.37) | copy-start | bytes 393220
  533.3 152.4 %copy-start.37 = (f32[128]{0:T(128)S(1)}, f32[128]{0:T(128)}, u32[]{:S(2)}) copy-start(f32[128]{0:T(128)} %get-tuple-element.474) | copy-start | bytes 1540
Sparse Core Ops, SparseCore 0:
  19.9 49.0 all-gather.4
  71.9 45.6 all-gather.8
  120.0 142.6 all-reduce.4
  265.0 55.4 reduce-scatter.7
  384.1 21.8 reduce-scatter.9
  408.4 23.2 reduce-scatter.11
  433.8 44.9 all-gather.10
  480.5 35.4 all-gather.6
  519.6 80.6 reduce-scatter.13
  604.2 81.4 reduce-scatter.5
where the time goes:
time: 697 us; the launch traced here: 695 us
  waiting for transfers between devices  444 us (64%)
  blocking collectives  84.9 us (12%)
  matrix products  75 us (11%)
  other arithmetic  50.8 us (7%)
  local copies, waits for them, and re-layouts  24.6 us (4%)
  between operations  14.8 us (2%)
    psum x1, waiting for transfers between devices, on_device(): summed = lax.psum(partial_in, 'narrow') + b_in  139 us
    psum x1, blocking collectives, on_device(): lax.psum((jnp.sum(grad_ln * normed, 0), jnp.sum(grad_ln, 0)), 'wide')  67.2 us
    reduce_scatter x1, waiting for transfers between devices, on_device(): lax.psum_scatter(lax.dot_general(rows, w_in, (((1,), (1,)), ((), ())), pr...  61.3 us
    all_gather x1, waiting for transfers between devices, on_device(): pre_all = lax.all_gather(grad_pre, 'narrow', axis=0, tiled=True)  43.7 us
    all_gather x1, waiting for transfers between devices, on_device(): ln_all = lax.all_gather(ln_low, 'wide', axis=0, tiled=True)  42.3 us
    all_gather x1, waiting for transfers between devices, on_device(): cot_all = lax.all_gather(cot_masked, 'wide', axis=0, tiled=True)  40 us
    reduce_scatter x1, waiting for transfers between devices, on_device(): lax.psum_scatter(lax.dot_general(rows, w_mix, (((1,), (1,)), ((), ())), p...  37 us
    all_gather x1, waiting for transfers between devices, on_device(): mixed_all = lax.all_gather(mixed, 'narrow', axis=0, tiled=True)  30.4 us
  transfers between devices with their start and end apart: 10, of which 10 were waited for; matrix products, arithmetic and copies ran while one was open for 11% of the time, Pallas kernels for 0%

commit v1 on v0

v1 whole, which is shorter than its diff:
```python
import functools

import jax
import jax.numpy as jnp
import numpy as np
from jax import lax
from jax.experimental import pallas as pl
from jax.experimental.pallas import tpu as pltpu
from jax.sharding import PartitionSpec as P

MESH = pl.DeviceIdType.MESH
D = 2048
HEAD_DIM = 64
ROT = 32
BLOCK = 128
MAXLEN = 2048
NBLK = 32
PART = 32
ROWS = NBLK * PART
COLS = 512
UNITS = 256
EPS = 1e-05
BF16 = jnp.bfloat16
F32 = jnp.float32


def rope_tables():
    half = ROT // 2
    inverse = (10000.0 ** (-(np.arange(half, dtype=np.float32) * np.float32(2.0) / np.float32(ROT)))).astype(np.float32)
    angles = (np.arange(MAXLEN, dtype=np.float32)[:, None] * inverse[None, :]).astype(np.float64)
    cosine = np.ones((MAXLEN, 128), np.float32)
    sine = np.zeros((MAXLEN, 128), np.float32)
    cosine[:, :half] = np.cos(angles)
    cosine[:, half:ROT] = np.cos(angles)
    sine[:, :half] = -np.sin(angles)
    sine[:, half:ROT] = np.sin(angles)
    return cosine, sine


class Net:
    def __init__(self, send, recv):
        self.send, self.recv, self.used, self.open = send, recv, 0, []

    def copy(self, src, dst, device):
        i = self.used
        self.used += 1
        c = pltpu.make_async_remote_copy(
            src_ref=src,
            dst_ref=dst,
            send_sem=self.send.at[i],
            recv_sem=self.recv.at[i],
            device_id=device,
            device_id_type=MESH,
        )
        c.start()
        self.open.append(c)
        return c

    def drain(self):
        for c in self.open:
            c.wait_send()


class Ring:
    def __init__(self, net, me, device, unit, half):
        self.net, self.unit, self.half = net, unit, half
        self.right, self.left = (me + 1) % 4, (me + 3) % 4
        self.to_right, self.to_left = device(self.right), device(self.left)
        self.me = me

    def start(self):
        own = self.unit(self.me)
        self.a = self.net.copy(own, own, self.to_right)
        self.b = self.net.copy(own, own, self.to_left)

    def forward(self):
        self.a.wait_recv()
        x = self.half(self.left, 0)
        self.c = self.net.copy(x, x, self.to_right)
        self.b.wait_recv()
        x = self.half(self.right, 1)
        self.d = self.net.copy(x, x, self.to_left)

    def finish(self):
        self.c.wait_recv()
        self.d.wait_recv()


def coords():
    w, n = lax.axis_index("wide"), lax.axis_index("narrow")
    return w // 8, (w // 2) % 4, w % 2, n


def wide_of(y, z, c):
    return (y * 4 + z) * 2 + c


def aligned(x, m):
    return pl.multiple_of(x, m)


def slot_a(c, z, y):
    return aligned(((c * 4 + z) * 4 + y) * 16, 16)


def slot_b(c, y, z):
    return aligned((32 + (c * 4 + y) * 4 + z) * 16, 16)


class WideGather:
    def __init__(self, net, buf, y, z, c, n):
        self.net, self.buf, self.y, self.z, self.c = net, buf, y, z, c

        def dev(y, z, c):
            return (wide_of(y, z, c), n)

        def rows(start, count):
            return buf.at[pl.ds(start, count)]

        def cols(start, h):
            return buf.at[pl.ds(start, 16), pl.ds(h * 1024, 1024)]

        def half(start, h):
            return buf.at[pl.ds(aligned(start + 32 * h, 16), 32)]

        self.rows = rows
        self.other = dev(y, z, 1 - c)
        self.one = (
            Ring(net, y, lambda i: dev(i, z, c), lambda i: rows(slot_a(c, z, i), 16), lambda i, h: cols(slot_a(c, z, i), h)),
            Ring(net, z, lambda i: dev(y, i, c), lambda i: rows(slot_b(c, y, i), 16), lambda i, h: cols(slot_b(c, y, i), h)),
        )
        self.two = (
            Ring(net, z, lambda i: dev(y, i, c), lambda i: rows(slot_a(c, i, 0), 64), lambda i, h: half(slot_a(c, i, 0), h)),
            Ring(net, y, lambda i: dev(i, z, c), lambda i: rows(slot_b(c, i, 0), 64), lambda i, h: half(slot_b(c, i, 0), h)),
        )
        self.cross = []

    def _cross(self, i):
        for part, slot in ((0, slot_a), (1, slot_b)):
            me = (self.z, self.y)[part]
            x = self.rows(slot(self.c, (me + i) % 4, 0), 64)
            self.cross.append(self.net.copy(x, x, self.other))

    def start(self):
        for r in self.one:
            r.start()

    def forward(self):
        for r in self.one:
            r.forward()

    def second(self):
        for r in self.one:
            r.finish()
        for r in self.two:
            r.start()
        self._cross(0)

    def forward_second(self):
        for r in self.two:
            r.forward()
        self._cross(1)
        self._cross(3)

    def finish(self):
        for r in self.two:
            r.finish()
        self._cross(2)
        for x in self.cross:
            x.wait_recv()


def greet(y, z, c, n):
    peers = [
        (wide_of((y + 1) % 4, z, c), n),
        (wide_of((y + 3) % 4, z, c), n),
        (wide_of(y, (z + 1) % 4, c), n),
        (wide_of(y, (z + 3) % 4, c), n),
        (wide_of(y, z, 1 - c), n),
        (wide_of(y, z, c), (n + 1) % 4),
        (wide_of(y, z, c), (n + 2) % 4),
        (wide_of(y, z, c), (n + 3) % 4),
    ]
    barrier = pltpu.get_barrier_semaphore()
    for p in peers:
        pl.semaphore_signal(barrier, inc=1, device_id=p, device_id_type=MESH)
    pl.semaphore_wait(barrier, len(peers))


def nt(a, b):
    return lax.dot_general(a, b, (((1,), (1,)), ((), ())), preferred_element_type=F32)


GELU_A = float(np.sqrt(2.0 / np.pi))
GELU_B = 0.044715


def first_kernel(
    chunk_ref, tok, cot, wq, wk, wv, wu, wo, wd, gb, bias, cosine, sine,
    ln, g, w, wm, xhat, q_log, do_log, kv, h_out, du_out,
    xs, gbs, pre, qp, dop, u, send, recv, local,
):
    y, z, c, n = coords()
    net = Net(send, recv)
    my_cols = pl.ds(aligned(n * COLS, COLS), COLS)
    my_rows = pl.ds(aligned(n * PART, PART), PART)
    me = wide_of(y, z, c)
    own_a, own_b = slot_a(c, z, y), slot_b(c, y, z)

    w[0:64, my_cols] = wk[...].T
    w[64:128, my_cols] = wv[...].T
    w[128:192, my_cols] = wq[...].T
    w[192:448, my_cols] = wu[...].T
    wm[0:64, my_cols] = wo[...]
    wm[64:320, my_cols] = wd[...]
    gbs[n] = gb[...]
    xs[:, my_cols] = tok[my_rows, :]
    g[pl.ds(own_a, 16), my_cols] = cot[pl.ds(aligned(n * PART, 16), 16), :]
    g[pl.ds(own_b, 16), my_cols] = cot[pl.ds(aligned(n * PART + 16, 16), 16), :]
    greet(y, z, c, n)

    def to(m):
        return (me, m)

    early, late = [], []
    for j in (1, 3, 2):
        m = (n + j) % 4
        early.append(net.copy(gbs.at[n], gbs.at[n], to(m)))
        early.append(net.copy(tok.at[pl.ds(aligned(m * PART, PART), PART)], xs.at[:, my_cols], to(m)))
    for j in (1, 3, 2):
        m = (n + j) % 4
        late.append(net.copy(cot.at[pl.ds(aligned(m * PART, 16), 16)], g.at[pl.ds(own_a, 16), my_cols], to(m)))
        late.append(net.copy(cot.at[pl.ds(aligned(m * PART + 16, 16), 16)], g.at[pl.ds(own_b, 16), my_cols], to(m)))

    def w_cols(i):
        return pl.ds(aligned(i * COLS, COLS), COLS)

    w_ring = Ring(net, n, to, lambda i: w.at[pl.ds(0, 448), w_cols(i)], lambda i, h: w.at[pl.ds(h * 224, 224), w_cols(i)])
    o_ring = Ring(net, n, to, lambda i: wm.at[pl.ds(0, 64), w_cols(i)], lambda i, h: wm.at[pl.ds(h * 32, 32), w_cols(i)])
    d_ring = Ring(net, n, to, lambda i: wm.at[pl.ds(64, 256), w_cols(i)], lambda i, h: wm.at[pl.ds(64 + h * 128, 128), w_cols(i)])
    w_ring.start()

    for x in early:
        x.wait_recv()
    x = xs[...].astype(F32)
    mean = jnp.sum(x, 1, keepdims=True) / D
    var = jnp.sum(x * x, 1, keepdims=True) / D - mean * mean
    inv = lax.rsqrt(var + EPS)
    xhat[...] = (x - mean) * inv
    for i in range(4):
        cs = slice(i * COLS, (i + 1) * COLS)
        low = (xhat[:, cs] * gbs[i, 0:1, :] + gbs[i, 1:2, :]).astype(BF16)
        ln[pl.ds(own_a, 16), cs] = low[0:16]
        ln[pl.ds(own_b, 16), cs] = low[16:32]

    lg = WideGather(net, ln, y, z, c, n)
    gg = WideGather(net, g, y, z, c, n)
    lg.start()
    for x in late:
        x.wait_recv()
    lg.forward()
    gg.start()
    lg.second()
    gg.forward()
    w_ring.forward()
    lg.forward_second()
    gg.second()
    o_ring.start()
    lg.finish()
    w_ring.finish()
    o_ring.forward()
    gg.forward_second()

    w[448:640, :] = w[0:192, :]
    w[640:656, :] = w[144:160, :]
    w[656:672, :] = w[128:144, :]
    w[672:688, :] = w[16:32, :]
    w[688:704, :] = w[0:16, :]

    def project(i, _):
        r = pl.ds(aligned(i * 256, 256), 256)
        x = ln[r, :]
        pre[pl.ds(i * 16, 16)] = (nt(x, w[448:704, :]) + bias[:, 0:256]).reshape(16, 16, 256)
        return 0

    lax.fori_loop(0, 4, project, 0)
    def arrange(i, _):
        both = pre[chunk_ref[i]]
        r = pl.ds(aligned(i * 16, 16), 16)
        tab = pl.ds(aligned((i % 32) * 16, 16), 16)
        a, b = both[:, 0:128], both[:, 128:256]
        cs, sn = cosine[tab, :], sine[tab, :]
        kv[n, r, :] = (a * cs + pltpu.roll(b, 32, 1) * sn).astype(BF16)
        q_log[r, :] = (b * cs + pltpu.roll(b, 64, 1) * sn).astype(BF16)
        return 0

    lax.fori_loop(0, 64, arrange, 0)
    kv_ring = Ring(net, n, to, lambda i: kv.at[i], lambda i, h: kv.at[i, pl.ds(h * 512, 512)])
    kv_ring.start()
    d_ring.start()

    def project_up(i, _):
        r = pl.ds(aligned(i * 256, 256), 256)
        u[r, :] = nt(ln[r, :], w[192:448, :]) + bias[:, 256:512]
        return 0

    lax.fori_loop(0, 4, project_up, 0)
    gg.finish()
    o_ring.finish()

    def grad_o(i, _):
        r = pl.ds(aligned(i * 256, 256), 256)
        dop[pl.ds(i * 16, 16)] = nt(g[r, :], wm[0:64, :]).reshape(16, 16, 64)
        return 0

    lax.fori_loop(0, 4, grad_o, 0)

    def arrange_do(i, _):
        do_log[pl.ds(aligned(i * 16, 16), 16), :] = dop[chunk_ref[i]].astype(BF16)
        return 0

    lax.fori_loop(0, 64, arrange_do, 0)
    kv_ring.forward()
    d_ring.forward()
    kv_ring.finish()
    d_ring.finish()

    def units(i, _):
        r = pl.ds(aligned(i * 256, 256), 256)
        v = u[r, :]
        dh = nt(g[r, :], wm[64:320, :])
        t = jnp.tanh(GELU_A * (v + GELU_B * (v * v * v)))
        h_out[r, :] = (0.5 * v * (1.0 + t)).astype(BF16)
        slope = 0.5 * (1.0 + t) + 0.5 * v * (1.0 - t * t) * (GELU_A * (1.0 + 3.0 * GELU_B * (v * v)))
        du_out[r, :] = (dh * slope).astype(BF16)
        return 0

    lax.fori_loop(0, 4, units, 0)
    net.drain()


def call_first(chunk, tok, cot, wq, wk, wv, wu, wo, wd, gb, bias, cosine, sine):
    vmem = pl.BlockSpec(memory_space=pltpu.VMEM)
    shape = jax.ShapeDtypeStruct
    return pl.pallas_call(
        first_kernel,
        out_shape=(
            shape((ROWS, D), BF16),
            shape((ROWS, D), BF16),
            shape((704, D), BF16),
            shape((320, D), BF16),
            shape((PART, D), F32),
            shape((ROWS, 128), BF16),
            shape((ROWS, 64), BF16),
            shape((4, ROWS, 128), BF16),
            shape((ROWS, UNITS), BF16),
            shape((ROWS, UNITS), BF16),
        ),
        in_specs=[pl.BlockSpec(memory_space=pltpu.SMEM)] + [vmem] * 12,
        out_specs=(vmem,) * 10,
        scratch_shapes=[
            pltpu.VMEM((PART, D), BF16),
            pltpu.VMEM((4, 8, COLS), F32),
            pltpu.VMEM((64, 16, 256), F32),
            pltpu.VMEM((8, 128), F32),
            pltpu.VMEM((64, 16, 64), F32),
            pltpu.VMEM((ROWS, UNITS), F32),
            pltpu.SemaphoreType.DMA((80,)),
            pltpu.SemaphoreType.DMA((80,)),
            pltpu.SemaphoreType.DMA((2,)),
        ],
        compiler_params=pltpu.CompilerParams(collective_id=0, has_side_effects=True, vmem_limit_bytes=56 * 2**20),
    )(chunk, tok, cot, wq, wk, wv, wu, wo, wd, gb, bias, cosine, sine)


def rotate_back(x, cosine, sine):
    half = ROT // 2
    swapped = jnp.concatenate([x[:, half:ROT], x[:, :half], x[:, ROT:]], 1)
    return x * cosine - swapped * sine


def on_device(
    tokens, ln_gain, ln_bias, w_query, b_query, w_key, b_key, w_value, b_value, w_out, b_out,
    w_fc1, b_fc1, w_fc2, b_fc2, cotangent, lengths, dealing,
):
    n, wide = lax.axis_index("narrow"), lax.axis_index("wide")
    per_seq = MAXLEN // BLOCK
    blocks = jnp.arange(NBLK, dtype=jnp.int32)
    inverse = jnp.sum(jnp.where(dealing[None, :] == blocks[:, None], blocks[None, :], 0), 1)
    iy, iz, ic = inverse // 8, (inverse // 2) % 4, inverse % 2
    starts = jnp.stack([((ic * 4 + iz) * 4 + iy) * 16, (32 + (ic * 4 + iy) * 4 + iz) * 16], 1).reshape(-1)

    mine = jnp.sum(jnp.where(blocks == wide, dealing, 0))
    limit = jnp.where(mine // per_seq == 0, lengths[0], lengths[1])
    valid_local = mine % per_seq * BLOCK + jnp.arange(BLOCK, dtype=jnp.int32) < limit
    cot_masked = jnp.where(valid_local[:, None], cotangent, jnp.zeros_like(cotangent))

    half = ROT // 2
    zero = jnp.zeros((6, COLS), F32)
    gb = jnp.concatenate([ln_gain[None], ln_bias[None], zero], 0)
    bias = jnp.concatenate(
        [
            b_key, b_value, b_query, b_query[half:ROT], b_query[:half], b_key[half:ROT], b_key[:half], b_fc1,
        ]
    ).astype(F32)[None]
    cosine, sine = rope_tables()
    shares = [t.reshape(per_seq, 4, PART, 128) for t in (cosine, sine)]
    cos_n, sin_n = (lax.dynamic_index_in_dim(jnp.asarray(t), n, 1, False).reshape(-1, 128) for t in shares)
    ln, g, w, wm, xhat, q, do, kv, h, du = call_first(
        starts // 16, tokens, cot_masked, w_query, w_key, w_value, w_fc1, w_out, w_fc2, gb, bias, cos_n, sin_n
    )

    q = q[:, :64]
    offset = jnp.arange(PART, dtype=jnp.int32)
    seq_q = jnp.repeat(blocks // per_seq, PART)
    pos_q = (blocks[:, None] % per_seq * BLOCK + n * PART + offset[None]).reshape(-1)
    keys = kv.reshape(4, NBLK, PART, 128).transpose(1, 0, 2, 3).reshape(-1, 128)
    k, v = keys[:, :64], keys[:, 64:]
    pos_k = jnp.tile(jnp.arange(MAXLEN, dtype=jnp.int32), 2)
    seq_k = jnp.repeat(jnp.arange(2, dtype=jnp.int32), MAXLEN)
    valid_k = pos_k < jnp.where(seq_k == 0, lengths[0], lengths[1])
    allowed = (seq_q[:, None] == seq_k[None]) & (pos_k[None] <= pos_q[:, None]) & valid_k[None]
    scale = HEAD_DIM**-0.5
    s = jnp.where(allowed, jnp.dot(q, k.T, preferred_element_type=F32) * scale, -1e30)
    p = jax.nn.softmax(s, -1)
    pb = p.astype(BF16)
    o = jnp.dot(pb, v, preferred_element_type=F32).astype(BF16)
    dp = jnp.dot(do, v.T, preferred_element_type=F32)
    ds = (p * (dp - jnp.sum(p * dp, -1, keepdims=True)) * scale).astype(BF16)
    dq = jnp.dot(ds, k, preferred_element_type=F32)
    dk = jnp.dot(ds.T, q, preferred_element_type=F32)
    dv = jnp.dot(pb.T, do, preferred_element_type=F32)
    dkv = jnp.concatenate([dk, dv], 1).reshape(NBLK, 4, PART, 128).transpose(1, 0, 2, 3)
    dkv = lax.psum_scatter(dkv, "narrow", scatter_dimension=0, tiled=True).reshape(ROWS, 128)
    c64 = jnp.tile(cos_n[:, :64], (2, 1))
    s64 = jnp.tile(sin_n[:, :64], (2, 1))
    dq = rotate_back(dq, c64, s64).astype(BF16)
    dk = rotate_back(dkv[:, :64], c64, s64).astype(BF16)
    logical = jnp.concatenate([dk, dkv[:, 64:].astype(BF16), dq, o], 1).reshape(64, 16, 256)
    chunks = jnp.arange(64, dtype=jnp.int32)
    back = jnp.sum(jnp.where((starts // 16)[None, :] == chunks[:, None], chunks[None, :], 0), 1)
    phys = logical[back].reshape(ROWS, 256)
    dqkv, o = phys[:, :192], phys[:, 192:]
    ones = jnp.ones((ROWS, 64), BF16)

    def by_device(x):
        a = x[:512].reshape(2, 4, 4, 16, D).transpose(2, 1, 0, 3, 4).reshape(32, 16, D)
        b = x[512:].reshape(2, 4, 4, 16, D).transpose(1, 2, 0, 3, 4).reshape(32, 16, D)
        return jnp.concatenate([a, b], 1).reshape(ROWS, D)

    def scatter_rows(x):
        return lax.psum_scatter(by_device(x.astype(BF16)), "wide", scatter_dimension=0, tiled=True)

    def turn(x):
        return lax.all_to_all(x, "narrow", 1, 0, tiled=True)

    branch = turn(scatter_rows(jnp.dot(jnp.concatenate([o, h], 1), wm, preferred_element_type=F32))).astype(F32)
    out_bias = b_out.astype(F32) + b_fc2.astype(F32)
    result = tokens.astype(F32) + valid_local[:, None].astype(F32) * (branch + out_bias)

    def gathered(x):
        return lax.psum_scatter(x, "narrow", scatter_dimension=1, tiled=True)

    grad_mix = gathered(lax.dot_general(jnp.concatenate([o, h, ones], 1), g, (((0,), (0,)), ((), ())), preferred_element_type=F32))
    dpre = jnp.concatenate([dqkv, du], 1)
    grad_in = gathered(lax.dot_general(dpre, ln, (((0,), (0,)), ((), ())), preferred_element_type=F32)).T
    grad_b_in = lax.psum(jnp.sum(dpre, 0, dtype=F32), "narrow")
    dln = scatter_rows(jnp.dot(dpre, w[:448], preferred_element_type=F32)).astype(F32)
    gain = lax.all_gather(ln_gain, "narrow", axis=0, tiled=True)
    e = dln * gain
    x = lax.all_gather(jnp.sum(tokens.astype(F32), 1), "narrow", axis=0)
    x2 = lax.all_gather(jnp.sum(tokens.astype(F32) ** 2, 1), "narrow", axis=0)
    mean = jnp.sum(x, 0) / D
    inv = lax.rsqrt(jnp.sum(x2, 0) / D - mean * mean + EPS)
    core = e - jnp.mean(e, 1, keepdims=True) - xhat * jnp.mean(e * xhat, 1, keepdims=True)
    input_grad = cotangent.astype(F32) + inv[:, None] * turn(core)
    sums = lax.psum(jnp.stack([jnp.sum(dln * xhat, 0), jnp.sum(dln, 0)]), "wide")
    sums = lax.psum_scatter(sums, "narrow", scatter_dimension=1, tiled=True)
    grad_b_out = grad_mix[320]
    return (
        result.astype(BF16),
        input_grad,
        sums[0],
        sums[1],
        grad_in[:, 128:192],
        grad_b_in[128:192],
        grad_in[:, 0:64],
        grad_b_in[0:64],
        grad_in[:, 64:128],
        grad_b_in[64:128],
        grad_mix[:64],
        grad_b_out,
        grad_in[:, 192:],
        grad_b_in[192:],
        grad_mix[64:320],
        grad_b_out,
    )


def solution(mesh):
    rows, col, units = P("wide", "narrow"), P("narrow"), P("wide")
    weight, out = P("narrow", "wide"), P("wide", "narrow")
    placed = (
        rows, col, col, weight, units, weight, units, weight, units, out, col, weight, units, out, col, rows, P(), P(),
    )
    given = (
        rows, rows, col, col, weight, units, weight, units, weight, units, out, col, weight, units, out, col,
    )
    return jax.shard_map(on_device, mesh=mesh, in_specs=placed, out_specs=given, check_vma=False)
```

time: 697 us -> 567 us (0.81)
  waiting for transfers between devices: 444 us -> 219 us
  Pallas kernels: 0 us -> 72.2 us
  local copies, waits for them, and re-layouts: 24.6 us -> 42.1 us
  other arithmetic: 50.8 us -> 33.7 us
  blocking collectives: 84.9 us -> 94.7 us
  starting transfers between devices: 0.63 us -> 7.88 us
    all_gather x4 -> x0, waiting for transfers between devices: 156 us -> none  [the longest x1 43.7 us: on_device(): pre_all = lax.all_gather(grad_pre, 'narrow', axis=0, tiled=True)]
    psum x1 -> x0, waiting for transfers between devices: 139 us -> none  [on_device(): summed = lax.psum(partial_in, 'narrow') + b_in]
    pallas_call x0 -> x1, Pallas kernels: none -> 72.2 us  [call_first(): pl.pallas_call(first_kernel, out_shape=(shape((ROWS, D), BF16), shape((RO...]
    unnamed x10 -> x8, waiting for transfers between devices: 0.4 us -> 56.8 us
    all_gather x0 -> x3, blocking collectives: none -> 21.3 us  [the longest x1 8.09 us: on_device(): x2 = lax.all_gather(jnp.sum(tokens.astype(F32) ** 2, 1), 'narrow', axis=0)]
    convert_element_type x10 -> x4, other arithmetic: 26.8 us -> 9.87 us  [the longest x1 8.27 us: on_device(): ds = (p * (dp - jnp.sum(p * dp, -1, keepdims=True)) * scale).astype(BF16)]
    reduce_scatter x5 -> x4, waiting for transfers between devices: 148 us -> 162 us  [the longest x2 140 us: scatter_rows(): lax.psum_scatter(by_device(x.astype(BF16)), 'wide', scatter_dimension=0,...]
    psum x3 -> x2, blocking collectives: 84.9 us -> 73.3 us  [the longest x1 64.1 us: on_device(): lax.psum(jnp.stack([jnp.sum(dln * xhat, 0), jnp.sum(dln, 0)]), 'wide')]
  transfers between devices with their start and end apart: 10 -> 8, of which waited for: 10 -> 5; matrix products, arithmetic and copies ran while one was open for 11% -> 9% of each run, Pallas kernels for 0% -> 0%
where the time goes in v1:
time: 567 us; the launch traced here: 559 us
  waiting for transfers between devices  219 us (39%)
  blocking collectives  94.7 us (17%)
  Pallas kernels  72.2 us (13%)
  matrix products  70.8 us (12%)
  local copies, waits for them, and re-layouts  42.1 us (7%)
  other arithmetic  33.7 us (6%)
  between operations  18.6 us (3%)
  starting transfers between devices  7.88 us (1%)
    reduce_scatter x2, waiting for transfers between devices, scatter_rows(): lax.psum_scatter(by_device(x.astype(BF16)), 'wide', scatter_dimension=0,...  140 us
    pallas_call x1, Pallas kernels, call_first(): pl.pallas_call(first_kernel, out_shape=(shape((ROWS, D), BF16), shape((RO...  72.2 us
    psum x1, blocking collectives, on_device(): lax.psum(jnp.stack([jnp.sum(dln * xhat, 0), jnp.sum(dln, 0)]), 'wide')  64.1 us
    unnamed x8, waiting for transfers between devices  56.8 us
    reduce_scatter x2, waiting for transfers between devices, gathered(): return lax.psum_scatter(x, 'narrow', scatter_dimension=1, tiled=True)  21.9 us
    unnamed x62, local copies, waits for them, and re-layouts  17.2 us
    dot_general x1, matrix products, on_device(): dp = jnp.dot(do, v.T, preferred_element_type=F32)  16.3 us
  transfers between devices with their start and end apart: 8, of which 5 were waited for; matrix products, arithmetic and copies ran while one was open for 9% of the time, Pallas kernels for 0%

profile of v1, /device:TPU:1, one launch (start us, length us, event | category | flops | bytes accessed | tf_op | source)
XLA Modules:
  0.0 559.0 jit_solution(17698909166420540428)
XLA Ops:
  7.2 1.3 fusion.45
  11.1 0.8 select_reduce_fusion.1
  11.9 1.3 fusion.62
  13.3 0.7 concatenate.64
  13.9 0.8 slice_bitcast_fusion
  14.7 0.8 concatenate.65
  16.9 1.6 copy.109.wq
  18.5 1.6 copy.110.wk
  20.1 1.6 copy.111.wv
  23.0 1.6 broadcast_select_fusion.cot
  24.7 1.9 constant_dynamic-slice_fusion.1
  26.5 1.4 maximum_maximum_fusion.gb
  27.9 72.2 %shard_map.315 = (bf16[1024,2048]{1,0:T(8,128)(2,1)}, bf16[1024,2048]{1,0:T(8,128)(2,1)}, bf16[704,2048]{1,0:T(8,128)(2,1)}, bf16[320,2048]{1,0:T(8,128)(2,1)}, ...) custom-call(s32[64]{0:T(128)} %and_select_fusion.chunk_ref, ...), custom_call_target="tpu_custom_call" | custom-call | tf_op jit(solution)/shard_map/pallas_call | solution.py:345
  100.1 1.4 copy.112
  101.8 1.3 select_compare_fusion
  103.1 9.9 %fusion.63 = (f32[1024]{0:T(1024)S(1)}, f32[1024,4096]{1,0:T(8,128)}) fusion(bf16[4096,128]{1,0:T(8,128)(2,1)S(1)} %bitcast.153, bf16[1024,128]{1,0:T(8,128)(2,1)} %get-tuple-element.26, pred[4096]{0:T(1024)(128)(4,1)S(1)} %select_compare_fusion, s32[1024]{0:T(1024)S(1)} %add.247, s32[4096]{0:T(1024)S(1)} %bitcast.191, s32[4096]{0:T(1024)S(1)} %bitcast.189, ...), kind=kOutput, calls=%fused_computation.136 | convolution fusion | flops 566230016 | bytes 18137088 | tf_op jit(solution)/shard_map/dot_general | solution.py:424
  113.0 8.1 %fusion.1 = f32[1024]{0:T(1024)S(1)} fusion(f32[1024,4096]{1,0:T(8,128)} %get-tuple-element.154, f32[1024]{0:T(1024)S(1)} %get-tuple-element.153), kind=kLoop, calls=%fused_computation.6 | loop fusion | flops 8387584 | bytes 16785408 | tf_op jit(solution)/shard_map/reduce_sum | solution.py:425
  121.2 16.3 %multiply_reduce_fusion = (f32[1024]{0:T(1024)S(1)}, f32[1024,4096]{1,0:T(8,128)}, f32[1024,4096]{1,0:T(8,128)}) fusion(f32[1024]{0:T(1024)S(1)} %fusion.1, f32[1024,4096]{1,0:T(8,128)} %get-tuple-element.154, f32[1024]{0:T(1024)S(1)} %get-tuple-element.153, bf16[1024,64]{1,0:T(8,128)(2,1)S(1)} %copy-done.13, bf16[4096,128]{1,0:T(8,128)(2,1)S(1)} %bitcast.154), kind=kOutput, calls=%fused_computation.2 | convolution fusion | flops 553647104 | bytes 51523584 | tf_op jit(solution)/shard_map/dot_general | solution.py:428
  137.4 8.6 %fusion.4 = f32[4096,64]{0,1:T(8,128)} fusion(bf16[1024,64]{1,0:T(8,128)(2,1)S(1)} %copy-done.13, f32[1024,4096]{1,0:T(8,128)} %get-tuple-element.123), kind=kOutput, calls=%fused_computation.11 | convolution fusion | flops 541065216 | bytes 17956864 | tf_op jit(solution)/shard_map/dot_general | solution.py:432
  146.1 2.3 copy-done
  148.4 8.3 %multiply_convert_fusion = bf16[1024,4096]{1,0:T(8,128)(2,1)S(1)} fusion(f32[1024,4096]{1,0:T(8,128)S(1)} %copy-done, f32[1024,4096]{1,0:T(8,128)} %get-tuple-element.155, f32[1024]{0:T(1024)S(1)} %get-tuple-element.122), kind=kLoop, calls=%fused_computation.1 | loop fusion | flops 16777216 | bytes 41947136 | tf_op jit(solution)/shard_map/convert_element_type | solution.py:429
  156.7 1.6 fusion.40
  158.3 1.6 copy-done.1
  160.0 1.8 copy.113
  162.0 6.1 %fusion.13 = f32[1024,64]{0,1:T(8,128)S(1)} fusion(bf16[1024,4096]{1,0:T(8,128)(2,1)} %copy-done.1, bf16[4096,128]{1,0:T(8,128)(2,1)S(1)} %bitcast.155), kind=kOutput, calls=%fused_computation.23 | convolution fusion | flops 536870912 | bytes 9699328 | tf_op jit(solution)/shard_map/dot_general | solution.py:430
  169.4 0.7 fusion.59
  170.0 8.6 %fusion.7 = bf16[1024,64]{0,1:T(8,128)(2,1)S(1)} fusion(f32[1024,4096]{1,0:T(8,128)} %get-tuple-element.123, bf16[4096,128]{1,0:T(8,128)(2,1)S(1)} %bitcast.156), kind=kOutput, calls=%fused_computation.18 | convolution fusion | flops 541130752 | bytes 17956864 | tf_op jit(solution)/shard_map/dot_general | solution.py:427
  178.6 41.0 %all-reduce.3.cloned.1.call-done = f32[4,32,32,128]{3,2,0,1:T(8,128)} async-done(((f32[4,32,32,128]{3,2,0,1:T(8,128)}), f32[4,32,32,128]{3,2,0,1:T(8,128)}) %all-reduce.3.cloned.1.call-update) | async-done | bytes 2097168
  219.7 1.8 constant_dynamic-slice_fusion
  222.9 1.0 fusion.35
  224.1 0.6 gather_fusion
  224.7 3.9 convolution_convert_fusion
  229.7 2.6 pad_maximum_fusion.1
  233.3 5.9 %fusion.19 = f32[384,2048]{1,0:T(8,128)} fusion(bf16[1024,2048]{1,0:T(8,128)(2,1)} %get-tuple-element.35, bf16[1024,256]{1,0:T(8,128)(2,1)S(1)} %copy-done.8, bf16[1024,64]{1,0:T(8,128)(2,1)S(1)} %slice.176, bf16[384]{0:T(512)(128)(2,1)S(1)} %pad.2.clone), kind=kOutput, calls=%fused_computation.29 | convolution fusion | flops 1612972032 | bytes 7996160 | tf_op jit(solution)/shard_map/dot_general | solution.py:464
  239.2 3.7 convolution_convert_fusion.1
  244.0 2.5 pad_maximum_fusion
  246.6 0.6 copy-done.16
  247.2 8.1 %all-gather.4 = f32[4,1,512]{2,1,0:T(1,128)S(1)} all-gather(f32[1,1,512]{2,1,0:T(1,128)S(1)} %bitcast.197), channel_id=1, replica_groups=mesh['wide'=32,'narrow'=4] {'narrow'}, dimensions={0}, use_global_device_ids=true | all-gather | bytes 10240 | tf_op jit(solution)/shard_map/all_gather | solution.py:469
  255.3 57.5 %reduce-scatter.13.cloned.1.call-done = bf16[32,2048]{1,0:T(8,128)(2,1)} async-done(((bf16[1024,2048]{1,0:T(8,128)(2,1)}), bf16[32,2048]{1,0:T(8,128)(2,1)}) %reduce-scatter.13.cloned.1.call-update) | async-done | bytes 131088 | tf_op jit(solution)/shard_map/reduce_scatter | solution.py:452
  312.8 1.1 fusion.33
  314.0 1.3 copy.131
  315.4 6.2 %fusion.28 = f32[448,2048]{1,0:T(8,128)} fusion(bf16[1024,2048]{1,0:T(8,128)(2,1)} %get-tuple-element.34, bf16[1024,256]{1,0:T(8,128)(2,1)S(1)} %copy-done.10, bf16[1024,192]{1,0:T(8,128)(2,1)S(1)} %bitcast.169), kind=kOutput, calls=%fused_computation.45 | convolution fusion | flops 1880883200 | bytes 8781824 | tf_op jit(solution)/shard_map/dot_general | solution.py:466
  322.2 9.2 %psum.15 = f32[448]{0:T(512)S(1)} all-reduce(f32[448]{0:T(512)S(1)} %convert_reduce_fusion), channel_id=1, replica_groups=mesh['wide'=32,'narrow'=4] {'narrow'}, use_global_device_ids=true, to_apply=%region_21.22 | all-reduce | flops 448 | bytes 3584 | tf_op jit(solution)/shard_map/psum | solution.py:467
  331.4 0.6 slice.160
  332.6 21.9 %reduce-scatter.17.cloned.1.call-done = f32[384,512]{1,0:T(8,128)} async-done(((f32[384,2048]{1,0:T(8,128)}), f32[384,512]{1,0:T(8,128)}) %reduce-scatter.17.cloned.1.call-update) | async-done | bytes 786448 | tf_op jit(solution)/shard_map/reduce_scatter | solution.py:462
  354.5 0.7 slice.188
  355.2 82.9 %reduce-scatter.11.cloned.1.call-done = bf16[32,2048]{1,0:T(8,128)(2,1)} async-done(((bf16[1024,2048]{1,0:T(8,128)(2,1)}), bf16[32,2048]{1,0:T(8,128)(2,1)}) %reduce-scatter.11.cloned.1.call-update) | async-done | bytes 131088 | tf_op jit(solution)/shard_map/reduce_scatter | solution.py:452
  438.1 1.6 copy.147
  439.7 4.0 all-to-all-start
  443.8 0.7 copy.146
  444.5 1.9 slice.190
  446.4 1.6 slice.187
  447.9 15.7 %reduce-scatter.19.cloned.1.call-done = f32[512,2]{1,0:T(8,128)} async-done(((f32[2048,2]{1,0:T(8,128)}), f32[512,2]{1,0:T(8,128)}) %reduce-scatter.19.cloned.1.call-update) | async-done | bytes 4112
  463.6 1.1 copy.132
  464.7 64.1 %psum.16 = f32[2,512]{1,0:T(2,128)S(1)} all-reduce(f32[2,512]{1,0:T(2,128)S(1)} %copy.132), channel_id=1, replica_groups=mesh['wide'=32,'narrow'=4] {'wide'}, use_global_device_ids=true, to_apply=%region_17.18 | all-reduce | flops 1024 | bytes 8192 | tf_op jit(solution)/shard_map/psum | solution.py:477
  528.8 0.6 fusion.60
  529.4 3.4 all-to-all-start.1
  532.8 0.8 fusion.32
  533.6 8.1 %all-gather.2 = f32[4,1,128]{2,1,0:T(1,128)S(1)} all-gather(f32[1,1,128]{2,1,0:T(1,128)S(1)} %bitcast.201), channel_id=2, replica_groups=mesh['wide'=32,'narrow'=4] {'narrow'}, dimensions={0}, use_global_device_ids=true | all-gather | bytes 2560 | tf_op jit(solution)/shard_map/all_gather | solution.py:472
  541.7 5.2 all-gather.3
  546.9 0.8 fusion.38
  547.7 1.1 slice.189
  548.8 1.8 fusion.57
  550.6 1.0 copy.128
  (115 shorter events, 10.0 us)
Async XLA Ops:
  7.2 212.5 %all-reduce.3.cloned.1.call-start = ((), (), s32[]{:S(2)}) async-start(), calls=%async_computation.12 | async-start | bytes 4194304
  113.0 8.1 %copy-start.13 = (bf16[1024,64]{1,0:T(8,128)(2,1)S(1)}, bf16[1024,64]{1,0:T(8,128)(2,1)}, u32[]{:S(2)}) copy-start(bf16[1024,64]{1,0:T(8,128)(2,1)} %get-tuple-element.28) | copy-start | bytes 393220
  137.4 10.9 %copy-start = (f32[1024,4096]{1,0:T(8,128)S(1)}, f32[1024,4096]{1,0:T(8,128)}, u32[]{:S(2)}) copy-start(f32[1024,4096]{1,0:T(8,128)} %get-tuple-element.123) | copy-start | bytes 50331652
  148.4 8.3 %copy-start.14 = (bf16[1024,128]{1,0:T(8,128)(2,1)S(1)}, bf16[1024,128]{1,0:T(8,128)(2,1)}, u32[]{:S(2)}) copy-start(bf16[1024,128]{1,0:T(8,128)(2,1)} %get-tuple-element.26) | copy-start | bytes 786436
  156.7 3.2 copy-start.1
  156.7 3.2 copy-start.2
  161.9 151.0 %reduce-scatter.13.cloned.1.call-start = ((), (), s32[]{:S(2)}) async-start(), calls=%async_computation.8 | async-start | bytes 4325376 | tf_op jit(solution)/shard_map/reduce_scatter | solution.py:452
  161.9 6.2 %copy-start.6 = (f32[16,1,32,128]{3,2,0,1:T(8,128)S(1)}, f32[16,1,32,128]{3,2,0,1:T(8,128)}, u32[]{:S(2)}) copy-start(f32[16,1,32,128]{3,2,0,1:T(8,128)} %get-tuple-element.161) | copy-start | bytes 786436
  161.9 6.4 %copy-start.5 = (f32[16,1,32,128]{3,2,0,1:T(8,128)S(1)}, f32[16,1,32,128]{3,2,0,1:T(8,128)}, u32[]{:S(2)}) copy-start(f32[16,1,32,128]{3,2,0,1:T(8,128)} %get-tuple-element.160) | copy-start | bytes 786436
  161.9 6.7 %copy-start.20 = (u32[128]{0:T(128)S(1)}, u32[128]{0:T(128)}, u32[]{:S(2)}) copy-start(u32[128]{0:T(128)} %constant.157) | copy-start | bytes 1540
  162.0 7.3 %copy-start.19 = (s32[64]{0:T(128)S(1)}, s32[64]{0:T(128)}, u32[]{:S(2)}) copy-start(s32[64]{0:T(128)} %and_select_fusion.chunk_ref) | copy-start | bytes 772
  168.1 10.5 %copy-start.3 = (f32[1024,64]{0,1:T(8,128)}, f32[1024,64]{0,1:T(8,128)S(1)}, u32[]{:S(2)}) copy-start(f32[1024,64]{0,1:T(8,128)S(1)} %fusion.13) | copy-start | bytes 786436
  219.7 3.2 copy-start.4
  219.7 3.2 slice-start
  222.2 2.6 copy-start.10
  232.3 1.0 copy-start.8
  232.3 122.2 %reduce-scatter.17.cloned.1.call-start = ((), (), s32[]{:S(2)}) async-start(), calls=%async_computation.10 | async-start | bytes 3932160 | tf_op jit(solution)/shard_map/reduce_scatter | solution.py:462
  239.2 198.9 %reduce-scatter.11.cloned.1.call-start = ((), (), s32[]{:S(2)}) async-start(), calls=%async_computation.7 | async-start | bytes 4325376 | tf_op jit(solution)/shard_map/reduce_scatter | solution.py:452
  246.6 0.7 copy-start.16
  246.6 66.3 %copy-start.7 = (f32[32,2048]{1,0:T(8,128)S(1)}, f32[32,2048]{1,0:T(8,128)}, u32[]{:S(2)}) copy-start(f32[32,2048]{1,0:T(8,128)} %get-tuple-element.33) | copy-start | bytes 786436
  246.6 217.0 %reduce-scatter.19.cloned.1.call-start = ((), (), s32[]{:S(2)}) async-start(), calls=%async_computation.11 | async-start | bytes 1310720
  315.3 232.4 %reduce-scatter.15.cloned.1.call-start = ((), (), s32[]{:S(2)}) async-start(), calls=%async_computation.9 | async-start | bytes 4587520 | tf_op jit(solution)/shard_map/reduce_scatter | solution.py:462
  315.4 6.3 %copy-start.17 = (bf16[512]{0:T(512)(128)(2,1)S(1)}, bf16[512]{0:T(512)(128)(2,1)}, u32[]{:S(2)}) copy-start(bf16[512]{0:T(512)(128)(2,1)} %param.34) | copy-start | bytes 3076
  315.4 6.3 %copy-start.18 = (bf16[512]{0:T(512)(128)(2,1)S(1)}, bf16[512]{0:T(512)(128)(2,1)}, u32[]{:S(2)}) copy-start(bf16[512]{0:T(512)(128)(2,1)} %param.30) | copy-start | bytes 3076
  321.7 122.0 %copy-start.11 = (bf16[32,2048]{1,0:T(8,128)(2,1)S(1)}, bf16[32,2048]{1,0:T(8,128)(2,1)}, u32[]{:S(2)}) copy-start(bf16[32,2048]{1,0:T(8,128)(2,1)} %reduce-scatter.13.cloned.1.call-done) | copy-start | bytes 393220
  321.7 211.1 %copy-start.9 = (bf16[128,512]{1,0:T(8,128)(2,1)S(1)}, bf16[128,512]{1,0:T(8,128)(2,1)}, u32[]{:S(2)}) copy-start(bf16[128,512]{1,0:T(8,128)(2,1)} %tok.1) | copy-start | bytes 393220
  321.7 225.3 %copy-start.12 = (bf16[128,512]{1,0:T(8,128)(2,1)S(1)}, bf16[128,512]{1,0:T(8,128)(2,1)}, u32[]{:S(2)}) copy-start(bf16[128,512]{1,0:T(8,128)(2,1)} %param.35) | copy-start | bytes 393220
  355.2 196.9 %copy-start.15 = (f32[1,512]{1,0:T(1,128)}, f32[1,512]{1,0:T(1,128)S(1)}, u32[]{:S(2)}) copy-start(f32[1,512]{1,0:T(1,128)S(1)} %slice.188) | copy-start | bytes 6148
  439.7 89.7 %all-to-all-start = ((bf16[32,4,512]{2,0,1:T(8,128)(2,1)}), bf16[32,4,512]{2,0,1:T(8,128)(2,1)S(1)}, u32[]{:S(2)}, u32[]{:S(2)}) async-start(bf16[32,4,512]{2,0,1:T(8,128)(2,1)} %bitcast.142), calls=%async_computation.1 | async-start | bytes 262144 | tf_op jit(solution)/shard_map/all_to_all | solution.py:455
  529.4 17.6 %all-to-all-start.1 = ((f32[32,4,512]{2,0,1:T(8,128)}), f32[32,4,512]{2,0,1:T(8,128)S(1)}, u32[]{:S(2)}, u32[]{:S(2)}) async-start(f32[32,4,512]{2,0,1:T(8,128)} %bitcast.141), calls=%async_computation.3 | async-start | bytes 524288 | tf_op jit(solution)/shard_map/all_to_all | solution.py:455
Sparse Core Ops, SparseCore 0:
  162.0 57.6 all-reduce.2
  232.4 80.3 reduce-scatter.12
  315.2 39.2 reduce-scatter.16
  358.0 80.0 reduce-scatter.10
  440.5 23.1 reduce-scatter.18
  465.9 43.4 reduce-scatter.14

commit v2 on v1

v2 whole, which is shorter than its diff:
```python
import jax
import jax.numpy as jnp
import numpy as np
from jax import lax
from jax.experimental import pallas as pl
from jax.experimental.pallas import tpu as pltpu
from jax.sharding import PartitionSpec as P

MESH = pl.DeviceIdType.MESH
D = 2048
HEAD_DIM = 64
ROT = 32
BLOCK = 128
MAXLEN = 2048
NBLK = 32
PART = 32
ROWS = NBLK * PART
COLS = 512
UNITS = 256
EPS = 1e-05
BF16 = jnp.bfloat16
F32 = jnp.float32


def rope_tables():
    half = ROT // 2
    inverse = (10000.0 ** (-(np.arange(half, dtype=np.float32) * np.float32(2.0) / np.float32(ROT)))).astype(np.float32)
    angles = (np.arange(MAXLEN, dtype=np.float32)[:, None] * inverse[None, :]).astype(np.float64)
    cosine = np.ones((MAXLEN, 128), np.float32)
    sine = np.zeros((MAXLEN, 128), np.float32)
    cosine[:, :half] = np.cos(angles)
    cosine[:, half:ROT] = np.cos(angles)
    sine[:, :half] = -np.sin(angles)
    sine[:, half:ROT] = np.sin(angles)
    return cosine, sine


class Net:
    def __init__(self, send, recv):
        self.send, self.recv, self.used, self.open = send, recv, 0, []

    def copy(self, src, dst, device):
        i = self.used
        self.used += 1
        c = pltpu.make_async_remote_copy(
            src_ref=src,
            dst_ref=dst,
            send_sem=self.send.at[i],
            recv_sem=self.recv.at[i],
            device_id=device,
            device_id_type=MESH,
        )
        c.start()
        self.open.append(c)
        return c

    def drain(self):
        for c in self.open:
            c.wait_send()


class Ring:
    def __init__(self, net, me, device, unit, half):
        self.net, self.unit, self.half = net, unit, half
        self.right, self.left = (me + 1) % 4, (me + 3) % 4
        self.to_right, self.to_left = device(self.right), device(self.left)
        self.me = me

    def start(self):
        own = self.unit(self.me)
        self.a = self.net.copy(own, own, self.to_right)
        self.b = self.net.copy(own, own, self.to_left)

    def forward(self):
        self.a.wait_recv()
        x = self.half(self.left, 0)
        self.c = self.net.copy(x, x, self.to_right)
        self.b.wait_recv()
        x = self.half(self.right, 1)
        self.d = self.net.copy(x, x, self.to_left)

    def finish(self):
        self.c.wait_recv()
        self.d.wait_recv()


def coords():
    w, n = lax.axis_index("wide"), lax.axis_index("narrow")
    return w // 8, (w // 2) % 4, w % 2, n


def wide_of(y, z, c):
    return (y * 4 + z) * 2 + c


def aligned(x, m):
    return pl.multiple_of(x, m)


def slot_a(c, z, y):
    return aligned(((c * 4 + z) * 4 + y) * 16, 16)


def slot_b(c, y, z):
    return aligned((32 + (c * 4 + y) * 4 + z) * 16, 16)


class WideGather:
    def __init__(self, net, buf, y, z, c, n):
        self.net, self.buf, self.y, self.z, self.c = net, buf, y, z, c

        def dev(y, z, c):
            return (wide_of(y, z, c), n)

        def rows(start, count):
            return buf.at[pl.ds(start, count)]

        def cols(start, h):
            return buf.at[pl.ds(start, 16), pl.ds(h * 1024, 1024)]

        def half(start, h):
            return buf.at[pl.ds(aligned(start + 32 * h, 16), 32)]

        self.rows = rows
        self.other = dev(y, z, 1 - c)
        self.one = (
            Ring(net, y, lambda i: dev(i, z, c), lambda i: rows(slot_a(c, z, i), 16), lambda i, h: cols(slot_a(c, z, i), h)),
            Ring(net, z, lambda i: dev(y, i, c), lambda i: rows(slot_b(c, y, i), 16), lambda i, h: cols(slot_b(c, y, i), h)),
        )
        self.two = (
            Ring(net, z, lambda i: dev(y, i, c), lambda i: rows(slot_a(c, i, 0), 64), lambda i, h: half(slot_a(c, i, 0), h)),
            Ring(net, y, lambda i: dev(i, z, c), lambda i: rows(slot_b(c, i, 0), 64), lambda i, h: half(slot_b(c, i, 0), h)),
        )
        self.cross = []

    def _cross(self, i):
        for part, slot in ((0, slot_a), (1, slot_b)):
            me = (self.z, self.y)[part]
            x = self.rows(slot(self.c, (me + i) % 4, 0), 64)
            self.cross.append(self.net.copy(x, x, self.other))

    def start(self):
        for r in self.one:
            r.start()

    def forward(self):
        for r in self.one:
            r.forward()

    def second(self):
        for r in self.one:
            r.finish()
        for r in self.two:
            r.start()
        self._cross(0)

    def forward_second(self):
        for r in self.two:
            r.forward()
        self._cross(1)
        self._cross(3)

    def finish(self):
        for r in self.two:
            r.finish()
        self._cross(2)
        for x in self.cross:
            x.wait_recv()


class Scatter:
    def __init__(self, net, me, device, part, rh, rl, rr):
        self.net, self.part, self.rh, self.rl, self.rr = net, part, rh, rl, rr
        self.me, self.right, self.left = me, (me + 1) % 4, (me + 3) % 4
        self.to_right, self.to_left = device(self.right), device(self.left)

    def start(self):
        copy, far = self.net.copy, (self.me + 2) % 4
        self.s0 = copy(self.part(far, 0), self.rh[0], self.to_right)
        self.s1 = copy(self.part(far, 1), self.rh[1], self.to_left)
        self.a0 = copy(self.part(self.right, 1), self.rl(1), self.to_right)
        self.a1 = copy(self.part(self.left, 0), self.rr(0), self.to_left)

    def step(self):
        self.s0.wait_recv()
        p = self.part(self.right, 0)
        p[...] = (p[...].astype(F32) + self.rh[0][...].astype(F32)).astype(BF16)
        self.b0 = self.net.copy(p, self.rl(0), self.to_right)
        self.s1.wait_recv()
        p = self.part(self.left, 1)
        p[...] = (p[...].astype(F32) + self.rh[1][...].astype(F32)).astype(BF16)
        self.b1 = self.net.copy(p, self.rr(1), self.to_left)

    def finish(self):
        for x in (self.a0, self.a1, self.b0, self.b1):
            x.wait_recv()

    def half(self, h):
        return self.part(self.me, h)[...].astype(F32) + (self.rl(h)[...].astype(F32) + self.rr(h)[...].astype(F32))


class WideScatter:
    def __init__(self, net, tile, out, got, own, acc, r1, r2, y, z, c, n):
        self.net, self.tile, self.out, self.got, self.own, self.acc, self.c = net, tile, out, got, own, acc, c

        def dev(y, z, c):
            return (wide_of(y, z, c), n)

        self.other = dev(y, z, 1 - c)

        def rows(ref, start, count):
            return ref.at[pl.ds(aligned(start, 16), count)]

        def first(base, k):
            return dict(
                part=lambda i, h: rows(acc, base + i * 64 + h * 32, 32),
                rh=(r1.at[k, pl.ds(0, 32)], r1.at[k, pl.ds(32, 32)]),
                rl=lambda h: r1.at[k, pl.ds(64 + 32 * h, 32)],
                rr=lambda h: r1.at[k, pl.ds(128 + 32 * h, 32)],
            )

        def cols(ref, start, h):
            return ref.at[pl.ds(aligned(start, 16), 16), pl.ds(h * 1024, 1024)]

        def second(base, me, k):
            return dict(
                part=lambda i, h: cols(acc, base + me * 64 + i * 16, h),
                rh=(cols(r2, k * 48, 0), cols(r2, k * 48, 1)),
                rl=lambda h: cols(r2, k * 48 + 16, h),
                rr=lambda h: cols(r2, k * 48 + 32, h),
            )

        self.one = (
            Scatter(net, z, lambda i: dev(y, i, c), **first(0, 0)),
            Scatter(net, y, lambda i: dev(i, z, c), **first(256, 1)),
        )
        self.two = (
            Scatter(net, y, lambda i: dev(i, z, c), **second(0, z, 0)),
            Scatter(net, z, lambda i: dev(y, i, c), **second(256, y, 1)),
        )

    def exchange(self):
        self.cross = []
        for p in range(2):
            mine = pl.ds(p * 256, 256)
            for i in range(4):
                cs = slice(i * COLS, (i + 1) * COLS)
                self.out[mine, cs] = self.tile(aligned(p * 512 + (1 - self.c) * 256, 256), cs).astype(BF16)
            self.cross.append(self.net.copy(self.out.at[mine], self.got.at[mine], self.other))
        for p in range(2):
            for i in range(4):
                cs = slice(i * COLS, (i + 1) * COLS)
                self.own[p * 256 : p * 256 + 256, cs] = self.tile(aligned(p * 512 + self.c * 256, 256), cs)

    def start(self):
        for p in range(2):
            self.cross[p].wait_recv()

            def add(i, _, p=p):
                r = pl.ds(aligned(p * 256 + i * 64, 64), 64)
                self.acc[r, :] = (self.own[r, :] + self.got[r, :].astype(F32)).astype(BF16)
                return 0

            lax.fori_loop(0, 4, add, 0)
            self.one[p].start()

    def step(self):
        for r in self.one:
            r.step()

    def second(self):
        for r, t in zip(self.one, self.two):
            r.finish()
            for h in range(2):
                r.part(r.me, h)[...] = r.half(h).astype(BF16)
            t.start()

    def second_step(self):
        for r in self.two:
            r.step()

    def finish(self):
        for r in self.two:
            r.finish()

    def result(self, i, cs):
        return self.two[i].half(cs)


def greet(y, z, c, n):
    peers = [
        (wide_of((y + 1) % 4, z, c), n),
        (wide_of((y + 3) % 4, z, c), n),
        (wide_of(y, (z + 1) % 4, c), n),
        (wide_of(y, (z + 3) % 4, c), n),
        (wide_of((y + 2) % 4, z, c), n),
        (wide_of(y, (z + 2) % 4, c), n),
        (wide_of(y, z, 1 - c), n),
        (wide_of(y, z, c), (n + 1) % 4),
        (wide_of(y, z, c), (n + 2) % 4),
        (wide_of(y, z, c), (n + 3) % 4),
    ]
    barrier = pltpu.get_barrier_semaphore()
    for p in peers:
        pl.semaphore_signal(barrier, inc=1, device_id=p, device_id_type=MESH)
    pl.semaphore_wait(barrier, len(peers))


def nt(a, b):
    return lax.dot_general(a, b, (((1,), (1,)), ((), ())), preferred_element_type=F32)


GELU_A = float(np.sqrt(2.0 / np.pi))
GELU_B = 0.044715


def dot(a, b):
    return jnp.dot(a, b, preferred_element_type=F32)


def lanes(shape):
    return lax.broadcasted_iota(jnp.int32, shape, len(shape) - 1)


def swap(x):
    return jnp.where(lanes(x.shape) < ROT // 2, pltpu.roll(x, 128 - ROT // 2, 1), pltpu.roll(x, ROT // 2, 1))


def block_kernel(
    meta, tok, cot, wq, wk, wv, wu, wo, wd, gb, bias, cos_all, sin_all,
    res, ig, grad_l, grad_u, grad_f, small,
    ln, g, w, wm, wmo, xs, gbs, xhat, cosine, sine, pre, slope, hb, dpre, kv, kk, xq, xd, od, dkvt, dkv, dkvp,
    rdkv, sum_f, sum_u, sum_l, r_f, r_u, r_l, out_1, got_1, acc_1, r1_1, r2_1, out_2, got_2, acc_2, r1_2, r2_2, own,
    trans, cmask, bsend, bfin, csend, cfin, ssend, srecv, brecv, yrecv, zrecv, crecv, kpos, send, recv, local,
):
    y, z, c, n = coords()
    net = Net(send, recv)
    my_cols = pl.ds(aligned(n * COLS, COLS), COLS)
    me = wide_of(y, z, c)
    own_a, own_b = slot_a(c, z, y), slot_b(c, y, z)

    def to(m):
        return (me, m)

    def w_cols(i):
        return pl.ds(aligned(i * COLS, COLS), COLS)

    def share(i):
        return pl.ds(aligned(i * PART, PART), PART)

    tables = [
        pltpu.make_async_copy(cos_all.at[n], cosine, local.at[0]),
        pltpu.make_async_copy(sin_all.at[n], sine, local.at[1]),
    ]
    for t in tables:
        t.start()
    w[256:320, my_cols] = wk[...]
    w[320:384, my_cols] = wv[...]
    w[384:448, my_cols] = wq[...]
    w[0:256, my_cols] = wu[...].T
    wm[0:256, my_cols] = wd[...]
    wm[256:320, my_cols] = wo[...]
    gbs[n] = gb[...]
    xs[:, my_cols] = tok[share(n), :]
    row = lax.broadcasted_iota(jnp.int32, (BLOCK, COLS), 0)
    valid = meta[128] + row < meta[129]
    cmask[...] = jnp.where(valid, cot[...], jnp.zeros_like(cot))
    mine = cmask[share(n), :]
    g[pl.ds(own_a, 16), my_cols] = mine[0:16]
    g[pl.ds(own_b, 16), my_cols] = mine[16:32]
    greet(y, z, c, n)

    early, late = [], []
    for j in (1, 3, 2):
        m = (n + j) % 4
        early.append(net.copy(gbs.at[n], gbs.at[n], to(m)))
        early.append(net.copy(tok.at[share(m)], xs.at[:, my_cols], to(m)))
    w_ring = Ring(net, n, to, lambda i: w.at[pl.ds(0, 448), w_cols(i)], lambda i, h: w.at[pl.ds(h * 224, 224), w_cols(i)])
    d_ring = Ring(net, n, to, lambda i: wm.at[pl.ds(0, 256), w_cols(i)], lambda i, h: wm.at[pl.ds(h * 128, 128), w_cols(i)])
    o_ring = Ring(net, n, to, lambda i: wm.at[pl.ds(256, 64), w_cols(i)], lambda i, h: wm.at[pl.ds(256 + h * 32, 32), w_cols(i)])
    kv_ring = Ring(net, n, to, lambda i: kv.at[i], lambda i, h: kv.at[i, pl.ds(h * 512, 512)])
    w_ring.start()
    for j in (1, 3, 2):
        m = (n + j) % 4
        late.append(net.copy(cmask.at[pl.ds(aligned(m * PART, 16), 16)], g.at[pl.ds(own_a, 16), my_cols], to(m)))
        late.append(net.copy(cmask.at[pl.ds(aligned(m * PART + 16, 16), 16)], g.at[pl.ds(own_b, 16), my_cols], to(m)))
    o_ring.start()

    for x in early:
        x.wait_recv()
    x = xs[...].astype(F32)
    mean = jnp.sum(x, 1, keepdims=True) / D
    var = jnp.sum(x * x, 1, keepdims=True) / D - mean * mean
    inv = lax.rsqrt(var + EPS)
    xhat[...] = (x - mean) * inv
    for i in range(4):
        cs = slice(i * COLS, (i + 1) * COLS)
        low = (xhat[:, cs] * gbs[i, 0:1, :] + gbs[i, 1:2, :]).astype(BF16)
        ln[pl.ds(own_a, 16), cs] = low[0:16]
        ln[pl.ds(own_b, 16), cs] = low[16:32]

    lg = WideGather(net, ln, y, z, c, n)
    gg = WideGather(net, g, y, z, c, n)
    lg.start()
    for x in late:
        x.wait_recv()
    for t in tables:
        t.wait()
    for s in range(2):
        at = lanes((8, MAXLEN))
        kpos[s] = jnp.where(at < meta[130 + s], at, 1 << 20)
    wmo[0:64, :] = jnp.zeros((64, D), BF16)
    lg.forward()
    gg.start()
    lg.second()
    gg.forward()
    w_ring.forward()
    o_ring.forward()
    lg.forward_second()
    gg.second()
    w_ring.finish()
    lg.finish()
    gg.forward_second()

    w[448:640, :] = w[256:448, :]
    w[640:656, :] = w[400:416, :]
    w[656:672, :] = w[384:400, :]
    w[672:688, :] = w[272:288, :]
    w[688:704, :] = w[256:272, :]

    def project(i, _):
        r = pl.ds(aligned(i * 256, 256), 256)
        pre[pl.ds(i * 16, 16)] = (nt(ln[r, :], w[448:704, :]) + bias[:, 256:512]).reshape(16, 16, 256)
        return 0

    lax.fori_loop(0, 4, project, 0)

    def arrange(i, _):
        both = pre[meta[i]]
        r = pl.ds(aligned(i * 16, 16), 16)
        tab = pl.ds(aligned((i % 32) * 16, 16), 16)
        a, b = both[:, 0:128], both[:, 128:256]
        cs, sn = cosine[tab, :], sine[tab, :]
        kv[n, r, :] = (a * cs + pltpu.roll(b, 32, 1) * sn).astype(BF16)
        q = (b * cs + pltpu.roll(b, 64, 1) * sn) * (HEAD_DIM**-0.5)
        xq[r, :] = jnp.where(lanes((16, 128)) < HEAD_DIM, q, 0.0).astype(BF16)
        return 0

    lax.fori_loop(0, 64, arrange, 0)
    kv_ring.start()
    d_ring.start()

    def units(i, _):
        r = pl.ds(aligned(i * 256, 256), 256)
        v = nt(ln[r, :], w[0:256, :]) + bias[:, 0:256]
        t = jnp.tanh(GELU_A * (v + GELU_B * (v * v * v)))
        hb[r, :] = (0.5 * v * (1.0 + t)).astype(BF16)
        slope[r, :] = 0.5 * (1.0 + t) + 0.5 * v * (1.0 - t * t) * (GELU_A * (1.0 + 3.0 * GELU_B * (v * v)))
        return 0

    lax.fori_loop(0, 4, units, 0)
    o_ring.finish()
    wmo[64:128, :] = wm[256:320, :]
    gg.finish()

    def grad_o(i, _):
        r = pl.ds(aligned(i * 256, 256), 256)
        pre[pl.ds(i * 16, 16), :, 0:128] = nt(g[r, :], wmo[...]).reshape(16, 16, 128)
        return 0

    lax.fori_loop(0, 4, grad_o, 0)

    def arrange_do(i, _):
        xd[pl.ds(aligned(i * 16, 16), 16), :] = pre[meta[i], :, 0:128].astype(BF16)
        return 0

    lax.fori_loop(0, 64, arrange_do, 0)

    def scatter_cols(buf, count, r):
        half = count // 2
        return Scatter(
            net, n, to,
            lambda i, h: buf.at[pl.ds(h * half, half), w_cols(i)],
            (r.at[0, pl.ds(0, half)], r.at[0, pl.ds(half, half)]),
            lambda h: r.at[1, pl.ds(h * half, half)],
            lambda h: r.at[2, pl.ds(h * half, half)],
        )

    f_sum = scatter_cols(sum_f, 288, r_f)
    u_sum = scatter_cols(sum_u, 256, r_u)
    l_sum = scatter_cols(sum_l, 256, r_l)

    trans[...] = hb[...].T

    def weight_f(i, _):
        cs = pl.ds(aligned(i * COLS, COLS), COLS)
        sum_f[0:256, cs] = dot(trans[...], g[:, cs]).astype(BF16)
        sum_f[256:288, cs] = dot(jnp.ones((32, ROWS), BF16), g[:, cs]).astype(BF16)
        return 0

    lax.fori_loop(0, 4, weight_f, 0)
    f_sum.start()
    kv_ring.forward()
    d_ring.forward()
    kv_ring.finish()

    def gather_keys(i, _):
        for m in range(4):
            kk[pl.ds(aligned(i * BLOCK + m * PART, PART), PART), :] = kv[m, share(i), :]
        return 0

    lax.fori_loop(0, NBLK, gather_keys, 0)

    def attend(s, t):
        keys = 512 * (t + 1)
        r = pl.ds(s * 512 + t * 128, 128)
        x = jnp.concatenate([xq[r, :], xd[r, :]], 0)
        near = kk[pl.ds(s * MAXLEN, keys), :]
        both = nt(x, near)
        i = lax.broadcasted_iota(jnp.int32, (128, 1), 0)
        qpos = (4 * t + i // PART) * BLOCK + n * PART + i % PART
        scores = jnp.where(kpos[s, 0:1, 0:keys] <= qpos, both[0:128], -1e30)
        e = jnp.exp(scores - jnp.max(scores, 1, keepdims=True))
        p = e * (1.0 / jnp.sum(e, 1, keepdims=True))
        dp = both[128:256]
        ds = p * (dp - jnp.sum(p * dp, 1, keepdims=True))
        yy = jnp.concatenate([ds.astype(BF16), p.astype(BF16)], 0)
        back = dot(yy, near)
        od[pl.ds(s * 32 + t * 8, 8)] = jnp.where(lanes((128, 128)) < HEAD_DIM, back[0:128] * (HEAD_DIM**-0.5), back[128:256]).reshape(8, 16, 128)
        grads = dot(x.T, yy)
        if t == 3:
            dkvt[s, :, 0:keys] = grads
        else:
            dkvt[s, :, 0:keys] += grads

    attend(0, 3)
    attend(1, 3)
    f_sum.step()
    attend(0, 2)
    d_ring.finish()

    def grad_units(i, _):
        r = pl.ds(aligned(i * 256, 256), 256)
        dpre[r, 0:256] = (nt(g[r, :], wm[0:256, :]) * slope[r, :]).astype(BF16)
        return 0

    lax.fori_loop(0, 4, grad_units, 0)
    trans[...] = dpre[:, 0:256].T

    def weight_u(i, _):
        cs = pl.ds(aligned(i * COLS, COLS), COLS)
        sum_u[:, cs] = dot(trans[...], ln[:, cs]).astype(BF16)
        return 0

    lax.fori_loop(0, 4, weight_u, 0)
    u_sum.start()
    attend(1, 2)
    attend(0, 1)
    attend(1, 1)
    attend(0, 0)
    attend(1, 0)

    for s in range(2):

        def turn_keys(i, _, s=s):
            t = dkvt[s, :, pl.ds(aligned(i * BLOCK, BLOCK), BLOCK)].T.astype(BF16)
            for m in range(4):
                dkv[m, pl.ds(aligned(s * 512 + i * PART, PART), PART), :] = t[m * PART : (m + 1) * PART]
            return 0

        lax.fori_loop(0, 16, turn_keys, 0)
    kv_sum = Scatter(
        net, n, to,
        lambda i, h: dkv.at[i, pl.ds(h * 512, 512)],
        (rdkv.at[0, pl.ds(0, 512)], rdkv.at[0, pl.ds(512, 512)]),
        lambda h: rdkv.at[1, pl.ds(h * 512, 512)],
        lambda h: rdkv.at[2, pl.ds(h * 512, 512)],
    )
    kv_sum.start()

    def unrope(i, _):
        tab = pl.ds(aligned((i % 32) * 16, 16), 16)
        x = od[i]
        od[i] = x * cosine[tab, :] - swap(x) * sine[tab, :]
        return 0

    lax.fori_loop(0, 64, unrope, 0)

    def place(i, _):
        dpre[pl.ds(aligned(i * 16, 16), 16), 384:512] = od[meta[64 + i]].astype(BF16)
        return 0

    lax.fori_loop(0, 64, place, 0)

    def branch_tile(start, cs):
        r = pl.ds(start, 256)
        return dot(hb[r, :], wm[0:256, cs]) + dot(dpre[r, 384:512], wmo[:, cs])

    branch = WideScatter(net, branch_tile, out_1, got_1, own, acc_1, r1_1, r2_1, y, z, c, n)
    branch.exchange()
    kv_sum.step()
    branch.start()
    u_sum.step()
    f_sum.finish()
    for h in range(2):
        grad_f[h * 144 : (h + 1) * 144, :] = f_sum.half(h)
    kv_sum.finish()

    def unrope_keys(i, _):
        tab = pl.ds(aligned((i % 32) * 16, 16), 16)
        r = pl.ds(aligned(i * 16, 16), 16)
        x = dkv[n, r, :].astype(F32) + (rdkv[1, r, :].astype(F32) + rdkv[2, r, :].astype(F32))
        dkvp[i] = x * cosine[tab, :] - swap(x) * sine[tab, :]
        return 0

    lax.fori_loop(0, 64, unrope_keys, 0)

    def place_keys(i, _):
        dpre[pl.ds(aligned(i * 16, 16), 16), 256:384] = dkvp[meta[64 + i]].astype(BF16)
        return 0

    lax.fori_loop(0, 64, place_keys, 0)

    def dln_tile(start, cs):
        r = pl.ds(start, 256)
        return dot(dpre[r, 0:448], w[0:448, cs])

    dln = WideScatter(net, dln_tile, out_2, got_2, own, acc_2, r1_2, r2_2, y, z, c, n)
    dln.exchange()
    branch.step()
    trans[...] = dpre[:, 256:512].T

    def weight_l(i, _):
        cs = pl.ds(aligned(i * COLS, COLS), COLS)
        sum_l[0:192, cs] = dot(trans[0:192, :], ln[:, cs]).astype(BF16)
        sum_l[192:256, cs] = dot(trans[192:256, :], g[:, cs]).astype(BF16)
        return 0

    lax.fori_loop(0, 4, weight_l, 0)
    dln.start()
    l_sum.start()
    brecv[n] = jnp.broadcast_to(jnp.sum(dpre[...].astype(F32), 0, keepdims=True), (8, COLS))
    late = []
    for j in (1, 3, 2):
        late.append(net.copy(brecv.at[n], brecv.at[n], to((n + j) % 4)))
    branch.second()
    u_sum.finish()
    for h in range(2):
        grad_u[h * 128 : (h + 1) * 128, :] = u_sum.half(h)
    dln.step()
    branch.second_step()
    l_sum.step()
    dln.second()
    branch.finish()
    for i in range(2):
        for h in range(2):
            bsend[i * 16 : (i + 1) * 16, h * 1024 : (h + 1) * 1024] = branch.result(i, h).astype(BF16)
    bfin[share(n), :] = bsend[:, my_cols]
    for j in (1, 3, 2):
        m = (n + j) % 4
        late.append(net.copy(bsend.at[:, w_cols(m)], bfin.at[share(n)], to(m)))
    dln.second_step()
    dln.finish()

    for i in range(2):
        for h in range(2):
            csend[i * 16 : (i + 1) * 16, h * 1024 : (h + 1) * 1024] = dln.result(i, h)
    grad = csend[...]
    ssend[...] = jnp.broadcast_to(jnp.sum(grad, 0, keepdims=True), (8, D))
    ssend[0:1, :] = jnp.sum(grad * xhat[...], 0, keepdims=True)
    for j in range(4):
        cs = slice(j * COLS, (j + 1) * COLS)
        csend[:, cs] = csend[:, cs] * gbs[j, 0:1, :]
    srecv[n] = ssend[:, my_cols]
    last = []
    for j in (1, 3, 2):
        m = (n + j) % 4
        last.append(net.copy(ssend.at[:, w_cols(m)], srecv.at[n], to(m)))
    grad = csend[...]
    first = jnp.sum(grad, 1, keepdims=True) / D
    second = jnp.sum(grad * xhat[...], 1, keepdims=True) / D
    x = xs[...].astype(F32)
    mean = jnp.sum(x, 1, keepdims=True) / D
    var = jnp.sum(x * x, 1, keepdims=True) / D - mean * mean
    csend[...] = lax.rsqrt(var + EPS) * (grad - first - xhat[...] * second)
    cfin[share(n), :] = csend[:, my_cols]
    final = []
    for j in (1, 3, 2):
        m = (n + j) % 4
        final.append(net.copy(csend.at[:, w_cols(m)], cfin.at[share(n)], to(m)))
    for x in last:
        x.wait_recv()
    yrecv[y] = (srecv[0] + srecv[1]) + (srecv[2] + srecv[3])
    last = []
    for j in (1, 3, 2):
        last.append(net.copy(yrecv.at[y], yrecv.at[y], (wide_of((y + j) % 4, z, c), n)))
    l_sum.finish()
    for h in range(2):
        grad_l[h * 128 : (h + 1) * 128, :] = l_sum.half(h)
    for x in late:
        x.wait_recv()
    valid = meta[128] + row < meta[129]
    base = bfin[...].astype(F32) + gb[2:3, :]
    res[...] = (tok[...].astype(F32) + jnp.where(valid, base, 0.0)).astype(BF16)
    for x in last:
        x.wait_recv()
    zrecv[z] = (yrecv[0] + yrecv[1]) + (yrecv[2] + yrecv[3])
    last = []
    for j in (1, 3, 2):
        last.append(net.copy(zrecv.at[z], zrecv.at[z], (wide_of(y, (z + j) % 4, c), n)))
    for x in final:
        x.wait_recv()
    ig[...] = cot[...].astype(F32) + cfin[...]
    for x in last:
        x.wait_recv()
    crecv[c] = (zrecv[0] + zrecv[1]) + (zrecv[2] + zrecv[3])
    x = net.copy(crecv.at[c], crecv.at[c], (wide_of(y, z, 1 - c), n))
    x.wait_recv()
    small[0:8, :] = crecv[0] + crecv[1]
    small[8:16, :] = (brecv[0] + brecv[1]) + (brecv[2] + brecv[3])
    net.drain()


def call_block(*args):
    vmem, anywhere = pl.BlockSpec(memory_space=pltpu.VMEM), pl.BlockSpec(memory_space=pl.ANY)
    shape = jax.ShapeDtypeStruct

    def buf(dtype, *size):
        return pltpu.VMEM(size, dtype)

    wide = [buf(BF16, 512, D), buf(BF16, 512, D), buf(BF16, 512, D), buf(BF16, 2, 192, D), buf(BF16, 96, D)]
    return pl.pallas_call(
        block_kernel,
        out_shape=(
            shape((BLOCK, COLS), BF16),
            shape((BLOCK, COLS), F32),
            shape((256, COLS), F32),
            shape((256, COLS), F32),
            shape((288, COLS), F32),
            shape((16, COLS), F32),
        ),
        in_specs=[pl.BlockSpec(memory_space=pltpu.SMEM)] + [vmem] * 10 + [anywhere] * 2,
        out_specs=(vmem,) * 6,
        scratch_shapes=[
            buf(BF16, ROWS, D),
            buf(BF16, ROWS, D),
            buf(BF16, 704, D),
            buf(BF16, 320, D),
            buf(BF16, 128, D),
            buf(BF16, PART, D),
            buf(F32, 4, 8, COLS),
            buf(F32, PART, D),
            buf(F32, 512, 128),
            buf(F32, 512, 128),
            buf(F32, 64, 16, 256),
            buf(F32, ROWS, UNITS),
            buf(BF16, ROWS, UNITS),
            buf(BF16, ROWS, 512),
            buf(BF16, 4, ROWS, 128),
            buf(BF16, 2 * MAXLEN, 128),
            buf(BF16, ROWS, 128),
            buf(BF16, ROWS, 128),
            buf(F32, 64, 16, 128),
            buf(F32, 2, 128, MAXLEN),
            buf(BF16, 4, ROWS, 128),
            buf(F32, 64, 16, 128),
            buf(BF16, 3, ROWS, 128),
            buf(BF16, 288, D),
            buf(BF16, 256, D),
            buf(BF16, 256, D),
            buf(BF16, 3, 288, COLS),
            buf(BF16, 3, 256, COLS),
            buf(BF16, 3, 256, COLS),
            *wide,
            *wide,
            buf(F32, 512, D),
            buf(BF16, 256, ROWS),
            buf(BF16, BLOCK, COLS),
            buf(BF16, PART, D),
            buf(BF16, BLOCK, COLS),
            buf(F32, PART, D),
            buf(F32, BLOCK, COLS),
            buf(F32, 8, D),
            buf(F32, 4, 8, COLS),
            buf(F32, 4, 8, COLS),
            buf(F32, 4, 8, COLS),
            buf(F32, 4, 8, COLS),
            buf(F32, 2, 8, COLS),
            buf(jnp.int32, 2, 8, MAXLEN),
            pltpu.SemaphoreType.DMA((200,)),
            pltpu.SemaphoreType.DMA((200,)),
            pltpu.SemaphoreType.DMA((2,)),
        ],
        compiler_params=pltpu.CompilerParams(collective_id=0, has_side_effects=True, vmem_limit_bytes=63 * 2**20),
    )(*args)


def split_kernel(res, ig, grad_l, grad_u, grad_f, small, res_o, ig_o, k_o, v_o, q_o, o_o, u_o, f_o, small_o):
    res_o[...] = res[...]
    ig_o[...] = ig[...]
    k_o[...] = grad_l[0:64, :]
    v_o[...] = grad_l[64:128, :]
    q_o[...] = grad_l[128:192, :]
    o_o[...] = grad_l[192:256, :]
    u_o[...] = grad_u[...].T
    f_o[...] = grad_f[0:256, :]
    small_o[0:16, :] = small[...]
    small_o[16:24, :] = grad_f[256:264, :]


def call_split(*args):
    vmem = pl.BlockSpec(memory_space=pltpu.VMEM)
    sizes = [(BLOCK, COLS), (64, COLS), (64, COLS), (64, COLS), (64, COLS), (COLS, UNITS), (UNITS, COLS), (24, COLS)]
    return pl.pallas_call(
        split_kernel,
        out_shape=(jax.ShapeDtypeStruct((BLOCK, COLS), BF16), *(jax.ShapeDtypeStruct(s, F32) for s in sizes)),
        in_specs=[vmem] * 6,
        out_specs=(vmem,) * 9,
        compiler_params=pltpu.CompilerParams(vmem_limit_bytes=32 * 2**20),
    )(*args)


def on_device(
    tokens, ln_gain, ln_bias, w_query, b_query, w_key, b_key, w_value, b_value, w_out, b_out,
    w_fc1, b_fc1, w_fc2, b_fc2, cotangent, lengths, dealing,
):
    wide = lax.axis_index("wide")
    per_seq = MAXLEN // BLOCK
    blocks = jnp.arange(NBLK, dtype=jnp.int32)
    slot_y, slot_z, slot_c = blocks // 8, (blocks // 2) % 4, blocks % 2
    chunk = jnp.stack([(slot_c * 4 + slot_z) * 4 + slot_y, 32 + (slot_c * 4 + slot_y) * 4 + slot_z], 1)
    hit = dealing[None, :] == blocks[:, None]
    there = jnp.sum(jnp.where(hit[:, :, None], chunk[None], 0), 1).reshape(-1)
    logical = jnp.stack([2 * dealing, 2 * dealing + 1], 1).reshape(-1)
    back = jnp.sum(jnp.where(chunk.reshape(-1)[None, :] == jnp.arange(64)[:, None], logical[None, :], 0), 1)
    mine = jnp.sum(jnp.where(blocks == wide, dealing, 0))
    limit = jnp.where(mine // per_seq == 0, lengths[0], lengths[1])
    meta = jnp.concatenate([there, back, jnp.stack([mine % per_seq * BLOCK, limit, lengths[0], lengths[1]])]).astype(jnp.int32)

    half = ROT // 2
    zero = jnp.zeros((5, COLS), F32)
    out_bias = b_out.astype(F32) + b_fc2.astype(F32)
    gb = jnp.concatenate([ln_gain[None], ln_bias[None], out_bias[None], zero], 0)
    bias = jnp.concatenate(
        [
            b_fc1, b_key, b_value, b_query, b_query[half:ROT], b_query[:half], b_key[half:ROT], b_key[:half],
        ]
    ).astype(F32)[None]
    cosine, sine = (
        np.ascontiguousarray(t.reshape(per_seq, 4, PART, 128).transpose(1, 0, 2, 3)).reshape(4, -1, 128)
        for t in rope_tables()
    )
    out = call_block(
        meta, tokens, cotangent, w_query.T, w_key.T, w_value.T, w_fc1, w_out, w_fc2, gb, bias,
        jnp.asarray(cosine), jnp.asarray(sine),
    )
    result, input_grad, key, value, query, proj, up, down, small = call_split(*out)
    sums = small[8]
    return (
        result,
        input_grad,
        small[0],
        small[1],
        query.T,
        sums[384:448],
        key.T,
        sums[256:320],
        value.T,
        sums[320:384],
        proj,
        small[16],
        up,
        sums[0:256],
        down,
        small[16],
    )


def solution(mesh):
    rows, col, units = P("wide", "narrow"), P("narrow"), P("wide")
    weight, out = P("narrow", "wide"), P("wide", "narrow")
    placed = (
        rows, col, col, weight, units, weight, units, weight, units, out, col, weight, units, out, col, rows, P(), P(),
    )
    given = (
        rows, rows, col, col, weight, units, weight, units, weight, units, out, col, weight, units, out, col,
    )
    return jax.shard_map(on_device, mesh=mesh, in_specs=placed, out_specs=given, check_vma=False)
```

time: 567 us -> 174 us (0.31); the launches traced: 559 us -> 173 us
  waiting for transfers between devices: 219 us -> 0 us
  blocking collectives: 94.7 us -> 0 us
  Pallas kernels: 72.2 us -> 151 us
  matrix products: 70.8 us -> 0 us
  other arithmetic: 33.7 us -> 2.16 us
  local copies, waits for them, and re-layouts: 42.1 us -> 15.1 us
  between operations: 18.6 us -> 4.68 us
  starting transfers between devices: 7.88 us -> 0 us
    reduce_scatter x4 -> x0, waiting for transfers between devices: 162 us -> none  [the longest x2 140 us: scatter_rows(): lax.psum_scatter(by_device(x.astype(BF16)), 'wide', scatter_dimension=0,...]
    pallas_call x1 -> x2, Pallas kernels: 72.2 us -> 151 us  [the longest x1 150 us: call_block(): pl.pallas_call(block_kernel, out_shape=(shape((BLOCK, COLS), BF16), shape...]
    psum x2 -> x0, blocking collectives: 73.3 us -> none  [the longest x1 64.1 us: on_device(): lax.psum(jnp.stack([jnp.sum(dln * xhat, 0), jnp.sum(dln, 0)]), 'wide')]
    dot_general x10 -> x0, matrix products: 70.8 us -> none  [the longest x1 16.3 us: on_device(): dp = jnp.dot(do, v.T, preferred_element_type=F32)]
    unnamed x8 -> x0, waiting for transfers between devices: 56.8 us -> none
    all_gather x3 -> x0, blocking collectives: 21.3 us -> none  [the longest x1 8.09 us: on_device(): x2 = lax.all_gather(jnp.sum(tokens.astype(F32) ** 2, 1), 'narrow', axis=0)]
    reduce_sum x8 -> x2, other arithmetic: 11.4 us -> 0.22 us  [the longest x1 0.11 us: on_device(): there = jnp.sum(jnp.where(hit[:, :, None], chunk[None], 0), 1).reshape(-1)]
    slice x19 -> x3, local copies, waits for them, and re-layouts: 11.5 us -> 1.73 us  [the longest x1 0.59 us: on_device(): small[16]]
  transfers between devices with their start and end apart: 8 -> 0, of which waited for: 5 -> 0; matrix products, arithmetic and copies ran while one was open for 9% -> 0% of each run, Pallas kernels for 0% -> 0%
where the time goes in v2:
time: 174 us; the launch traced here: 173 us
  Pallas kernels  151 us (87%)
  local copies, waits for them, and re-layouts  15.1 us (9%)
  between operations  4.68 us (3%)
  other arithmetic  2.16 us (1%)
    pallas_call x1, Pallas kernels, call_block(): pl.pallas_call(block_kernel, out_shape=(shape((BLOCK, COLS), BF16), shape...  150 us
    unnamed x35, local copies, waits for them, and re-layouts  11.3 us

profile of v2, /device:TPU:1, one launch (start us, length us, event | category | flops | bytes accessed | tf_op | source)
XLA Modules:
  0.0 173.0 jit_solution(11033879203644043432)
XLA Ops:
  0.7 0.0 copy-start.16
  0.7 0.1 pad.3.clone
  0.7 0.6 copy-done.16
  1.3 0.0 copy-start.12
  1.3 0.6 copy-done.12
  2.0 0.6 fusion.1
  5.2 0.0 copy-start.7
  5.2 0.6 copy-done.7
  5.9 0.6 fusion.4
  7.8 0.0 copy-start.13
  7.8 0.0 copy-start.14
  7.8 0.6 copy-done.13
  8.5 0.0 copy-done.14
  8.5 0.0 copy-start.8
  8.5 0.0 copy-start.9
  8.5 0.7 copy-done.8
  9.1 0.0 copy-done.9
  9.2 0.1 slice_bitcast_fusion.3
  9.2 0.0 copy-start.15
  9.2 0.7 copy-done.15
  9.9 0.1 concatenate.42
  10.0 0.6 convert_element_type.18.bias
  10.6 0.0 copy-start.10
  10.6 0.0 copy-start.11
  10.6 0.1 select_reduce_fusion.1
  10.7 0.6 copy-done.10
  11.3 0.0 copy-done.11
  11.3 0.7 maximum_maximum_fusion.gb
  12.0 0.1 copy.42
  12.0 0.1 eq.49
  12.1 0.1 copy.41
  12.2 0.1 reshape.298
  12.3 0.1 copy.43
  12.4 0.1 broadcast_in_dim.57
  12.5 0.1 select_reduce_fusion
  12.7 0.7 concatenate.32.meta
  13.3 149.6 %shard_map.315 = (bf16[128,512]{1,0:T(8,128)(2,1)}, f32[128,512]{1,0:T(8,128)}, f32[256,512]{1,0:T(8,128)}, f32[256,512]{1,0:T(8,128)}, f32[288,512]{1,0:T(8,128)}, /*index=5*/f32[16,512]{1,0:T(8,128)}) custom-call(s32[132]{0:T(256)} %concatenate.32.meta, bf16[128,512]{1,0:T(8,128)(2,1)} %tok.1, bf16[128,512]{1,0:T(8,128)(2,1)} %cot.1, ...), custom_call_target="tpu_custom_call" | custom-call | tf_op jit(solution)/shard_map/pallas_call | solution.py:732
  162.9 0.0 copy-start
  162.9 1.1 copy-done
  164.0 0.0 copy-start.1
  164.0 1.0 copy-done.1
  165.0 0.0 copy-start.2
  165.0 1.0 copy-done.2
  166.1 0.0 copy-start.3
  166.1 0.9 copy-done.3
  167.0 0.0 copy-start.4
  167.0 0.9 copy-done.4
  167.9 0.0 copy-start.5
  167.9 0.8 copy-done.5
  168.7 1.4 shard_map.316
  170.1 0.6 slice.75
  170.7 0.6 slice_bitcast_fusion
  171.3 0.6 fusion.3
  171.8 0.0 copy-start.6
  171.8 0.6 copy-done.6
  172.4 0.6 copy.45
  (7 shorter events, 0.1 us)
Async XLA Ops:
  0.7 0.7 copy-start.16
  1.3 0.7 copy-start.12
  5.2 0.7 copy-start.7
  7.8 0.7 copy-start.13
  7.8 0.7 copy-start.14
  8.5 0.7 copy-start.8
  8.5 0.7 copy-start.9
  9.2 0.7 copy-start.15
  10.6 0.7 copy-start.10
  10.6 0.7 copy-start.11
  162.9 1.1 copy-start
  164.0 1.0 copy-start.1
  165.0 1.0 copy-start.2
  166.1 0.9 copy-start.3
  167.0 0.9 copy-start.4
  167.9 0.8 copy-start.5
  171.8 0.6 copy-start.6

commit v3 on v2

v3 whole, which is shorter than its diff:
```python
import jax
import jax.numpy as jnp
import numpy as np
from jax import lax
from jax.experimental import pallas as pl
from jax.experimental.pallas import tpu as pltpu
from jax.sharding import PartitionSpec as P

MESH = pl.DeviceIdType.MESH
D = 2048
HEAD_DIM = 64
ROT = 32
BLOCK = 128
MAXLEN = 2048
NBLK = 32
PART = 32
ROWS = NBLK * PART
COLS = 512
UNITS = 256
EPS = 1e-05
BF16 = jnp.bfloat16
F32 = jnp.float32


def rope_tables():
    half = ROT // 2
    inverse = (10000.0 ** (-(np.arange(half, dtype=np.float32) * np.float32(2.0) / np.float32(ROT)))).astype(np.float32)
    angles = (np.arange(MAXLEN, dtype=np.float32)[:, None] * inverse[None, :]).astype(np.float64)
    cosine = np.ones((MAXLEN, 128), np.float32)
    sine = np.zeros((MAXLEN, 128), np.float32)
    cosine[:, :half] = np.cos(angles)
    cosine[:, half:ROT] = np.cos(angles)
    sine[:, :half] = -np.sin(angles)
    sine[:, half:ROT] = np.sin(angles)
    return cosine, sine


class Net:
    def __init__(self, send, recv):
        self.send, self.recv, self.used, self.open = send, recv, 0, []

    def copy(self, src, dst, device):
        i = self.used
        self.used += 1
        c = pltpu.make_async_remote_copy(
            src_ref=src,
            dst_ref=dst,
            send_sem=self.send.at[i],
            recv_sem=self.recv.at[i],
            device_id=device,
            device_id_type=MESH,
        )
        c.start()
        self.open.append(c)
        return c

    def drain(self):
        for c in self.open:
            c.wait_send()


class Ring:
    def __init__(self, net, me, device, unit, half):
        self.net, self.unit, self.half = net, unit, half
        self.right, self.left = (me + 1) % 4, (me + 3) % 4
        self.to_right, self.to_left = device(self.right), device(self.left)
        self.me = me

    def start(self):
        own = self.unit(self.me)
        self.a = self.net.copy(own, own, self.to_right)
        self.b = self.net.copy(own, own, self.to_left)

    def forward(self):
        self.a.wait_recv()
        x = self.half(self.left, 0)
        self.c = self.net.copy(x, x, self.to_right)
        self.b.wait_recv()
        x = self.half(self.right, 1)
        self.d = self.net.copy(x, x, self.to_left)

    def finish(self):
        self.c.wait_recv()
        self.d.wait_recv()


def coords():
    w, n = lax.axis_index("wide"), lax.axis_index("narrow")
    return w // 8, (w // 2) % 4, w % 2, n


def wide_of(y, z, c):
    return (y * 4 + z) * 2 + c


def aligned(x, m):
    return pl.multiple_of(x, m)


def slot_a(c, z, y):
    return aligned(((c * 4 + z) * 4 + y) * 16, 16)


def slot_b(c, y, z):
    return aligned((32 + (c * 4 + y) * 4 + z) * 16, 16)


class Gather2:
    def __init__(self, net, one, two, first, second, block, half):
        self.net, self.block, self.half = net, block, half
        self.one, self.two = one, two
        self.first = [first((one + j) % 4) for j in range(4)]
        self.second = [second((two + j) % 4) for j in range(4)]
        self.p, self.q, self.r, self.s = {}, {}, {}, {}

    def at(self, j, k):
        return (self.one + j) % 4, (self.two + k) % 4

    def send(self, j):
        x = self.block(*self.at(j, 0))
        self.p[j] = self.net.copy(x, x, self.second[1])
        self.q[j] = self.net.copy(x, x, self.second[3])

    def start(self):
        x = self.block(*self.at(0, 0))
        self.a = self.net.copy(x, x, self.first[1])
        self.b = self.net.copy(x, x, self.first[3])
        self.send(0)

    def near_one(self):
        self.a.wait_recv()
        x = self.half(*self.at(3, 0), 0)
        self.c = self.net.copy(x, x, self.first[1])
        self.send(3)
        self.b.wait_recv()
        x = self.half(*self.at(1, 0), 1)
        self.d = self.net.copy(x, x, self.first[3])
        self.send(1)

    def far_one(self):
        self.c.wait_recv()
        self.d.wait_recv()
        self.send(2)

    def near_two(self, j):
        self.p[j].wait_recv()
        x = self.half(*self.at(j, 3), 0)
        self.r[j] = self.net.copy(x, x, self.second[1])
        self.q[j].wait_recv()
        x = self.half(*self.at(j, 1), 1)
        self.s[j] = self.net.copy(x, x, self.second[3])

    def far_two(self, j):
        self.r[j].wait_recv()
        self.s[j].wait_recv()


class WideGather:
    def __init__(self, net, buf, y, z, c, n):
        self.net, self.buf, self.c = net, buf, c

        def dev(y, z, c):
            return (wide_of(y, z, c), n)

        def block(start):
            return buf.at[pl.ds(start, 16)]

        def half(start, h):
            return buf.at[pl.ds(start, 16), pl.ds(h * 1024, 1024)]

        self.other = dev(y, z, 1 - c)
        self.slots = (slot_a, slot_b)
        self.parts = (
            Gather2(
                net, y, z, lambda i: dev(i, z, c), lambda i: dev(y, i, c),
                lambda i, k: block(slot_a(c, k, i)), lambda i, k, h: half(slot_a(c, k, i), h),
            ),
            Gather2(
                net, z, y, lambda i: dev(y, i, c), lambda i: dev(i, z, c),
                lambda i, k: block(slot_b(c, k, i)), lambda i, k, h: half(slot_b(c, k, i), h),
            ),
        )
        self.crossed = []

    def cross(self, k):
        for part, slot in zip(self.parts, self.slots):
            x = self.buf.at[pl.ds(slot(self.c, (part.two + k) % 4, 0), 64)]
            self.crossed.append(self.net.copy(x, x, self.other))

    def start(self):
        for x in self.parts:
            x.start()

    def near_one(self):
        for x in self.parts:
            x.near_one()

    def far_one(self):
        for x in self.parts:
            x.far_one()
        self.cross(0)

    def near_two(self, j):
        for x in self.parts:
            x.near_two(j)

    def cross_near(self):
        self.cross(3)
        self.cross(1)

    def far_two(self, j):
        for x in self.parts:
            x.far_two(j)
            b = x.block(*x.at(j, 2))
            self.crossed.append(self.net.copy(b, b, self.other))

    def finish(self):
        for x in self.crossed:
            x.wait_recv()


class Scatter:
    def __init__(self, net, me, device, part, rh, rl, rr):
        self.net, self.part, self.rh, self.rl, self.rr = net, part, rh, rl, rr
        self.me, self.right, self.left = me, (me + 1) % 4, (me + 3) % 4
        self.to_right, self.to_left = device(self.right), device(self.left)

    def start(self):
        self.start_far()
        self.start_right()
        self.start_left()

    def start_far(self):
        far = (self.me + 2) % 4
        self.s0 = self.net.copy(self.part(far, 0), self.rh[0], self.to_right)
        self.s1 = self.net.copy(self.part(far, 1), self.rh[1], self.to_left)

    def start_right(self):
        self.a0 = self.net.copy(self.part(self.right, 1), self.rl(1), self.to_right)

    def start_left(self):
        self.a1 = self.net.copy(self.part(self.left, 0), self.rr(0), self.to_left)

    def step(self):
        self.s0.wait_recv()
        p = self.part(self.right, 0)
        p[...] = (p[...].astype(F32) + self.rh[0][...].astype(F32)).astype(BF16)
        self.b0 = self.net.copy(p, self.rl(0), self.to_right)
        self.s1.wait_recv()
        p = self.part(self.left, 1)
        p[...] = (p[...].astype(F32) + self.rh[1][...].astype(F32)).astype(BF16)
        self.b1 = self.net.copy(p, self.rr(1), self.to_left)

    def finish(self):
        for x in (self.a0, self.a1, self.b0, self.b1):
            x.wait_recv()

    def half(self, h):
        return self.part(self.me, h)[...].astype(F32) + (self.rl(h)[...].astype(F32) + self.rr(h)[...].astype(F32))


class WideScatter:
    def __init__(self, net, tile, out, got, own, acc, r1, r2, y, z, c, n):
        self.net, self.tile, self.out, self.got, self.own, self.acc, self.c = net, tile, out, got, own, acc, c

        def dev(y, z, c):
            return (wide_of(y, z, c), n)

        self.other = dev(y, z, 1 - c)

        def cols(ref, start, h):
            return ref.at[pl.ds(aligned(start, 16), 16), pl.ds(h * 1024, 1024)]

        def ring(me, device, part, ref, base):
            return Scatter(
                net, me, device, part, (cols(ref, base, 0), cols(ref, base, 1)),
                lambda h: cols(ref, base + 16, h), lambda h: cols(ref, base + 32, h),
            )

        def first(base, one, two, device, k):
            return {
                j: ring(two, device, lambda i, h, j=j: cols(acc, base + i * 64 + (one + j) % 4 * 16, h), r1.at[k], j * 48)
                for j in (2, 1, 3, 0)
            }

        def second(base, one, two, device, k):
            return ring(one, device, lambda i, h: cols(acc, base + two * 64 + i * 16, h), r2, k * 48)

        def along_y(i):
            return dev(i, z, c)

        def along_z(i):
            return dev(y, i, c)

        self.one = (first(0, y, z, along_z, 0), first(256, z, y, along_y, 1))
        self.two = (second(0, y, z, along_y, 0), second(256, z, y, along_z, 1))

    def exchange(self):
        self.cross = []
        for p in range(2):
            mine = pl.ds(p * 256, 256)
            for i in range(4):
                cs = slice(i * COLS, (i + 1) * COLS)
                self.out[mine, cs] = self.tile(aligned(p * 512 + (1 - self.c) * 256, 256), cs).astype(BF16)
            self.cross.append(self.net.copy(self.out.at[mine], self.got.at[mine], self.other))
        for p in range(2):
            for i in range(4):
                cs = slice(i * COLS, (i + 1) * COLS)
                self.own[p * 256 : p * 256 + 256, cs] = self.tile(aligned(p * 512 + self.c * 256, 256), cs)

    def start(self):
        for p in range(2):
            self.cross[p].wait_recv()

            def add(i, p=p):
                r = pl.ds(aligned(p * 256 + i * 16, 16), 16)
                self.acc[r, :] = (self.own[r, :] + self.got[r, :].astype(F32)).astype(BF16)

            repeat(16, 4, add)
            for j in (2, 1, 3, 0):
                self.one[p][j].start()

    def step(self, j):
        for x in self.one:
            x[j].step()

    def hand_on(self, j):
        for x, t in zip(self.one, self.two):
            r = x[j]
            r.finish()
            for h in range(2):
                r.part(r.me, h)[...] = r.half(h).astype(BF16)
            if j == 2:
                t.start_far()
            if j == 1:
                t.start_right()
            if j == 3:
                t.start_left()

    def second_step(self):
        for r in self.two:
            r.step()

    def finish(self):
        for r in self.two:
            r.finish()

    def result(self, i, cs):
        return self.two[i].half(cs)


def wide_peers(y, z, c):
    for d in range(1, 32):
        yield wide_of((y + d // 8) % 4, (z + d // 2 % 4) % 4, (c + d % 2) % 2)


def greet(y, z, c, n):
    barrier = pltpu.get_barrier_semaphore()
    for w in wide_peers(y, z, c):
        pl.semaphore_signal(barrier, inc=1, device_id=(w, n), device_id_type=MESH)
    for j in (1, 2, 3):
        pl.semaphore_signal(barrier, inc=1, device_id=(wide_of(y, z, c), (n + j) % 4), device_id_type=MESH)
    pl.semaphore_wait(barrier, 34)


def repeat(count, step, body):
    def turn(i, _):
        for j in range(step):
            body(i * step + j)
        return 0

    lax.fori_loop(0, count // step, turn, 0)


def nt(a, b):
    return lax.dot_general(a, b, (((1,), (1,)), ((), ())), preferred_element_type=F32)


GELU_A = float(np.sqrt(2.0 / np.pi))
GELU_B = 0.044715


def dot(a, b):
    return jnp.dot(a, b, preferred_element_type=F32)


def lanes(shape):
    return lax.broadcasted_iota(jnp.int32, shape, len(shape) - 1)


def swap(x):
    return jnp.where(lanes(x.shape) < ROT // 2, pltpu.roll(x, 128 - ROT // 2, 1), pltpu.roll(x, ROT // 2, 1))


def block_kernel(
    dealing, lengths, tok, cot, wq, wk, wv, wu, wo, wd, v_gain, v_bias, b_q, b_k, b_v, b_o, b_u, b_d, cos_all, sin_all,
    res, ig, grad_l, grad_u, grad_f, small, norm,
    ln, g, w, wm, wmo, xs, gbs, xhat, cosine, sine, pre, slope, hb, dpre, kv, kk, xq, xd, od, dkvt, dkv, dkvp,
    rdkv, sum_f, sum_u, sum_l, r_f, r_u, r_l, out_1, got_1, acc_1, r1_1, r2_1, out_2, got_2, acc_2, r1_2, r2_2, own,
    trans, cmask, bsend, bfin, csend, cfin, ssend, srecv, brecv, wrecv, bias, index, there, kpos, send, recv, local,
):
    y, z, c, n = coords()
    net = Net(send, recv)
    my_cols = pl.ds(aligned(n * COLS, COLS), COLS)
    me = wide_of(y, z, c)
    own_a, own_b = slot_a(c, z, y), slot_b(c, y, z)

    def to(m):
        return (me, m)

    def w_cols(i):
        return pl.ds(aligned(i * COLS, COLS), COLS)

    def share(i):
        return pl.ds(aligned(i * PART, PART), PART)

    tables = [
        pltpu.make_async_copy(cos_all.at[n], cosine, local.at[0]),
        pltpu.make_async_copy(sin_all.at[n], sine, local.at[1]),
    ]
    for t in tables:
        t.start()
    w[256:320, my_cols] = wk[...]
    w[320:384, my_cols] = wv[...]
    w[384:448, my_cols] = wq[...]
    w[0:256, my_cols] = wu[...].T
    wm[0:256, my_cols] = wd[...]
    wm[256:320, my_cols] = wo[...]
    gbs[n, 0:1, :] = v_gain[...]
    gbs[n, 1:2, :] = v_bias[...]
    xs[:, my_cols] = tok[share(n), :]
    row = lax.broadcasted_iota(jnp.int32, (BLOCK, COLS), 0)
    block = dealing[me]
    valid = block % (MAXLEN // BLOCK) * BLOCK + row < jnp.where(block < MAXLEN // BLOCK, lengths[0], lengths[1])
    cmask[...] = jnp.where(valid, cot[...], jnp.zeros_like(cot))
    mine = cmask[share(n), :]
    g[pl.ds(own_a, 16), my_cols] = mine[0:16]
    g[pl.ds(own_b, 16), my_cols] = mine[16:32]
    greet(y, z, c, n)

    early, late = [], []
    for j in (1, 3, 2):
        m = (n + j) % 4
        early.append(net.copy(gbs.at[n], gbs.at[n], to(m)))
        early.append(net.copy(tok.at[share(m)], xs.at[:, my_cols], to(m)))
    for j in (1, 3, 2):
        m = (n + j) % 4
        late.append(net.copy(cmask.at[pl.ds(aligned(m * PART, 16), 16)], g.at[pl.ds(own_a, 16), my_cols], to(m)))
        late.append(net.copy(cmask.at[pl.ds(aligned(m * PART + 16, 16), 16)], g.at[pl.ds(own_b, 16), my_cols], to(m)))
    a_ring = Ring(net, n, to, lambda i: w.at[pl.ds(256, 192), w_cols(i)], lambda i, h: w.at[pl.ds(256 + h * 96, 96), w_cols(i)])
    u_ring = Ring(net, n, to, lambda i: w.at[pl.ds(0, 256), w_cols(i)], lambda i, h: w.at[pl.ds(h * 128, 128), w_cols(i)])
    d_ring = Ring(net, n, to, lambda i: wm.at[pl.ds(0, 256), w_cols(i)], lambda i, h: wm.at[pl.ds(h * 128, 128), w_cols(i)])
    o_ring = Ring(net, n, to, lambda i: wm.at[pl.ds(256, 64), w_cols(i)], lambda i, h: wm.at[pl.ds(256 + h * 32, 32), w_cols(i)])
    kv_ring = [
        Ring(
            net, n, to,
            lambda i, s=s: kv.at[i, pl.ds(s * 512, 512)],
            lambda i, h, s=s: kv.at[i, pl.ds(s * 512 + h * 256, 256)],
        )
        for s in range(2)
    ]
    a_ring.start()
    u_ring.start()
    o_ring.start()

    at = lanes((8, 128))
    part = lax.broadcasted_iota(jnp.int32, (8, 128), 0)
    found = jnp.zeros((8, 128), jnp.int32)
    for b in range(NBLK):
        sy, sz, sc = b // 8, b // 2 % 4, b % 2
        found = jnp.where((part < 2) & (at == dealing[b]), jnp.where(part == 0, (sc * 4 + sz) * 4 + sy, 32 + (sc * 4 + sy) * 4 + sz), found)
        found = jnp.where((part == 2) & (at == (sc * 4 + sz) * 4 + sy), 2 * dealing[b], found)
        found = jnp.where((part == 2) & (at == 32 + (sc * 4 + sy) * 4 + sz), 2 * dealing[b] + 1, found)
    index[...] = found
    to_scalars = pltpu.make_async_copy(index, there, local.at[2])
    to_scalars.start()
    half = ROT // 2
    bias[:, 0:256] = b_u[...].astype(F32)
    bias[:, 256:320] = b_k[...].astype(F32)
    bias[:, 320:384] = b_v[...].astype(F32)
    bias[:, 384:448] = b_q[...].astype(F32)
    bias[:, 448:464] = b_q[:, half:ROT].astype(F32)
    bias[:, 464:480] = b_q[:, 0:half].astype(F32)
    bias[:, 480:496] = b_k[:, half:ROT].astype(F32)
    bias[:, 496:512] = b_k[:, 0:half].astype(F32)
    for s in range(2):
        at = lanes((8, MAXLEN))
        kpos[s] = jnp.where(at < lengths[s], at, 1 << 20)
    wmo[0:64, :] = jnp.zeros((64, D), BF16)

    for x in early:
        x.wait_recv()
    x = xs[...].astype(F32)
    mean = jnp.sum(x, 1, keepdims=True) / D
    var = jnp.sum(x * x, 1, keepdims=True) / D - mean * mean
    inv = lax.rsqrt(var + EPS)
    xhat[...] = (x - mean) * inv
    for i in range(4):
        cs = slice(i * COLS, (i + 1) * COLS)
        low = (xhat[:, cs] * gbs[i, 0:1, :] + gbs[i, 1:2, :]).astype(BF16)
        ln[pl.ds(own_a, 16), cs] = low[0:16]
        ln[pl.ds(own_b, 16), cs] = low[16:32]

    lg = WideGather(net, ln, y, z, c, n)
    gg = WideGather(net, g, y, z, c, n)
    lg.start()
    for t in tables:
        t.wait()
    to_scalars.wait()
    lg.near_one()
    a_ring.forward()
    lg.near_two(0)
    lg.far_one()
    lg.near_two(3)
    lg.near_two(1)
    for x in late:
        x.wait_recv()
    u_ring.forward()
    o_ring.forward()
    lg.near_two(2)
    lg.cross_near()
    gg.start()
    for j in (0, 3, 1, 2):
        lg.far_two(j)
    d_ring.start()
    a_ring.finish()
    gg.near_one()

    w[448:640, :] = w[256:448, :]
    w[640:656, :] = w[400:416, :]
    w[656:672, :] = w[384:400, :]
    w[672:688, :] = w[272:288, :]
    w[688:704, :] = w[256:272, :]

    gg.near_two(0)
    gg.far_one()
    lg.finish()

    def project(i, _):
        r = pl.ds(aligned(i * 256, 256), 256)
        pre[pl.ds(i * 16, 16)] = (nt(ln[r, :], w[448:704, :]) + bias[:, 256:512]).reshape(16, 16, 256)
        return 0

    lax.fori_loop(0, 4, project, 0)

    def arrange(i):
        both = pre[there[i % 2, i // 2]]
        r = pl.ds(aligned(i * 16, 16), 16)
        tab = pl.ds(aligned((i % 32) * 16, 16), 16)
        a, b = both[:, 0:128], both[:, 128:256]
        cs, sn = cosine[tab, :], sine[tab, :]
        kv[n, r, :] = (a * cs + pltpu.roll(b, 32, 1) * sn).astype(BF16)
        q = (b * cs + pltpu.roll(b, 64, 1) * sn) * (HEAD_DIM**-0.5)
        xq[r, :] = jnp.where(lanes((16, 128)) < HEAD_DIM, q, 0.0).astype(BF16)

    repeat(32, 8, arrange)
    kv_ring[0].start()
    gg.near_two(3)
    gg.near_two(1)
    repeat(32, 8, lambda i: arrange(i + 32))
    kv_ring[1].start()
    gg.near_two(2)
    gg.cross_near()
    u_ring.finish()

    def units(i, _):
        r = pl.ds(aligned(i * 256, 256), 256)
        v = nt(ln[r, :], w[0:256, :]) + bias[:, 0:256]
        t = jnp.tanh(GELU_A * (v + GELU_B * (v * v * v)))
        hb[r, :] = (0.5 * v * (1.0 + t)).astype(BF16)
        slope[r, :] = 0.5 * (1.0 + t) + 0.5 * v * (1.0 - t * t) * (GELU_A * (1.0 + 3.0 * GELU_B * (v * v)))
        return 0

    lax.fori_loop(0, 4, units, 0)
    kv_ring[0].forward()
    for j in (0, 3, 1, 2):
        gg.far_two(j)
    d_ring.forward()
    o_ring.finish()
    wmo[64:128, :] = wm[256:320, :]
    gg.finish()

    def grad_o(i, _):
        r = pl.ds(aligned(i * 256, 256), 256)
        pre[pl.ds(i * 16, 16), :, 0:128] = nt(g[r, :], wmo[...]).reshape(16, 16, 128)
        return 0

    lax.fori_loop(0, 4, grad_o, 0)

    def arrange_do(i):
        xd[pl.ds(aligned(i * 16, 16), 16), :] = pre[there[i % 2, i // 2], :, 0:128].astype(BF16)

    repeat(64, 8, arrange_do)
    kv_ring[1].forward()

    def scatter_cols(buf, count, r):
        half = count // 2
        return Scatter(
            net, n, to,
            lambda i, h: buf.at[pl.ds(h * half, half), w_cols(i)],
            (r.at[0, pl.ds(0, half)], r.at[0, pl.ds(half, half)]),
            lambda h: r.at[1, pl.ds(h * half, half)],
            lambda h: r.at[2, pl.ds(h * half, half)],
        )

    f_sum = scatter_cols(sum_f, 288, r_f)
    u_sum = scatter_cols(sum_u, 256, r_u)
    l_sum = scatter_cols(sum_l, 256, r_l)

    def gather_keys(i):
        for m in range(4):
            kk[pl.ds(aligned(i * BLOCK + m * PART, PART), PART), :] = kv[m, share(i), :]

    def attend(s, t):
        keys = 512 * (t + 1)
        r = pl.ds(s * 512 + t * 128, 128)
        x = jnp.concatenate([xq[r, :], xd[r, :]], 0)
        near = kk[pl.ds(s * MAXLEN, keys), :]
        both = nt(x, near)
        i = lax.broadcasted_iota(jnp.int32, (128, 1), 0)
        qpos = (4 * t + i // PART) * BLOCK + n * PART + i % PART
        scores = jnp.where(kpos[s, 0:1, 0:keys] <= qpos, both[0:128], -1e30)
        e = jnp.exp(scores - jnp.max(scores, 1, keepdims=True))
        p = e * (1.0 / jnp.sum(e, 1, keepdims=True))
        dp = both[128:256]
        ds = p * (dp - jnp.sum(p * dp, 1, keepdims=True))
        yy = jnp.concatenate([ds.astype(BF16), p.astype(BF16)], 0)
        back = dot(yy, near)
        back = jnp.where(lanes((128, 128)) < HEAD_DIM, back[0:128] * (HEAD_DIM**-0.5), back[128:256])
        od[pl.ds(s * 32 + t * 8, 8)] = back.reshape(8, 16, 128)
        grads = dot(x.T, yy)
        if t == 3:
            dkvt[s, :, 0:keys] = grads
        else:
            dkvt[s, :, 0:keys] += grads

    def key_sum(s):
        return Scatter(
            net, n, to,
            lambda i, h: dkv.at[i, pl.ds(s * 512 + h * 256, 256)],
            (rdkv.at[0, pl.ds(s * 512, 256)], rdkv.at[0, pl.ds(s * 512 + 256, 256)]),
            lambda h: rdkv.at[1, pl.ds(s * 512 + h * 256, 256)],
            lambda h: rdkv.at[2, pl.ds(s * 512 + h * 256, 256)],
        )

    def weight_f(i, _):
        cs = pl.ds(aligned(i * COLS, COLS), COLS)
        sum_f[0:256, cs] = dot(trans[...], g[:, cs]).astype(BF16)
        sum_f[256:288, cs] = dot(jnp.ones((32, ROWS), BF16), g[:, cs]).astype(BF16)
        return 0

    kv_sum = [key_sum(0), key_sum(1)]
    for s in range(2):
        kv_ring[s].finish()
        repeat(16, 4, lambda i, s=s: gather_keys(i + 16 * s))
        for t in (3, 2, 1, 0):
            attend(s, t)

        def turn_keys(i, s=s):
            t = dkvt[s, :, pl.ds(aligned(i * BLOCK, BLOCK), BLOCK)].T.astype(BF16)
            for m in range(4):
                dkv[m, pl.ds(aligned(s * 512 + i * PART, PART), PART), :] = t[m * PART : (m + 1) * PART]

        repeat(16, 4, turn_keys)
        kv_sum[s].start()
        if s == 0:
            trans[...] = hb[...].T
            lax.fori_loop(0, 4, weight_f, 0)
            f_sum.start()
            d_ring.finish()

    def grad_units(i, _):
        r = pl.ds(aligned(i * 256, 256), 256)
        dpre[r, 0:256] = (nt(g[r, :], wm[0:256, :]) * slope[r, :]).astype(BF16)
        return 0

    lax.fori_loop(0, 4, grad_units, 0)
    kv_sum[0].step()

    def unrope(i):
        tab = pl.ds(aligned((i % 32) * 16, 16), 16)
        x = od[i]
        od[i] = x * cosine[tab, :] - swap(x) * sine[tab, :]

    repeat(64, 8, unrope)

    def place(i):
        dpre[pl.ds(aligned(i * 16, 16), 16), 384:512] = od[there[2, i]].astype(BF16)

    repeat(64, 8, place)
    kv_sum[1].step()

    def branch_tile(start, cs):
        r = pl.ds(start, 256)
        return dot(hb[r, :], wm[0:256, cs]) + dot(dpre[r, 384:512], wmo[:, cs])

    branch = WideScatter(net, branch_tile, out_1, got_1, own, acc_1, r1_1, r2_1, y, z, c, n)
    branch.exchange()
    branch.start()
    trans[...] = dpre[:, 0:256].T

    def weight_u(i, _):
        cs = pl.ds(aligned(i * COLS, COLS), COLS)
        sum_u[:, cs] = dot(trans[...], ln[:, cs]).astype(BF16)
        return 0

    lax.fori_loop(0, 4, weight_u, 0)
    u_sum.start()
    def unrope_keys(i):
        tab = pl.ds(aligned((i % 32) * 16, 16), 16)
        r = pl.ds(aligned(i * 16, 16), 16)
        x = dkv[n, r, :].astype(F32) + (rdkv[1, r, :].astype(F32) + rdkv[2, r, :].astype(F32))
        dkvp[i] = x * cosine[tab, :] - swap(x) * sine[tab, :]

    for s in range(2):
        kv_sum[s].finish()
        repeat(32, 8, lambda i, s=s: unrope_keys(i + 32 * s))

    def place_keys(i):
        dpre[pl.ds(aligned(i * 16, 16), 16), 256:384] = dkvp[there[2, i]].astype(BF16)

    repeat(64, 8, place_keys)

    def dln_tile(start, cs):
        r = pl.ds(start, 256)
        return dot(dpre[r, 0:448], w[0:448, cs])

    dln = WideScatter(net, dln_tile, out_2, got_2, own, acc_2, r1_2, r2_2, y, z, c, n)
    dln.exchange()
    for j in (2, 1, 3, 0):
        branch.step(j)
    dln.start()
    f_sum.step()
    u_sum.step()
    for j in (2, 1, 3, 0):
        branch.hand_on(j)
    trans[...] = dpre[:, 256:512].T

    def weight_l(i, _):
        cs = pl.ds(aligned(i * COLS, COLS), COLS)
        sum_l[0:192, cs] = dot(trans[0:192, :], ln[:, cs]).astype(BF16)
        sum_l[192:256, cs] = dot(trans[192:256, :], g[:, cs]).astype(BF16)
        return 0

    lax.fori_loop(0, 4, weight_l, 0)
    l_sum.start()
    for j in (2, 1, 3, 0):
        dln.step(j)
    branch.second_step()
    for j in (2, 1, 3, 0):
        dln.hand_on(j)
    brecv[n] = jnp.broadcast_to(jnp.sum(dpre[...].astype(F32), 0, keepdims=True), (8, COLS))
    late = []
    for j in (1, 3, 2):
        late.append(net.copy(brecv.at[n], brecv.at[n], to((n + j) % 4)))
    dln.second_step()
    branch.finish()
    for i in range(2):
        for h in range(2):
            bsend[i * 16 : (i + 1) * 16, h * 1024 : (h + 1) * 1024] = branch.result(i, h).astype(BF16)
    bfin[share(n), :] = bsend[:, my_cols]
    for j in (1, 3, 2):
        m = (n + j) % 4
        late.append(net.copy(bsend.at[:, w_cols(m)], bfin.at[share(n)], to(m)))
    l_sum.step()
    dln.finish()

    for i in range(2):
        for h in range(2):
            csend[i * 16 : (i + 1) * 16, h * 1024 : (h + 1) * 1024] = dln.result(i, h)
    grad = csend[...]
    sums = (jnp.sum(grad * xhat[...], 0, keepdims=True), jnp.sum(grad, 0, keepdims=True))
    for m in range(4):
        for k in range(2):
            for i in range(4):
                ssend[m, 4 * k + i : 4 * k + i + 1, :] = sums[k][:, m * COLS + i * 128 : m * COLS + i * 128 + 128]
    srecv[n] = ssend[n]
    last = []
    for j in (1, 3, 2):
        m = (n + j) % 4
        last.append(net.copy(ssend.at[m], srecv.at[n], to(m)))
    for j in range(4):
        cs = slice(j * COLS, (j + 1) * COLS)
        csend[:, cs] = csend[:, cs] * gbs[j, 0:1, :]
    grad = csend[...]
    first = jnp.sum(grad, 1, keepdims=True) / D
    second = jnp.sum(grad * xhat[...], 1, keepdims=True) / D
    x = xs[...].astype(F32)
    mean = jnp.sum(x, 1, keepdims=True) / D
    var = jnp.sum(x * x, 1, keepdims=True) / D - mean * mean
    csend[...] = lax.rsqrt(var + EPS) * (grad - first - xhat[...] * second)
    cfin[share(n), :] = csend[:, my_cols]
    final = []
    for j in (1, 3, 2):
        m = (n + j) % 4
        final.append(net.copy(csend.at[:, w_cols(m)], cfin.at[share(n)], to(m)))
    for x in last:
        x.wait_recv()
    wrecv[me] = (srecv[0] + srecv[1]) + (srecv[2] + srecv[3])
    last = [net.copy(wrecv.at[me], wrecv.at[me], (p, n)) for p in wide_peers(y, z, c)]
    f_sum.finish()
    for h in range(2):
        grad_f[h * 144 : (h + 1) * 144, :] = f_sum.half(h)
    u_sum.finish()
    for h in range(2):
        grad_u[h * 128 : (h + 1) * 128, :] = u_sum.half(h)
    l_sum.finish()
    for h in range(2):
        grad_l[h * 128 : (h + 1) * 128, :] = l_sum.half(h)
    for x in late:
        x.wait_recv()
    block = dealing[me]
    valid = block % (MAXLEN // BLOCK) * BLOCK + row < jnp.where(block < MAXLEN // BLOCK, lengths[0], lengths[1])
    base = bfin[...].astype(F32) + (b_o[...].astype(F32) + b_d[...].astype(F32))
    res[...] = (tok[...].astype(F32) + jnp.where(valid, base, 0.0)).astype(BF16)
    small[...] = (brecv[0] + brecv[1]) + (brecv[2] + brecv[3])
    for x in final:
        x.wait_recv()
    ig[...] = cot[...].astype(F32) + cfin[...]
    for x in last:
        x.wait_recv()
    norm[...] = jnp.sum(wrecv[...], 0)
    net.drain()


def call_block(*args):
    vmem, anywhere = pl.BlockSpec(memory_space=pltpu.VMEM), pl.BlockSpec(memory_space=pl.ANY)
    shape = jax.ShapeDtypeStruct

    def buf(dtype, *size):
        return pltpu.VMEM(size, dtype)

    wide = [buf(BF16, 512, D), buf(BF16, 512, D), buf(BF16, 512, D), buf(BF16, 2, 192, D), buf(BF16, 96, D)]
    return pl.pallas_call(
        block_kernel,
        out_shape=(
            shape((BLOCK, COLS), BF16),
            shape((BLOCK, COLS), F32),
            shape((256, COLS), F32),
            shape((256, COLS), F32),
            shape((288, COLS), F32),
            shape((8, COLS), F32),
            shape((8, 128), F32),
        ),
        in_specs=[pl.BlockSpec(memory_space=pltpu.SMEM)] * 2 + [vmem] * 16 + [anywhere] * 2,
        out_specs=(vmem,) * 7,
        scratch_shapes=[
            buf(BF16, ROWS, D),
            buf(BF16, ROWS, D),
            buf(BF16, 704, D),
            buf(BF16, 320, D),
            buf(BF16, 128, D),
            buf(BF16, PART, D),
            buf(F32, 4, 8, COLS),
            buf(F32, PART, D),
            buf(F32, 512, 128),
            buf(F32, 512, 128),
            buf(F32, 64, 16, 256),
            buf(F32, ROWS, UNITS),
            buf(BF16, ROWS, UNITS),
            buf(BF16, ROWS, 512),
            buf(BF16, 4, ROWS, 128),
            buf(BF16, 2 * MAXLEN, 128),
            buf(BF16, ROWS, 128),
            buf(BF16, ROWS, 128),
            buf(F32, 64, 16, 128),
            buf(F32, 2, 128, MAXLEN),
            buf(BF16, 4, ROWS, 128),
            buf(F32, 64, 16, 128),
            buf(BF16, 3, ROWS, 128),
            buf(BF16, 288, D),
            buf(BF16, 256, D),
            buf(BF16, 256, D),
            buf(BF16, 3, 288, COLS),
            buf(BF16, 3, 256, COLS),
            buf(BF16, 3, 256, COLS),
            *wide,
            *wide,
            buf(F32, 512, D),
            buf(BF16, 256, ROWS),
            buf(BF16, BLOCK, COLS),
            buf(BF16, PART, D),
            buf(BF16, BLOCK, COLS),
            buf(F32, PART, D),
            buf(F32, BLOCK, COLS),
            buf(F32, 4, 8, 128),
            buf(F32, 4, 8, 128),
            buf(F32, 4, 8, COLS),
            buf(F32, 32, 8, 128),
            buf(F32, 1, COLS),
            buf(jnp.int32, 8, 128),
            pltpu.SMEM((8, 128), jnp.int32),
            buf(jnp.int32, 2, 8, MAXLEN),
            pltpu.SemaphoreType.DMA((400,)),
            pltpu.SemaphoreType.DMA((400,)),
            pltpu.SemaphoreType.DMA((3,)),
        ],
        compiler_params=pltpu.CompilerParams(collective_id=0, has_side_effects=True, vmem_limit_bytes=63 * 2**20),
    )(*args)


def split_kernel(
    res, ig, grad_l, grad_u, grad_f, small, norm,
    res_o, ig_o, gain_o, bias_o, q_o, bq_o, k_o, bk_o, v_o, bv_o, o_o, bo_o, u_o, bu_o, f_o, bf_o,
):
    res_o[...] = res[...]
    ig_o[...] = ig[...]
    k_o[...] = grad_l[0:64, :]
    v_o[...] = grad_l[64:128, :]
    q_o[...] = grad_l[128:192, :]
    o_o[...] = grad_l[192:256, :]
    u_o[...] = grad_u[...].T
    f_o[...] = grad_f[0:256, :]
    for i in range(4):
        gain_o[:, i * 128 : i * 128 + 128] = norm[i : i + 1, :]
        bias_o[:, i * 128 : i * 128 + 128] = norm[4 + i : 5 + i, :]
    bu_o[...] = small[0:1, 0:256]
    bk_o[...] = small[0:1, 256:320]
    bv_o[...] = small[0:1, 320:384]
    bq_o[...] = small[0:1, 384:448]
    bo_o[...] = grad_f[256:257, :]
    bf_o[...] = grad_f[256:257, :]


def call_split(*args):
    vmem = pl.BlockSpec(memory_space=pltpu.VMEM)
    head, vector = (64, COLS), (1, COLS)
    sizes = [
        (BLOCK, COLS), vector, vector, head, (1, 64), head, (1, 64), head, (1, 64), head, vector,
        (COLS, UNITS), (1, UNITS), (UNITS, COLS), vector,
    ]
    return pl.pallas_call(
        split_kernel,
        out_shape=(jax.ShapeDtypeStruct((BLOCK, COLS), BF16), *(jax.ShapeDtypeStruct(s, F32) for s in sizes)),
        in_specs=[vmem] * 7,
        out_specs=(vmem,) * 16,
        compiler_params=pltpu.CompilerParams(vmem_limit_bytes=62 * 2**20),
    )(*args)


def on_device(
    tokens, ln_gain, ln_bias, w_query, b_query, w_key, b_key, w_value, b_value, w_out, b_out,
    w_fc1, b_fc1, w_fc2, b_fc2, cotangent, lengths, dealing,
):
    cosine, sine = (
        np.ascontiguousarray(t.reshape(MAXLEN // BLOCK, 4, PART, 128).transpose(1, 0, 2, 3)).reshape(4, -1, 128)
        for t in rope_tables()
    )
    out = call_block(
        dealing, lengths, tokens, cotangent, w_query.T, w_key.T, w_value.T, w_fc1, w_out, w_fc2,
        ln_gain[None], ln_bias[None], b_query[None], b_key[None], b_value[None], b_out[None], b_fc1[None], b_fc2[None],
        jnp.asarray(cosine), jnp.asarray(sine),
    )
    out = list(call_split(*out))
    for i in (4, 6, 8):
        out[i] = out[i].T
    for i in (2, 3, 5, 7, 9, 11, 13, 15):
        out[i] = out[i][0]
    return tuple(out)


def solution(mesh):
    rows, col, units = P("wide", "narrow"), P("narrow"), P("wide")
    weight, out = P("narrow", "wide"), P("wide", "narrow")
    placed = (
        rows, col, col, weight, units, weight, units, weight, units, out, col, weight, units, out, col, rows, P(), P(),
    )
    given = (
        rows, rows, col, col, weight, units, weight, units, weight, units, out, col, weight, units, out, col,
    )
    return jax.shard_map(on_device, mesh=mesh, in_specs=placed, out_specs=given, check_vma=False)
```

time: 174 us -> 125 us (0.72)
  Pallas kernels: 151 us -> 121 us
  local copies, waits for them, and re-layouts: 15.1 us -> 2.59 us
  between operations: 4.68 us -> 0.82 us
  other arithmetic: 2.16 us -> 0 us
    pallas_call x1, Pallas kernels: 150 us -> 118 us  [call_block(): pl.pallas_call(block_kernel, out_shape=(shape((BLOCK, COLS), BF16), shape...]
    unnamed x35 -> x6, local copies, waits for them, and re-layouts: 11.3 us -> 0.86 us
    slice x4 -> x0, local copies, waits for them, and re-layouts: 2.31 us -> none  [the longest x1 0.59 us: on_device(): small[16]]
where the time goes in v3:
time: 125 us
  Pallas kernels  121 us (97%)
  local copies, waits for them, and re-layouts  2.59 us (2%)
    pallas_call x1, Pallas kernels, call_block(): pl.pallas_call(block_kernel, out_shape=(shape((BLOCK, COLS), BF16), shape...  118 us
    pallas_call x1, Pallas kernels, call_split(): pl.pallas_call(split_kernel, out_shape=(jax.ShapeDtypeStruct((BLOCK, COLS...  2.98 us

profile of v3, /device:TPU:1, one launch (start us, length us, event | category | flops | bytes accessed | tf_op | source)
XLA Modules:
  0.0 124.8 jit_solution(8120849286984484722)
XLA Ops:
  0.6 0.0 copy-start.2
  0.7 0.6 copy-done.2
  1.3 0.0 copy-start
  1.3 0.6 broadcast_in_dim.30.b_u
  1.9 0.1 copy-done
  2.0 0.0 copy-start.1
  2.0 0.6 broadcast_in_dim.29.b_o
  2.6 0.1 copy-done.1
  2.7 0.6 broadcast_in_dim.31.b_d
  3.2 118.4 %shard_map.315 = (bf16[128,512]{1,0:T(8,128)(2,1)}, f32[128,512]{1,0:T(8,128)}, f32[256,512]{1,0:T(8,128)}, f32[256,512]{1,0:T(8,128)}, f32[288,512]{1,0:T(8,128)}, /*index=5*/f32[8,512]{1,0:T(8,128)}, f32[8,128]{1,0:T(8,128)}) custom-call(s32[32]{0:T(128)} %dealing.1, s32[2]{0:T(128)} %lengths.1, bf16[128,512]{1,0:T(8,128)(2,1)} %tok.1, ...), custom_call_target="tpu_custom_call" | custom-call | tf_op jit(solution)/shard_map/pallas_call | solution.py:834
  121.7 3.0 %shard_map.316 = (bf16[128,512]{1,0:T(8,128)(2,1)}, f32[128,512]{1,0:T(8,128)}, f32[1,512]{1,0:T(1,128)}, f32[1,512]{1,0:T(1,128)}, f32[64,512]{1,0:T(8,128)}, /...) custom-call(bf16[128,512]{1,0:T(8,128)(2,1)} %get-tuple-element.39.r, ...), custom_call_target="tpu_custom_call" | custom-call | tf_op jit(solution)/shard_map/pallas_call | solution.py:932
Async XLA Ops:
  0.6 0.7 copy-start.2
  1.3 0.7 copy-start
  2.0 0.7 copy-start.1

commit v4 on v3

v4 whole, which is shorter than its diff:
```python
import jax
import jax.numpy as jnp
import numpy as np
from jax import lax
from jax.experimental import pallas as pl
from jax.experimental.pallas import tpu as pltpu
from jax.sharding import PartitionSpec as P

MESH = pl.DeviceIdType.MESH
D = 2048
HEAD_DIM = 64
ROT = 32
BLOCK = 128
MAXLEN = 2048
NBLK = 32
PART = 32
ROWS = NBLK * PART
COLS = 512
UNITS = 256
EPS = 1e-05
SENDS, ARRIVALS = 16, 142
BF16 = jnp.bfloat16
F32 = jnp.float32


def rope_tables():
    half = ROT // 2
    inverse = (10000.0 ** (-(np.arange(half, dtype=np.float32) * np.float32(2.0) / np.float32(ROT)))).astype(np.float32)
    angles = (np.arange(MAXLEN, dtype=np.float32)[:, None] * inverse[None, :]).astype(np.float64)
    cosine = np.ones((MAXLEN, 128), np.float32)
    sine = np.zeros((MAXLEN, 128), np.float32)
    cosine[:, :half] = np.cos(angles)
    cosine[:, half:ROT] = np.cos(angles)
    sine[:, :half] = -np.sin(angles)
    sine[:, half:ROT] = np.sin(angles)
    return cosine, sine


class Net:
    def __init__(self, send, recv, anyone):
        self.send, self.recv, self.anyone = send, recv, anyone
        self.groups = self.slots = 0

    def group(self):
        self.groups += 1
        return self.groups - 1

    def slot(self):
        self.slots += 1
        return self.slots - 1

    def make(self, src, dst, device, group, slot):
        return pltpu.make_async_remote_copy(
            src_ref=src,
            dst_ref=dst,
            send_sem=self.send.at[group],
            recv_sem=self.recv.at[slot],
            device_id=device,
            device_id_type=MESH,
        )

    def copy(self, src, dst, device, group, slot):
        self.make(src, dst, device, group, slot).start()

    def arrived(self, ref, slot):
        self.make(ref, ref, self.anyone, 0, slot).wait_recv()

    def sent(self, ref, group):
        self.make(ref, ref, self.anyone, group, 0).wait_send()


class Ring:
    def __init__(self, net, group, me, device, unit, half):
        self.net, self.group, self.unit, self.half = net, group, unit, half
        self.me, self.right, self.left = me, (me + 1) % 4, (me + 3) % 4
        self.to_right, self.to_left = device(self.right), device(self.left)
        self.a, self.b, self.c = net.slot(), net.slot(), net.slot()

    def send(self, x, device, slot):
        self.net.copy(x, x, device, self.group, slot)

    def start(self):
        own = self.unit(self.me)
        self.send(own, self.to_right, self.a)
        self.send(own, self.to_left, self.b)

    def forward(self):
        self.net.arrived(self.unit(self.left), self.a)
        self.send(self.half(self.left, 0), self.to_right, self.c)
        self.net.arrived(self.unit(self.right), self.b)
        self.send(self.half(self.right, 1), self.to_left, self.c)

    def finish(self):
        self.net.arrived(self.unit((self.me + 2) % 4), self.c)


def coords():
    w, n = lax.axis_index("wide"), lax.axis_index("narrow")
    return w // 8, (w // 2) % 4, w % 2, n


def wide_of(y, z, c):
    return (y * 4 + z) * 2 + c


def aligned(x, m):
    return pl.multiple_of(x, m)


def slot_a(c, z, y):
    return aligned(((c * 4 + z) * 4 + y) * 16, 16)


def slot_b(c, y, z):
    return aligned((32 + (c * 4 + y) * 4 + z) * 16, 16)


class Gather2:
    def __init__(self, net, group, one, two, first, second, block, half):
        self.net, self.group, self.block, self.half = net, group, block, half
        self.one, self.two = one, two
        self.first = [first((one + j) % 4) for j in range(4)]
        self.second = [second((two + j) % 4) for j in range(4)]
        self.a, self.b, self.c = net.slot(), net.slot(), net.slot()
        self.p, self.q, self.r = ([net.slot() for _ in range(4)] for _ in range(3))

    def at(self, j, k):
        return (self.one + j) % 4, (self.two + k) % 4

    def move(self, x, device, slot):
        self.net.copy(x, x, device, self.group, slot)

    def send(self, j):
        x = self.block(*self.at(j, 0))
        self.move(x, self.second[1], self.p[j])
        self.move(x, self.second[3], self.q[j])

    def start(self):
        x = self.block(*self.at(0, 0))
        self.move(x, self.first[1], self.a)
        self.move(x, self.first[3], self.b)
        self.send(0)

    def near_one(self):
        self.net.arrived(self.block(*self.at(3, 0)), self.a)
        self.move(self.half(*self.at(3, 0), 0), self.first[1], self.c)
        self.net.arrived(self.block(*self.at(1, 0)), self.b)
        self.move(self.half(*self.at(1, 0), 1), self.first[3], self.c)

    def far_one(self):
        self.net.arrived(self.block(*self.at(2, 0)), self.c)
        self.send(2)

    def near_two(self, j):
        self.net.arrived(self.block(*self.at(j, 3)), self.p[j])
        self.move(self.half(*self.at(j, 3), 0), self.second[1], self.r[j])
        self.net.arrived(self.block(*self.at(j, 1)), self.q[j])
        self.move(self.half(*self.at(j, 1), 1), self.second[3], self.r[j])

    def far_two(self, j):
        self.net.arrived(self.block(*self.at(j, 2)), self.r[j])


class WideGather:
    def __init__(self, net, buf, y, z, c, n):
        self.net, self.buf, self.c = net, buf, c
        self.group, self.slot = net.group(), net.slot()

        def dev(y, z, c):
            return (wide_of(y, z, c), n)

        def block(start):
            return buf.at[pl.ds(start, 16)]

        def half(start, h):
            return buf.at[pl.ds(start, 16), pl.ds(h * 1024, 1024)]

        self.other = dev(y, z, 1 - c)
        self.slots = (slot_a, slot_b)
        self.parts = (
            Gather2(
                net, self.group, y, z, lambda i: dev(i, z, c), lambda i: dev(y, i, c),
                lambda i, k: block(slot_a(c, k, i)), lambda i, k, h: half(slot_a(c, k, i), h),
            ),
            Gather2(
                net, self.group, z, y, lambda i: dev(y, i, c), lambda i: dev(i, z, c),
                lambda i, k: block(slot_b(c, k, i)), lambda i, k, h: half(slot_b(c, k, i), h),
            ),
        )

    def cross(self, k):
        for part, slot in zip(self.parts, self.slots):
            x = self.buf.at[pl.ds(slot(self.c, (part.two + k) % 4, 0), 64)]
            self.net.copy(x, x, self.other, self.group, self.slot)

    def start(self):
        for x in self.parts:
            x.start()

    def near_one(self):
        for x in self.parts:
            x.near_one()
        for x in self.parts:
            x.send(3)
        for x in self.parts:
            x.send(1)

    def far_one(self):
        for x in self.parts:
            x.far_one()
        self.cross(0)

    def near_two(self, j):
        for x in self.parts:
            x.near_two(j)

    def cross_near(self):
        self.cross(3)
        self.cross(1)

    def far_two(self, j):
        for x in self.parts:
            x.far_two(j)
            b = x.block(*x.at(j, 2))
            self.net.copy(b, b, self.other, self.group, self.slot)

    def finish(self):
        self.net.arrived(self.buf.at[pl.ds(0, 512)], self.slot)

    def drain(self):
        self.net.sent(self.buf.at[pl.ds(0, 992)], self.group)


class Scatter:
    def __init__(self, net, group, me, device, part, passed, rh, got, rl, rr):
        self.net, self.group, self.part = net, group, part
        self.passed, self.rh, self.got, self.rl, self.rr = passed, rh, got, rl, rr
        self.me, self.right, self.left = me, (me + 1) % 4, (me + 3) % 4
        self.to_right, self.to_left = device(self.right), device(self.left)
        self.s, self.a = net.slot(), net.slot()

    def move(self, x, to, device, slot):
        self.net.copy(x, to, device, self.group, slot)

    def start(self):
        self.start_far()
        self.start_right()
        self.start_left()

    def start_far(self):
        far = (self.me + 2) % 4
        self.move(self.part(far, 0), self.rh[0], self.to_right, self.s)
        self.move(self.part(far, 1), self.rh[1], self.to_left, self.s)

    def start_right(self):
        self.move(self.part(self.right, 1), self.rl(1), self.to_right, self.a)

    def start_left(self):
        self.move(self.part(self.left, 0), self.rr(0), self.to_left, self.a)

    def step(self):
        self.net.arrived(self.passed, self.s)
        p = self.part(self.right, 0)
        p[...] = (p[...].astype(F32) + self.rh[0][...].astype(F32)).astype(BF16)
        self.move(p, self.rl(0), self.to_right, self.a)
        p = self.part(self.left, 1)
        p[...] = (p[...].astype(F32) + self.rh[1][...].astype(F32)).astype(BF16)
        self.move(p, self.rr(1), self.to_left, self.a)

    def finish(self):
        self.net.arrived(self.got, self.a)

    def half(self, h):
        return self.part(self.me, h)[...].astype(F32) + (self.rl(h)[...].astype(F32) + self.rr(h)[...].astype(F32))


class WideScatter:
    def __init__(self, net, tile, out, got, acc, r1, r2, y, z, c, n):
        self.net, self.tile, self.out, self.got, self.acc, self.c = net, tile, out, got, acc, c
        self.group, self.slots = net.group(), (net.slot(), net.slot())

        def dev(y, z, c):
            return (wide_of(y, z, c), n)

        self.other = dev(y, z, 1 - c)

        def cols(ref, start, h):
            return ref.at[pl.ds(aligned(start, 16), 16), pl.ds(h * 1024, 1024)]

        def ring(me, device, part, ref, base):
            return Scatter(
                net, self.group, me, device, part,
                ref.at[pl.ds(base, 16)], (cols(ref, base, 0), cols(ref, base, 1)),
                ref.at[pl.ds(base + 16, 32)], lambda h: cols(ref, base + 16, h), lambda h: cols(ref, base + 32, h),
            )

        def first(base, one, two, device, k):
            return {
                j: ring(two, device, lambda i, h, j=j: cols(acc, base + i * 64 + (one + j) % 4 * 16, h), r1.at[k], j * 48)
                for j in (2, 1, 3, 0)
            }

        def second(base, one, two, device, k):
            return ring(one, device, lambda i, h: cols(acc, base + two * 64 + i * 16, h), r2, k * 48)

        def along_y(i):
            return dev(i, z, c)

        def along_z(i):
            return dev(y, i, c)

        self.one = (first(0, y, z, along_z, 0), first(256, z, y, along_y, 1))
        self.two = (second(0, y, z, along_y, 0), second(256, z, y, along_z, 1))

    def exchange(self):
        for p in range(2):
            mine = pl.ds(p * 256, 256)
            for i in range(4):
                cs = slice(i * COLS, (i + 1) * COLS)
                self.out[mine, cs] = self.tile(aligned(p * 512 + (1 - self.c) * 256, 256), cs).astype(BF16)
            self.net.copy(self.out.at[mine], self.got.at[mine], self.other, self.group, self.slots[p])

    def start(self):
        for p in range(2):
            mine = pl.ds(p * 256, 256)
            self.net.arrived(self.got.at[mine], self.slots[p])
            for i in range(4):
                cs = slice(i * COLS, (i + 1) * COLS)
                term = self.tile(aligned(p * 512 + self.c * 256, 256), cs)
                self.acc[mine, cs] = (term + self.got[mine, cs].astype(F32)).astype(BF16)
            for j in (2, 1, 3, 0):
                self.one[p][j].start()

    def step(self, j):
        for x in self.one:
            x[j].step()

    def hand_on(self, j):
        for x, t in zip(self.one, self.two):
            r = x[j]
            r.finish()
            for h in range(2):
                r.part(r.me, h)[...] = r.half(h).astype(BF16)
            if j == 2:
                t.start_far()
            if j == 1:
                t.start_right()
            if j == 3:
                t.start_left()

    def second_step(self):
        for r in self.two:
            r.step()

    def finish(self):
        for r in self.two:
            r.finish()

    def result(self, i, cs):
        return self.two[i].half(cs)

    def drain(self, ref):
        self.net.sent(ref.at[pl.ds(0, 992)], self.group)


def wide_peers(y, z, c):
    for d in range(1, 32):
        yield wide_of((y + d // 8) % 4, (z + d // 2 % 4) % 4, (c + d % 2) % 2)


def greet(y, z, c, n):
    peers = [(wide_of((y + d) % 4, z, c), n) for d in (1, 3)]
    peers += [(wide_of(y, (z + d) % 4, c), n) for d in (1, 3)]
    peers += [(wide_of(y, z, 1 - c), n)]
    peers += [(wide_of(y, z, c), (n + d) % 4) for d in (1, 3, 2)]
    barrier = pltpu.get_barrier_semaphore()
    for p in peers:
        pl.semaphore_signal(barrier, inc=1, device_id=p, device_id_type=MESH)
    pl.semaphore_wait(barrier, len(peers))


def repeat(count, step, body):
    def turn(i, _):
        for j in range(step):
            body(i * step + j)
        return 0

    lax.fori_loop(0, count // step, turn, 0)


def nt(a, b):
    return lax.dot_general(a, b, (((1,), (1,)), ((), ())), preferred_element_type=F32)


GELU_A = float(np.sqrt(2.0 / np.pi))
GELU_B = 0.044715


def dot(a, b):
    return jnp.dot(a, b, preferred_element_type=F32)


def lanes(shape):
    return lax.broadcasted_iota(jnp.int32, shape, len(shape) - 1)


def swap(x):
    return jnp.where(lanes(x.shape) < ROT // 2, pltpu.roll(x, 128 - ROT // 2, 1), pltpu.roll(x, ROT // 2, 1))


def block_kernel(
    dealing, lengths, tok, cot, wq, wk, wv, wu, wo, wd, v_gain, v_bias, b_q, b_k, b_v, b_o, b_u, b_d, cos_all, sin_all,
    res, ig, grad_l, grad_u, grad_f, small, norm,
    ln, g, w, wm, wmo, xs, gbs, xhat, cosine, sine, pre, slope, hb, dpre, kv, kk, xq, xd, od, dkvt, dkv, dkvp,
    rdkv, sum_f, sum_u, sum_l, r_f, r_u, r_l, out_1, got_1, acc_1, r1_1, r2_1, out_2, got_2, acc_2, r1_2, r2_2,
    trans, hidden, cmask, bsend, bfin, csend, cfin, ssend, srecv, brecv, wrecv, bias, index, there, kpos, send, recv, local,
):
    y, z, c, n = coords()
    net = Net(send, recv, (wide_of(y, z, 1 - c), n))
    my_cols = pl.ds(aligned(n * COLS, COLS), COLS)
    me = wide_of(y, z, c)
    own_a, own_b = slot_a(c, z, y), slot_b(c, y, z)

    def to(m):
        return (me, m)

    def w_cols(i):
        return pl.ds(aligned(i * COLS, COLS), COLS)

    def share(i):
        return pl.ds(aligned(i * PART, PART), PART)

    tables = [
        pltpu.make_async_copy(cos_all.at[n], cosine, local.at[0]),
        pltpu.make_async_copy(sin_all.at[n], sine, local.at[1]),
    ]
    for t in tables:
        t.start()
    w[256:320, my_cols] = wk[...]
    w[320:384, my_cols] = wv[...]
    w[384:448, my_cols] = wq[...]
    w[0:256, my_cols] = wu[...].T
    wm[0:256, my_cols] = wd[...]
    wm[256:320, my_cols] = wo[...]
    for i in range(4):
        gbs[n, i : i + 1, :] = v_gain[:, i * 128 : i * 128 + 128]
        gbs[n, 4 + i : 5 + i, :] = v_bias[:, i * 128 : i * 128 + 128]
    xs[:, my_cols] = tok[share(n), :]
    row = lax.broadcasted_iota(jnp.int32, (BLOCK, COLS), 0)
    block = dealing[me]
    valid = block % (MAXLEN // BLOCK) * BLOCK + row < jnp.where(block < MAXLEN // BLOCK, lengths[0], lengths[1])
    cmask[...] = jnp.where(valid, cot[...], jnp.zeros_like(cot))
    mine = cmask[share(n), :]
    g[pl.ds(own_a, 16), my_cols] = mine[0:16]
    g[pl.ds(own_b, 16), my_cols] = mine[16:32]
    greet(y, z, c, n)

    rings, turns = net.group(), net.group()
    tokens_in, gains_in, cot_in = net.slot(), net.slot(), net.slot()
    gains_out = net.group()
    for j in (1, 3, 2):
        m = (n + j) % 4
        net.copy(tok.at[share(m)], xs.at[:, my_cols], to(m), turns, tokens_in)
        net.copy(gbs.at[n], gbs.at[n], to(m), gains_out, gains_in)

    def x_ring(ref, start, count):
        half = count // 2
        return Ring(
            net, rings, n, to,
            lambda i: ref.at[pl.ds(start, count), w_cols(i)],
            lambda i, h: ref.at[pl.ds(start + h * half, half), w_cols(i)],
        )

    a_ring = x_ring(w, 256, 192)
    u_ring = x_ring(w, 0, 256)
    d_ring = x_ring(wm, 0, 256)
    o_ring = x_ring(wm, 256, 64)
    kv_ring = [
        Ring(
            net, rings, n, to,
            lambda i, s=s: kv.at[i, pl.ds(s * 512, 512)],
            lambda i, h, s=s: kv.at[i, pl.ds(s * 512 + h * 256, 256)],
        )
        for s in range(2)
    ]
    a_ring.start()
    for j in (1, 3, 2):
        m = (n + j) % 4
        for p, start in enumerate((own_a, own_b)):
            x = cmask.at[pl.ds(aligned(m * PART + p * 16, 16), 16)]
            net.copy(x, g.at[pl.ds(start, 16), my_cols], to(m), turns, cot_in)
    u_ring.start()
    o_ring.start()

    at = lanes((8, 128))
    part = lax.broadcasted_iota(jnp.int32, (8, 128), 0)
    found = jnp.zeros((8, 128), jnp.int32)
    for b in range(NBLK):
        sy, sz, sc = b // 8, b // 2 % 4, b % 2
        found = jnp.where((part < 2) & (at == dealing[b]), jnp.where(part == 0, (sc * 4 + sz) * 4 + sy, 32 + (sc * 4 + sy) * 4 + sz), found)
        found = jnp.where((part == 2) & (at == (sc * 4 + sz) * 4 + sy), 2 * dealing[b], found)
        found = jnp.where((part == 2) & (at == 32 + (sc * 4 + sy) * 4 + sz), 2 * dealing[b] + 1, found)
    index[...] = found
    to_scalars = pltpu.make_async_copy(index, there, local.at[2])
    to_scalars.start()
    half = ROT // 2
    bias[:, 0:128] = b_u[0:1, :].astype(F32)
    bias[:, 128:256] = b_u[1:2, :].astype(F32)
    bias[:, 256:320] = b_k[...].astype(F32)
    bias[:, 320:384] = b_v[...].astype(F32)
    bias[:, 384:448] = b_q[...].astype(F32)
    bias[:, 448:464] = b_q[:, half:ROT].astype(F32)
    bias[:, 464:480] = b_q[:, 0:half].astype(F32)
    bias[:, 480:496] = b_k[:, half:ROT].astype(F32)
    bias[:, 496:512] = b_k[:, 0:half].astype(F32)
    for s in range(2):
        at = lanes((8, MAXLEN))
        kpos[s] = jnp.where(at < lengths[s], at, 1 << 20)
    wmo[0:64, :] = jnp.zeros((64, D), BF16)

    net.arrived(dpre.at[pl.ds(0, 96)], tokens_in)
    x = xs[...].astype(F32)
    mean = jnp.sum(x, 1, keepdims=True) / D
    var = jnp.sum(x * x, 1, keepdims=True) / D - mean * mean
    inv = lax.rsqrt(var + EPS)
    xhat[...] = (x - mean) * inv
    net.arrived(srecv.at[pl.ds(0, 3)], gains_in)
    for i in range(16):
        cs = slice(i * 128, (i + 1) * 128)
        low = (xhat[:, cs] * gbs[i // 4, i % 4 : i % 4 + 1, :] + gbs[i // 4, i % 4 + 4 : i % 4 + 5, :]).astype(BF16)
        ln[pl.ds(own_a, 16), cs] = low[0:16]
        ln[pl.ds(own_b, 16), cs] = low[16:32]

    lg = WideGather(net, ln, y, z, c, n)
    gg = WideGather(net, g, y, z, c, n)
    lg.start()
    for t in tables:
        t.wait()
    to_scalars.wait()
    lg.near_one()
    a_ring.forward()
    lg.near_two(0)
    net.arrived(dpre.at[pl.ds(0, 96)], cot_in)
    lg.far_one()
    gg.start()
    lg.near_two(3)
    u_ring.forward()
    lg.near_two(1)
    o_ring.forward()
    lg.near_two(2)
    lg.cross_near()
    gg.near_one()
    for j in (0, 3, 1, 2):
        lg.far_two(j)
    d_ring.start()
    a_ring.finish()
    gg.near_two(0)
    gg.far_one()

    w[448:640, :] = w[256:448, :]
    w[640:656, :] = w[400:416, :]
    w[656:672, :] = w[384:400, :]
    w[672:688, :] = w[272:288, :]
    w[688:704, :] = w[256:272, :]

    lg.finish()

    def project(i, _):
        r = pl.ds(aligned(i * 512, 512), 512)
        pre[pl.ds(i * 32, 32)] = (nt(ln[r, :], w[448:704, :]) + bias[:, 256:512]).reshape(32, 16, 256)
        return 0

    lax.fori_loop(0, 2, project, 0)

    def arrange(i):
        both = pre[there[i % 2, i // 2]]
        r = pl.ds(aligned(i * 16, 16), 16)
        tab = pl.ds(aligned((i % 32) * 16, 16), 16)
        a, b = both[:, 0:128], both[:, 128:256]
        cs, sn = cosine[tab, :], sine[tab, :]
        kv[n, r, :] = (a * cs + pltpu.roll(b, 32, 1) * sn).astype(BF16)
        q = (b * cs + pltpu.roll(b, 64, 1) * sn) * (HEAD_DIM**-0.5)
        xq[r, :] = jnp.where(lanes((16, 128)) < HEAD_DIM, q, 0.0).astype(BF16)

    repeat(32, 8, arrange)
    kv_ring[0].start()
    repeat(32, 8, lambda i: arrange(i + 32))
    kv_ring[1].start()
    gg.near_two(3)
    gg.near_two(1)
    gg.near_two(2)
    gg.cross_near()
    u_ring.finish()

    def units(i, _):
        r = pl.ds(aligned(i * 512, 512), 512)
        v = nt(ln[r, :], w[0:256, :]) + bias[:, 0:256]
        t = jnp.tanh(GELU_A * (v + GELU_B * (v * v * v)))
        hb[r, :] = (0.5 * v * (1.0 + t)).astype(BF16)
        slope[r, :] = 0.5 * (1.0 + t) + 0.5 * v * (1.0 - t * t) * (GELU_A * (1.0 + 3.0 * GELU_B * (v * v)))
        return 0

    lax.fori_loop(0, 2, units, 0)
    hidden[0:256, :] = hb[...].T
    hidden[256:288, :] = jnp.ones((32, ROWS), BF16)
    kv_ring[0].forward()
    for j in (0, 3, 1, 2):
        gg.far_two(j)
    o_ring.finish()
    wmo[64:128, :] = wm[256:320, :]
    gg.finish()

    def grad_o(i, _):
        r = pl.ds(aligned(i * 512, 512), 512)
        pre[pl.ds(i * 32, 32), :, 0:128] = nt(g[r, :], wmo[...]).reshape(32, 16, 128)
        return 0

    lax.fori_loop(0, 2, grad_o, 0)

    def arrange_do(i):
        xd[pl.ds(aligned(i * 16, 16), 16), :] = pre[there[i % 2, i // 2], :, 0:128].astype(BF16)

    repeat(64, 8, arrange_do)
    kv_ring[1].forward()

    def scatter_cols(buf, count, r):
        half = count // 2
        return Scatter(
            net, net.group(), n, to,
            lambda i, h: buf.at[pl.ds(h * half, half), w_cols(i)],
            r.at[0], (r.at[0, pl.ds(0, half)], r.at[0, pl.ds(half, half)]),
            r.at[pl.ds(1, 2)], lambda h: r.at[1, pl.ds(h * half, half)], lambda h: r.at[2, pl.ds(h * half, half)],
        )

    f_sum = scatter_cols(sum_f, 288, r_f)
    u_sum = scatter_cols(sum_u, 256, r_u)
    l_sum = scatter_cols(sum_l, 256, r_l)

    def gather_keys(i):
        for m in range(4):
            kk[pl.ds(aligned(i * BLOCK + m * PART, PART), PART), :] = kv[m, share(i), :]

    def attend(s, t):
        keys = 512 * (t + 1)
        r = pl.ds(s * 512 + t * 128, 128)
        x = jnp.concatenate([xq[r, :], xd[r, :]], 0)
        near = kk[pl.ds(s * MAXLEN, keys), :]
        both = nt(x, near)
        i = lax.broadcasted_iota(jnp.int32, (128, 1), 0)
        qpos = (4 * t + i // PART) * BLOCK + n * PART + i % PART
        scores = jnp.where(kpos[s, 0:1, 0:keys] <= qpos, both[0:128], -1e30)
        e = jnp.exp(scores - jnp.max(scores, 1, keepdims=True))
        p = e * (1.0 / jnp.sum(e, 1, keepdims=True))
        dp = both[128:256]
        ds = p * (dp - jnp.sum(p * dp, 1, keepdims=True))
        yy = jnp.concatenate([ds.astype(BF16), p.astype(BF16)], 0)
        back = dot(yy, near)
        back = jnp.where(lanes((128, 128)) < HEAD_DIM, back[0:128] * (HEAD_DIM**-0.5), back[128:256])
        od[pl.ds(s * 32 + t * 8, 8)] = back.reshape(8, 16, 128)
        grads = dot(x.T, yy)
        if t == 3:
            dkvt[s, :, 0:keys] = grads
        else:
            dkvt[s, :, 0:keys] += grads

    keys_out = net.group()

    def key_sum(s):
        def rows(start, count):
            return pl.ds(s * 512 + start, count)

        return Scatter(
            net, keys_out, n, to,
            lambda i, h: dkv.at[i, rows(h * 256, 256)],
            rdkv.at[0, rows(0, 512)], (rdkv.at[0, rows(0, 256)], rdkv.at[0, rows(256, 256)]),
            rdkv.at[pl.ds(1, 2), rows(0, 512)],
            lambda h: rdkv.at[1, rows(h * 256, 256)],
            lambda h: rdkv.at[2, rows(h * 256, 256)],
        )

    def weight_f(i, _):
        cs = pl.ds(aligned(i * COLS, COLS), COLS)
        sum_f[:, cs] = dot(hidden[...], g[:, cs]).astype(BF16)
        return 0

    kv_sum = [key_sum(0), key_sum(1)]
    for s in range(2):
        kv_ring[s].finish()
        repeat(16, 4, lambda i, s=s: gather_keys(i + 16 * s))
        for t in (3, 2, 1, 0):
            attend(s, t)
            if (s, t) == (1, 2):
                kv_sum[0].step()
            if (s, t) == (0, 2):
                d_ring.forward()

        def turn_keys(i, s=s):
            t = dkvt[s, :, pl.ds(aligned(i * BLOCK, BLOCK), BLOCK)].T.astype(BF16)
            for m in range(4):
                dkv[m, pl.ds(aligned(s * 512 + i * PART, PART), PART), :] = t[m * PART : (m + 1) * PART]

        repeat(16, 4, turn_keys)
        kv_sum[s].start()
    d_ring.finish()

    def grad_units(i, _):
        r = pl.ds(aligned(i * 512, 512), 512)
        dpre[r, 0:256] = (nt(g[r, :], wm[0:256, :]) * slope[r, :]).astype(BF16)
        return 0

    def unrope(i):
        tab = pl.ds(aligned((i % 32) * 16, 16), 16)
        x = od[i]
        od[i] = x * cosine[tab, :] - swap(x) * sine[tab, :]

    repeat(64, 8, unrope)

    def place(i):
        dpre[pl.ds(aligned(i * 16, 16), 16), 384:512] = od[there[2, i]].astype(BF16)

    repeat(64, 8, place)

    def dln_tile(start, cs):
        r = pl.ds(start, 256)
        return dot(dpre[r, 0:448], w[0:448, cs])

    def branch_tile(start, cs):
        r = pl.ds(start, 256)
        return dot(hb[r, :], wm[0:256, cs]) + dot(dpre[r, 384:512], wmo[:, cs])

    branch = WideScatter(net, branch_tile, out_1, got_1, acc_1, r1_1, r2_1, y, z, c, n)
    dln = WideScatter(net, dln_tile, out_2, got_2, acc_2, r1_2, r2_2, y, z, c, n)
    branch.exchange()
    kv_sum[1].step()
    lax.fori_loop(0, 2, grad_units, 0)

    def unrope_keys(i):
        tab = pl.ds(aligned((i % 32) * 16, 16), 16)
        r = pl.ds(aligned(i * 16, 16), 16)
        x = dkv[n, r, :].astype(F32) + (rdkv[1, r, :].astype(F32) + rdkv[2, r, :].astype(F32))
        dkvp[i] = x * cosine[tab, :] - swap(x) * sine[tab, :]

    kv_sum[0].finish()
    repeat(32, 8, unrope_keys)
    branch.start()
    kv_sum[1].finish()
    repeat(32, 8, lambda i: unrope_keys(i + 32))

    def place_keys(i):
        dpre[pl.ds(aligned(i * 16, 16), 16), 256:384] = dkvp[there[2, i]].astype(BF16)

    repeat(64, 8, place_keys)
    dln.exchange()
    lax.fori_loop(0, 4, weight_f, 0)
    f_sum.start()
    branch.step(2)
    branch.step(1)
    dln.start()
    branch.step(3)
    branch.step(0)
    trans[...] = dpre[:, 0:256].T

    def weight_u(i, _):
        cs = pl.ds(aligned(i * COLS, COLS), COLS)
        sum_u[:, cs] = dot(trans[...], ln[:, cs]).astype(BF16)
        return 0

    lax.fori_loop(0, 4, weight_u, 0)
    u_sum.start()
    dln.step(2)
    dln.step(1)
    branch.hand_on(2)
    branch.hand_on(1)
    dln.step(3)
    dln.step(0)
    f_sum.step()
    trans[...] = dpre[:, 256:512].T

    def weight_l(i, _):
        cs = pl.ds(aligned(i * COLS, COLS), COLS)
        sum_l[0:192, cs] = dot(trans[0:192, :], ln[:, cs]).astype(BF16)
        sum_l[192:256, cs] = dot(trans[192:256, :], g[:, cs]).astype(BF16)
        return 0

    lax.fori_loop(0, 4, weight_l, 0)
    l_sum.start()
    dln.hand_on(2)
    dln.hand_on(1)
    dln.hand_on(3)
    dln.second_step()
    dln.hand_on(0)
    branch.hand_on(3)
    branch.second_step()
    branch.hand_on(0)
    u_sum.step()
    sums = jnp.sum(dpre[...].astype(F32), 0, keepdims=True)
    for i in range(4):
        brecv[n, i : i + 1, :] = sums[:, i * 128 : i * 128 + 128]
    small_out, small_in, branch_out, branch_in = net.group(), net.slot(), net.group(), net.slot()
    for j in (1, 3, 2):
        net.copy(brecv.at[n], brecv.at[n], to((n + j) % 4), small_out, small_in)
    dln.finish()

    for i in range(2):
        for h in range(2):
            csend[i * 16 : (i + 1) * 16, h * 1024 : (h + 1) * 1024] = dln.result(i, h)
    grad = csend[...]
    sums = (jnp.sum(grad * xhat[...], 0, keepdims=True), jnp.sum(grad, 0, keepdims=True))
    for m in range(4):
        for k in range(2):
            for i in range(4):
                ssend[m, 4 * k + i : 4 * k + i + 1, :] = sums[k][:, m * COLS + i * 128 : m * COLS + i * 128 + 128]
    srecv[n] = ssend[n]
    norm_out, norm_in, final_out, final_in, all_out, all_in = net.group(), net.slot(), net.group(), net.slot(), net.group(), net.slot()
    for j in (1, 3, 2):
        m = (n + j) % 4
        net.copy(ssend.at[m], srecv.at[n], to(m), norm_out, norm_in)
    for i in range(16):
        cs = slice(i * 128, (i + 1) * 128)
        csend[:, cs] = csend[:, cs] * gbs[i // 4, i % 4 : i % 4 + 1, :]
    grad = csend[...]
    first = jnp.sum(grad, 1, keepdims=True) / D
    second = jnp.sum(grad * xhat[...], 1, keepdims=True) / D
    x = xs[...].astype(F32)
    mean = jnp.sum(x, 1, keepdims=True) / D
    var = jnp.sum(x * x, 1, keepdims=True) / D - mean * mean
    csend[...] = lax.rsqrt(var + EPS) * (grad - first - xhat[...] * second)
    cfin[share(n), :] = csend[:, my_cols]
    for j in (1, 3, 2):
        m = (n + j) % 4
        net.copy(csend.at[:, w_cols(m)], cfin.at[share(n)], to(m), final_out, final_in)
    net.arrived(srecv.at[pl.ds(0, 3)], norm_in)
    wrecv[me] = (srecv[0] + srecv[1]) + (srecv[2] + srecv[3])
    for p in wide_peers(y, z, c):
        net.copy(wrecv.at[me], wrecv.at[me], (p, n), all_out, all_in)
    l_sum.step()
    branch.finish()
    for i in range(2):
        for h in range(2):
            bsend[i * 16 : (i + 1) * 16, h * 1024 : (h + 1) * 1024] = branch.result(i, h).astype(BF16)
    bfin[share(n), :] = bsend[:, my_cols]
    for j in (1, 3, 2):
        m = (n + j) % 4
        net.copy(bsend.at[:, w_cols(m)], bfin.at[share(n)], to(m), branch_out, branch_in)
    f_sum.finish()
    for h in range(2):
        grad_f[h * 144 : (h + 1) * 144, :] = f_sum.half(h)
    u_sum.finish()
    for h in range(2):
        grad_u[h * 128 : (h + 1) * 128, :] = u_sum.half(h)
    l_sum.finish()
    for h in range(2):
        grad_l[h * 128 : (h + 1) * 128, :] = l_sum.half(h)
    net.arrived(dpre.at[pl.ds(0, 96)], branch_in)
    net.arrived(srecv.at[pl.ds(0, 3)], small_in)
    block = dealing[me]
    valid = block % (MAXLEN // BLOCK) * BLOCK + row < jnp.where(block < MAXLEN // BLOCK, lengths[0], lengths[1])
    valid = valid[:, 0:128]
    for i in range(4):
        cs = slice(i * 128, i * 128 + 128)
        base = bfin[:, cs].astype(F32) + (b_o[i : i + 1, :].astype(F32) + b_d[i : i + 1, :].astype(F32))
        res[:, cs] = (tok[:, cs].astype(F32) + jnp.where(valid, base, 0.0)).astype(BF16)
    small[...] = (brecv[0] + brecv[1]) + (brecv[2] + brecv[3])
    net.arrived(cfin.at[pl.ds(0, 96)], final_in)
    ig[...] = cot[...].astype(F32) + cfin[...]
    net.arrived(wrecv.at[pl.ds(0, 31)], all_in)
    norm[...] = jnp.sum(wrecv[...], 0)

    lg.drain()
    gg.drain()
    branch.drain(ln)
    dln.drain(ln)
    net.sent(ln.at[pl.ds(0, 768)], rings)
    net.sent(ln.at[pl.ds(0, 192)], keys_out)
    net.sent(dpre.at[pl.ds(0, 864)], f_sum.group)
    net.sent(dpre.at[pl.ds(0, 768)], u_sum.group)
    net.sent(dpre.at[pl.ds(0, 768)], l_sum.group)
    net.sent(dpre.at[pl.ds(0, 192)], turns)
    net.sent(srecv.at[pl.ds(0, 3)], gains_out)
    net.sent(srecv.at[pl.ds(0, 3)], small_out)
    net.sent(dpre.at[pl.ds(0, 96)], branch_out)
    net.sent(srecv.at[pl.ds(0, 3)], norm_out)
    net.sent(cfin.at[pl.ds(0, 96)], final_out)
    net.sent(wrecv.at[pl.ds(0, 31)], all_out)
    assert (net.groups, net.slots) == (SENDS, ARRIVALS), (net.groups, net.slots)


def call_block(*args):
    vmem, anywhere = pl.BlockSpec(memory_space=pltpu.VMEM), pl.BlockSpec(memory_space=pl.ANY)
    shape = jax.ShapeDtypeStruct

    def buf(dtype, *size):
        return pltpu.VMEM(size, dtype)

    wide = [buf(BF16, 512, D), buf(BF16, 512, D), buf(BF16, 512, D), buf(BF16, 2, 192, D), buf(BF16, 96, D)]
    return pl.pallas_call(
        block_kernel,
        out_shape=(
            shape((BLOCK, COLS), BF16),
            shape((BLOCK, COLS), F32),
            shape((256, COLS), F32),
            shape((256, COLS), F32),
            shape((288, COLS), F32),
            shape((8, 128), F32),
            shape((8, 128), F32),
        ),
        in_specs=[pl.BlockSpec(memory_space=pltpu.SMEM)] * 2 + [vmem] * 16 + [anywhere] * 2,
        out_specs=(vmem,) * 7,
        scratch_shapes=[
            buf(BF16, ROWS, D),
            buf(BF16, ROWS, D),
            buf(BF16, 704, D),
            buf(BF16, 320, D),
            buf(BF16, 128, D),
            buf(BF16, PART, D),
            buf(F32, 4, 8, 128),
            buf(F32, PART, D),
            buf(F32, 512, 128),
            buf(F32, 512, 128),
            buf(F32, 64, 16, 256),
            buf(F32, ROWS, UNITS),
            buf(BF16, ROWS, UNITS),
            buf(BF16, ROWS, 512),
            buf(BF16, 4, ROWS, 128),
            buf(BF16, 2 * MAXLEN, 128),
            buf(BF16, ROWS, 128),
            buf(BF16, ROWS, 128),
            buf(F32, 64, 16, 128),
            buf(F32, 2, 128, MAXLEN),
            buf(BF16, 4, ROWS, 128),
            buf(F32, 64, 16, 128),
            buf(BF16, 3, ROWS, 128),
            buf(BF16, 288, D),
            buf(BF16, 256, D),
            buf(BF16, 256, D),
            buf(BF16, 3, 288, COLS),
            buf(BF16, 3, 256, COLS),
            buf(BF16, 3, 256, COLS),
            *wide,
            *wide,
            buf(BF16, 256, ROWS),
            buf(BF16, 288, ROWS),
            buf(BF16, BLOCK, COLS),
            buf(BF16, PART, D),
            buf(BF16, BLOCK, COLS),
            buf(F32, PART, D),
            buf(F32, BLOCK, COLS),
            buf(F32, 4, 8, 128),
            buf(F32, 4, 8, 128),
            buf(F32, 4, 8, 128),
            buf(F32, 32, 8, 128),
            buf(F32, 1, COLS),
            buf(jnp.int32, 8, 128),
            pltpu.SMEM((8, 128), jnp.int32),
            buf(jnp.int32, 2, 8, MAXLEN),
            pltpu.SemaphoreType.DMA((SENDS,)),
            pltpu.SemaphoreType.DMA((ARRIVALS,)),
            pltpu.SemaphoreType.DMA((3,)),
        ],
        compiler_params=pltpu.CompilerParams(collective_id=0, has_side_effects=True, vmem_limit_bytes=63 * 2**20),
    )(*args)


def split_kernel(
    res, ig, grad_l, grad_u, grad_f, small, norm,
    res_o, ig_o, gain_o, bias_o, q_o, bq_o, k_o, bk_o, v_o, bv_o, o_o, bo_o, u_o, bu_o, f_o, bf_o,
):
    res_o[...] = res[...]
    ig_o[...] = ig[...]
    k_o[...] = grad_l[0:64, :]
    v_o[...] = grad_l[64:128, :]
    q_o[...] = grad_l[128:192, :]
    o_o[...] = grad_l[192:256, :]
    u_o[...] = grad_u[...].T
    f_o[...] = grad_f[0:256, :]
    for i in range(4):
        gain_o[:, i * 128 : i * 128 + 128] = norm[i : i + 1, :]
        bias_o[:, i * 128 : i * 128 + 128] = norm[4 + i : 5 + i, :]
    bu_o[:, 0:128] = small[0:1, :]
    bu_o[:, 128:256] = small[1:2, :]
    bk_o[...] = small[2:3, 0:64]
    bv_o[...] = small[2:3, 64:128]
    bq_o[...] = small[3:4, 0:64]
    bo_o[...] = grad_f[256:257, :]
    bf_o[...] = grad_f[256:257, :]


def call_split(*args):
    vmem = pl.BlockSpec(memory_space=pltpu.VMEM)
    head, vector = (64, COLS), (1, COLS)
    sizes = [
        (BLOCK, COLS), vector, vector, head, (1, 64), head, (1, 64), head, (1, 64), head, vector,
        (COLS, UNITS), (1, UNITS), (UNITS, COLS), vector,
    ]
    return pl.pallas_call(
        split_kernel,
        out_shape=(jax.ShapeDtypeStruct((BLOCK, COLS), BF16), *(jax.ShapeDtypeStruct(s, F32) for s in sizes)),
        in_specs=[vmem] * 7,
        out_specs=(vmem,) * 16,
        compiler_params=pltpu.CompilerParams(vmem_limit_bytes=62 * 2**20),
    )(*args)


def on_device(
    tokens, ln_gain, ln_bias, w_query, b_query, w_key, b_key, w_value, b_value, w_out, b_out,
    w_fc1, b_fc1, w_fc2, b_fc2, cotangent, lengths, dealing,
):
    cosine, sine = (
        np.ascontiguousarray(t.reshape(MAXLEN // BLOCK, 4, PART, 128).transpose(1, 0, 2, 3)).reshape(4, -1, 128)
        for t in rope_tables()
    )
    out = call_block(
        dealing, lengths, tokens, cotangent, w_query.T, w_key.T, w_value.T, w_fc1, w_out, w_fc2,
        ln_gain[None], ln_bias[None], b_query[None], b_key[None], b_value[None], b_out.reshape(-1, 128),
        b_fc1.reshape(-1, 128), b_fc2.reshape(-1, 128),
        jnp.asarray(cosine), jnp.asarray(sine),
    )
    out = list(call_split(*out))
    for i in (4, 6, 8):
        out[i] = out[i].T
    for i in (2, 3, 5, 7, 9, 11, 13, 15):
        out[i] = out[i][0]
    return tuple(out)


def solution(mesh):
    rows, col, units = P("wide", "narrow"), P("narrow"), P("wide")
    weight, out = P("narrow", "wide"), P("wide", "narrow")
    placed = (
        rows, col, col, weight, units, weight, units, weight, units, out, col, weight, units, out, col, rows, P(), P(),
    )
    given = (
        rows, rows, col, col, weight, units, weight, units, weight, units, out, col, weight, units, out, col,
    )
    return jax.shard_map(on_device, mesh=mesh, in_specs=placed, out_specs=given, check_vma=False)
```

time: 125 us -> 106 us (0.85)
  Pallas kernels: 121 us -> 106 us
  local copies, waits for them, and re-layouts: 2.59 us -> 0 us
    pallas_call x1, Pallas kernels: 118 us -> 103 us  [call_block(): pl.pallas_call(block_kernel, out_shape=(shape((BLOCK, COLS), BF16), shape...]
    broadcast_in_dim x3 -> x0, local copies, waits for them, and re-layouts: 1.73 us -> none  [the longest x1 0.58 us: on_device(): b_out[None]]
where the time goes in v4:
time: 106 us
  Pallas kernels  106 us (100%)
    pallas_call x1, Pallas kernels, call_block(): pl.pallas_call(block_kernel, out_shape=(shape((BLOCK, COLS), BF16), shape...  103 us
    pallas_call x1, Pallas kernels, call_split(): pl.pallas_call(split_kernel, out_shape=(jax.ShapeDtypeStruct((BLOCK, COLS...  2.97 us

profile of v4, /device:TPU:1, one launch (start us, length us, event | category | flops | bytes accessed | tf_op | source)
XLA Modules:
  0.0 106.3 jit_solution(13644135207944105803)
XLA Ops:
  0.7 102.5 %shard_map.315 = (bf16[128,512]{1,0:T(8,128)(2,1)}, f32[128,512]{1,0:T(8,128)}, f32[256,512]{1,0:T(8,128)}, f32[256,512]{1,0:T(8,128)}, f32[288,512]{1,0:T(8,128)}, /*index=5*/f32[8,128]{1,0:T(8,128)}, f32[8,128]{1,0:T(8,128)}) custom-call(s32[32]{0:T(128)} %dealing.1, s32[2]{0:T(128)} %lengths.1, bf16[128,512]{1,0:T(8,128)(2,1)} %tok.1, ...), custom_call_target="tpu_custom_call" | custom-call | tf_op jit(solution)/shard_map/pallas_call | solution.py:896
  103.2 3.0 %shard_map.316 = (bf16[128,512]{1,0:T(8,128)(2,1)}, f32[128,512]{1,0:T(8,128)}, f32[1,512]{1,0:T(1,128)}, f32[1,512]{1,0:T(1,128)}, f32[64,512]{1,0:T(8,128)}, /...) custom-call(bf16[128,512]{1,0:T(8,128)(2,1)} %get-tuple-element.39.r, ...), custom_call_target="tpu_custom_call" | custom-call | tf_op jit(solution)/shard_map/pallas_call | solution.py:995

commit v5 on v4

--- a/solution.py
+++ b/solution.py
@@ -18,7 +18,7 @@
 COLS = 512
 UNITS = 256
 EPS = 1e-05
-SENDS, ARRIVALS = 16, 142
+SENDS, ARRIVALS = 17, 143
 BF16 = jnp.bfloat16
 F32 = jnp.float32
 
@@ -139,13 +139,14 @@
         x = self.block(*self.at(0, 0))
         self.move(x, self.first[1], self.a)
         self.move(x, self.first[3], self.b)
+        self.move(x, self.first[2], self.c)
         self.send(0)
 
     def near_one(self):
         self.net.arrived(self.block(*self.at(3, 0)), self.a)
-        self.move(self.half(*self.at(3, 0), 0), self.first[1], self.c)
+        self.send(3)
         self.net.arrived(self.block(*self.at(1, 0)), self.b)
-        self.move(self.half(*self.at(1, 0), 1), self.first[3], self.c)
+        self.send(1)
 
     def far_one(self):
         self.net.arrived(self.block(*self.at(2, 0)), self.c)
@@ -200,10 +201,6 @@
     def near_one(self):
         for x in self.parts:
             x.near_one()
-        for x in self.parts:
-            x.send(3)
-        for x in self.parts:
-            x.send(1)
 
     def far_one(self):
         for x in self.parts:
@@ -274,6 +271,26 @@
         return self.part(self.me, h)[...].astype(F32) + (self.rl(h)[...].astype(F32) + self.rr(h)[...].astype(F32))
 
 
+class Direct:
+    def __init__(self, net, group, me, device, part, got, base):
+        self.net, self.group, self.me, self.part = net, group, me, part
+        self.device, self.got, self.base, self.slot = device, got, base, net.slot()
+
+    def send(self, j):
+        i = (self.me + j) % 4
+        x = self.part(i)
+        self.net.copy(x, self.got.at[pl.ds(self.base + 16 * (j - 1), 16)], self.device(i), self.group, self.slot)
+
+    def finish(self):
+        self.net.arrived(self.got.at[pl.ds(self.base, 48)], self.slot)
+
+    def result(self, cs):
+        total = self.part(self.me)[:, cs].astype(F32)
+        for j in range(3):
+            total += self.got[self.base + 16 * j : self.base + 16 * j + 16, cs].astype(F32)
+        return total
+
+
 class WideScatter:
     def __init__(self, net, tile, out, got, acc, r1, r2, y, z, c, n):
         self.net, self.tile, self.out, self.got, self.acc, self.c = net, tile, out, got, acc, c
@@ -301,7 +318,10 @@
             }
 
         def second(base, one, two, device, k):
-            return ring(one, device, lambda i, h: cols(acc, base + two * 64 + i * 16, h), r2, k * 48)
+            return Direct(
+                net, self.group, one, device,
+                lambda i: acc.at[pl.ds(aligned(base + two * 64 + i * 16, 16), 16)], r2, k * 48,
+            )
 
         def along_y(i):
             return dev(i, z, c)
@@ -329,54 +349,52 @@
                 term = self.tile(aligned(p * 512 + self.c * 256, 256), cs)
                 self.acc[mine, cs] = (term + self.got[mine, cs].astype(F32)).astype(BF16)
             for j in (2, 1, 3, 0):
-                self.one[p][j].start()
+                self.one[p][j].start_far()
+            for j in (2, 1, 3, 0):
+                self.one[p][j].start_right()
+                self.one[p][j].start_left()
 
     def step(self, j):
         for x in self.one:
             x[j].step()
 
-    def hand_on(self, j):
-        for x, t in zip(self.one, self.two):
+    def hand_on(self, j, also=None):
+        for p, (x, t) in enumerate(zip(self.one, self.two)):
             r = x[j]
             r.finish()
             for h in range(2):
-                r.part(r.me, h)[...] = r.half(h).astype(BF16)
-            if j == 2:
-                t.start_far()
-            if j == 1:
-                t.start_right()
-            if j == 3:
-                t.start_left()
-
-    def second_step(self):
-        for r in self.two:
-            r.step()
+                v = r.half(h)
+                r.part(r.me, h)[...] = v.astype(BF16)
+                if also is not None:
+                    also(p, (t.me + j) % 4, slice(h * 1024, (h + 1) * 1024), v)
+            if j:
+                t.send(j)
 
     def finish(self):
         for r in self.two:
             r.finish()
 
     def result(self, i, cs):
-        return self.two[i].half(cs)
+        return self.two[i].result(cs)
 
     def drain(self, ref):
         self.net.sent(ref.at[pl.ds(0, 992)], self.group)
 
 
-def wide_peers(y, z, c):
-    for d in range(1, 32):
-        yield wide_of((y + d // 8) % 4, (z + d // 2 % 4) % 4, (c + d % 2) % 2)
+def other_chips(y, z, c):
+    for d in range(1, 16):
+        yield wide_of((y + d // 4) % 4, (z + d % 4) % 4, c)
 
 
 def greet(y, z, c, n):
-    peers = [(wide_of((y + d) % 4, z, c), n) for d in (1, 3)]
-    peers += [(wide_of(y, (z + d) % 4, c), n) for d in (1, 3)]
+    peers = [(wide_of((y + d) % 4, z, c), n) for d in (1, 3, 2)]
+    peers += [(wide_of(y, (z + d) % 4, c), n) for d in (1, 3, 2)]
     peers += [(wide_of(y, z, 1 - c), n)]
     peers += [(wide_of(y, z, c), (n + d) % 4) for d in (1, 3, 2)]
     barrier = pltpu.get_barrier_semaphore()
     for p in peers:
         pl.semaphore_signal(barrier, inc=1, device_id=p, device_id_type=MESH)
-    pl.semaphore_wait(barrier, len(peers))
+    return lambda: pl.semaphore_wait(barrier, len(peers))
 
 
 def repeat(count, step, body):
@@ -409,11 +427,14 @@
 
 
 def block_kernel(
-    dealing, lengths, tok, cot, wq, wk, wv, wu, wo, wd, v_gain, v_bias, b_q, b_k, b_v, b_o, b_u, b_d, cos_all, sin_all,
-    res, ig, grad_l, grad_u, grad_f, small, norm,
-    ln, g, w, wm, wmo, xs, gbs, xhat, cosine, sine, pre, slope, hb, dpre, kv, kk, xq, xd, od, dkvt, dkv, dkvp,
+    dealing, lengths, i_tok, i_cot, i_wq, i_wk, i_wv, i_wu, i_wo, i_wd,
+    i_gain, i_bias, i_bq, i_bk, i_bv, i_bo, i_bu, i_bd, cos_all, sin_all,
+    o_res, o_ig, o_gain, o_bias, o_q, o_bq, o_k, o_bk, o_v, o_bv, o_o, o_bo, o_u, o_bu, o_f,
+    tok, cot, wu, v_gain, v_bias, b_q, b_k, b_v, b_o, b_u, b_d,
+    res, ig, grad_l, grad_u, grad_f, v_512, v_64, v_256,
+    ln, g, w, wm, wmo, xs, gbs, xhat, cosine, sine, cosine_held, sine_held, slope, hb, dpre, kv, kk, xq, xd, od, dkvt, dkv, dkvp,
     rdkv, sum_f, sum_u, sum_l, r_f, r_u, r_l, out_1, got_1, acc_1, r1_1, r2_1, out_2, got_2, acc_2, r1_2, r2_2,
-    trans, hidden, cmask, bsend, bfin, csend, cfin, ssend, srecv, brecv, wrecv, bias, index, there, kpos, send, recv, local,
+    trans, hidden, cmask, bsend, bfin, csend, clow, cfin, ssend, srecv, brecv, wrecv, nsum, hats, column, bias, index, there, kpos, send, recv, local, inward,
 ):
     y, z, c, n = coords()
     net = Net(send, recv, (wide_of(y, z, 1 - c), n))
@@ -430,18 +451,31 @@
     def share(i):
         return pl.ds(aligned(i * PART, PART), PART)
 
-    tables = [
-        pltpu.make_async_copy(cos_all.at[n], cosine, local.at[0]),
-        pltpu.make_async_copy(sin_all.at[n], sine, local.at[1]),
-    ]
-    for t in tables:
-        t.start()
-    w[256:320, my_cols] = wk[...]
-    w[320:384, my_cols] = wv[...]
-    w[384:448, my_cols] = wq[...]
+    loads = []
+
+    def load(x, to):
+        loads.append(pltpu.make_async_copy(x, to, inward.at[len(loads)]))
+        loads[-1].start()
+
+    load(i_tok, tok)
+    load(i_wk, w.at[pl.ds(256, 64), my_cols])
+    load(i_wv, w.at[pl.ds(320, 64), my_cols])
+    load(i_wq, w.at[pl.ds(384, 64), my_cols])
+    load(i_cot, cot)
+    load(i_wu, wu)
+    load(i_wo, wm.at[pl.ds(256, 64), my_cols])
+    load(i_gain, v_gain)
+    load(i_bias, v_bias)
+    early = len(loads)
+    load(i_wd, wm.at[pl.ds(0, 256), my_cols])
+    for x, at in ((i_bq, b_q), (i_bk, b_k), (i_bv, b_v), (i_bo, b_o), (i_bu, b_u), (i_bd, b_d)):
+        load(x, at)
+    load(cos_all.at[n], cosine)
+    load(sin_all.at[n], sine)
+    all_greeted = greet(y, z, c, n)
+    for x in loads[:early]:
+        x.wait()
     w[0:256, my_cols] = wu[...].T
-    wm[0:256, my_cols] = wd[...]
-    wm[256:320, my_cols] = wo[...]
     for i in range(4):
         gbs[n, i : i + 1, :] = v_gain[:, i * 128 : i * 128 + 128]
         gbs[n, 4 + i : 5 + i, :] = v_bias[:, i * 128 : i * 128 + 128]
@@ -453,7 +487,7 @@
     mine = cmask[share(n), :]
     g[pl.ds(own_a, 16), my_cols] = mine[0:16]
     g[pl.ds(own_b, 16), my_cols] = mine[16:32]
-    greet(y, z, c, n)
+    all_greeted()
 
     rings, turns = net.group(), net.group()
     tokens_in, gains_in, cot_in = net.slot(), net.slot(), net.slot()
@@ -478,8 +512,8 @@
     kv_ring = [
         Ring(
             net, rings, n, to,
-            lambda i, s=s: kv.at[i, pl.ds(s * 512, 512)],
-            lambda i, h, s=s: kv.at[i, pl.ds(s * 512 + h * 256, 256)],
+            lambda i, s=s: kv.at[i, pl.ds(s * 32, 32)],
+            lambda i, h, s=s: kv.at[i, pl.ds(s * 32 + h * 16, 16)],
         )
         for s in range(2)
     ]
@@ -492,6 +526,8 @@
     u_ring.start()
     o_ring.start()
 
+    for x in loads[early:]:
+        x.wait()
     at = lanes((8, 128))
     part = lax.broadcasted_iota(jnp.int32, (8, 128), 0)
     found = jnp.zeros((8, 128), jnp.int32)
@@ -500,8 +536,10 @@
         found = jnp.where((part < 2) & (at == dealing[b]), jnp.where(part == 0, (sc * 4 + sz) * 4 + sy, 32 + (sc * 4 + sy) * 4 + sz), found)
         found = jnp.where((part == 2) & (at == (sc * 4 + sz) * 4 + sy), 2 * dealing[b], found)
         found = jnp.where((part == 2) & (at == 32 + (sc * 4 + sy) * 4 + sz), 2 * dealing[b] + 1, found)
+        found = jnp.where((part == 3) & (at == (sc * 4 + sz) * 4 + sy), 2 * dealing[b] % 32, found)
+        found = jnp.where((part == 3) & (at == 32 + (sc * 4 + sy) * 4 + sz), 2 * dealing[b] % 32 + 1, found)
     index[...] = found
-    to_scalars = pltpu.make_async_copy(index, there, local.at[2])
+    to_scalars = pltpu.make_async_copy(index, there, local.at[0])
     to_scalars.start()
     half = ROT // 2
     bias[:, 0:128] = b_u[0:1, :].astype(F32)
@@ -534,25 +572,29 @@
     lg = WideGather(net, ln, y, z, c, n)
     gg = WideGather(net, g, y, z, c, n)
     lg.start()
-    for t in tables:
-        t.wait()
     to_scalars.wait()
+
+    def hold(i):
+        cosine_held[i] = cosine[there[3, i]]
+        sine_held[i] = sine[there[3, i]]
+
+    repeat(64, 8, hold)
     lg.near_one()
     a_ring.forward()
+    d_ring.start()
+    net.arrived(dpre.at[pl.ds(0, 96)], cot_in)
     lg.near_two(0)
-    net.arrived(dpre.at[pl.ds(0, 96)], cot_in)
     lg.far_one()
     gg.start()
     lg.near_two(3)
-    u_ring.forward()
     lg.near_two(1)
-    o_ring.forward()
     lg.near_two(2)
     lg.cross_near()
     gg.near_one()
+    u_ring.forward()
+    o_ring.forward()
     for j in (0, 3, 1, 2):
         lg.far_two(j)
-    d_ring.start()
     a_ring.finish()
     gg.near_two(0)
     gg.far_one()
@@ -564,28 +606,13 @@
     w[688:704, :] = w[256:272, :]
 
     lg.finish()
-
-    def project(i, _):
-        r = pl.ds(aligned(i * 512, 512), 512)
-        pre[pl.ds(i * 32, 32)] = (nt(ln[r, :], w[448:704, :]) + bias[:, 256:512]).reshape(32, 16, 256)
-        return 0
-
-    lax.fori_loop(0, 2, project, 0)
-
-    def arrange(i):
-        both = pre[there[i % 2, i // 2]]
-        r = pl.ds(aligned(i * 16, 16), 16)
-        tab = pl.ds(aligned((i % 32) * 16, 16), 16)
-        a, b = both[:, 0:128], both[:, 128:256]
-        cs, sn = cosine[tab, :], sine[tab, :]
-        kv[n, r, :] = (a * cs + pltpu.roll(b, 32, 1) * sn).astype(BF16)
-        q = (b * cs + pltpu.roll(b, 64, 1) * sn) * (HEAD_DIM**-0.5)
-        xq[r, :] = jnp.where(lanes((16, 128)) < HEAD_DIM, q, 0.0).astype(BF16)
-
-    repeat(32, 8, arrange)
+    x = (nt(ln[...], w[448:704, :]) + bias[:, 256:512]).reshape(64, 16, 256)
+    a, b = x[:, :, 0:128], x[:, :, 128:256]
+    kv[n] = (a * cosine_held[...] + pltpu.roll(b, 32, 2) * sine_held[...]).astype(BF16)
     kv_ring[0].start()
-    repeat(32, 8, lambda i: arrange(i + 32))
     kv_ring[1].start()
+    x = (b * cosine_held[...] + pltpu.roll(b, 64, 2) * sine_held[...]) * (HEAD_DIM**-0.5)
+    xq[...] = jnp.where(lanes((64, 16, 128)) < HEAD_DIM, x, 0.0).astype(BF16)
     gg.near_two(3)
     gg.near_two(1)
     gg.near_two(2)
@@ -603,26 +630,6 @@
     lax.fori_loop(0, 2, units, 0)
     hidden[0:256, :] = hb[...].T
     hidden[256:288, :] = jnp.ones((32, ROWS), BF16)
-    kv_ring[0].forward()
-    for j in (0, 3, 1, 2):
-        gg.far_two(j)
-    o_ring.finish()
-    wmo[64:128, :] = wm[256:320, :]
-    gg.finish()
-
-    def grad_o(i, _):
-        r = pl.ds(aligned(i * 512, 512), 512)
-        pre[pl.ds(i * 32, 32), :, 0:128] = nt(g[r, :], wmo[...]).reshape(32, 16, 128)
-        return 0
-
-    lax.fori_loop(0, 2, grad_o, 0)
-
-    def arrange_do(i):
-        xd[pl.ds(aligned(i * 16, 16), 16), :] = pre[there[i % 2, i // 2], :, 0:128].astype(BF16)
-
-    repeat(64, 8, arrange_do)
-    kv_ring[1].forward()
-
     def scatter_cols(buf, count, r):
         half = count // 2
         return Scatter(
@@ -636,14 +643,45 @@
     u_sum = scatter_cols(sum_u, 256, r_u)
     l_sum = scatter_cols(sum_l, 256, r_l)
 
+    def weight_f(i, _):
+        cs = pl.ds(aligned(i * 1024, 1024), 1024)
+        sum_f[:, cs] = dot(hidden[...], g[:, cs]).astype(BF16)
+        return 0
+
+    kv_ring[0].forward()
+    d_ring.forward()
+    o_ring.finish()
+    wmo[64:128, :] = wm[256:320, :]
+    for j in (0, 3, 1, 2):
+        gg.far_two(j)
+    kv_ring[1].forward()
+
+    gg.finish()
+    hats_out, hats_in = net.group(), net.slot()
+    hats[y] = xhat[0:16, :]
+    hats[4 + z] = xhat[16:32, :]
+    for d in (1, 3, 2):
+        net.copy(xhat.at[pl.ds(0, 16)], hats.at[y], (wide_of((y + d) % 4, z, c), n), hats_out, hats_in)
+        net.copy(xhat.at[pl.ds(16, 16)], hats.at[4 + z], (wide_of(y, (z + d) % 4, c), n), hats_out, hats_in)
+    lax.fori_loop(0, 2, weight_f, 0)
+    f_sum.start()
+
+    def grad_o(i, _):
+        r = pl.ds(aligned(i * 512, 512), 512)
+        xd[pl.ds(i * 32, 32)] = nt(g[r, :], wmo[...]).astype(BF16).reshape(32, 16, 128)
+        return 0
+
+    lax.fori_loop(0, 2, grad_o, 0)
+
     def gather_keys(i):
         for m in range(4):
-            kk[pl.ds(aligned(i * BLOCK + m * PART, PART), PART), :] = kv[m, share(i), :]
+            for p in range(2):
+                kk[pl.ds(aligned(i * BLOCK + m * PART + p * 16, 16), 16), :] = kv[m, there[p, i]]
 
     def attend(s, t):
         keys = 512 * (t + 1)
-        r = pl.ds(s * 512 + t * 128, 128)
-        x = jnp.concatenate([xq[r, :], xd[r, :]], 0)
+        held = [there[k % 2, s * 16 + t * 4 + k // 2] for k in range(8)]
+        x = jnp.concatenate([xq[i] for i in held] + [xd[i] for i in held], 0)
         near = kk[pl.ds(s * MAXLEN, keys), :]
         both = nt(x, near)
         i = lax.broadcasted_iota(jnp.int32, (128, 1), 0)
@@ -665,156 +703,170 @@
 
     keys_out = net.group()
 
-    def key_sum(s):
+    def key_sum(s, part):
         def rows(start, count):
-            return pl.ds(s * 512 + start, count)
+            return pl.ds(s * 512 + part * 256 + start, count)
 
         return Scatter(
             net, keys_out, n, to,
-            lambda i, h: dkv.at[i, rows(h * 256, 256)],
-            rdkv.at[0, rows(0, 512)], (rdkv.at[0, rows(0, 256)], rdkv.at[0, rows(256, 256)]),
-            rdkv.at[pl.ds(1, 2), rows(0, 512)],
-            lambda h: rdkv.at[1, rows(h * 256, 256)],
-            lambda h: rdkv.at[2, rows(h * 256, 256)],
+            lambda i, h: dkv.at[i, rows(h * 128, 128)],
+            rdkv.at[0, rows(0, 256)], (rdkv.at[0, rows(0, 128)], rdkv.at[0, rows(128, 128)]),
+            rdkv.at[pl.ds(1, 2), rows(0, 256)],
+            lambda h: rdkv.at[1, rows(h * 128, 128)],
+            lambda h: rdkv.at[2, rows(h * 128, 128)],
         )
 
-    def weight_f(i, _):
-        cs = pl.ds(aligned(i * COLS, COLS), COLS)
-        sum_f[:, cs] = dot(hidden[...], g[:, cs]).astype(BF16)
-        return 0
-
-    kv_sum = [key_sum(0), key_sum(1)]
-    for s in range(2):
-        kv_ring[s].finish()
-        repeat(16, 4, lambda i, s=s: gather_keys(i + 16 * s))
-        for t in (3, 2, 1, 0):
-            attend(s, t)
-            if (s, t) == (1, 2):
-                kv_sum[0].step()
-            if (s, t) == (0, 2):
-                d_ring.forward()
-
-        def turn_keys(i, s=s):
-            t = dkvt[s, :, pl.ds(aligned(i * BLOCK, BLOCK), BLOCK)].T.astype(BF16)
+    def turn_keys(s, h):
+        for i in range(8 * h, 8 * h + 8):
+            t = dkvt[s, :, i * BLOCK : (i + 1) * BLOCK].T.astype(BF16)
             for m in range(4):
-                dkv[m, pl.ds(aligned(s * 512 + i * PART, PART), PART), :] = t[m * PART : (m + 1) * PART]
-
-        repeat(16, 4, turn_keys)
-        kv_sum[s].start()
+                dkv[m, s * 512 + i * PART : s * 512 + (i + 1) * PART, :] = t[m * PART : (m + 1) * PART]
+
+    kv_sum = [key_sum(0, 1), key_sum(0, 0), key_sum(1, 1), key_sum(1, 0)]
+    kv_ring[0].finish()
+    kv_ring[1].finish()
+    repeat(32, 4, gather_keys)
+    attend(0, 3)
+    attend(0, 2)
+    turn_keys(0, 1)
+    kv_sum[0].start()
+    attend(0, 1)
+    attend(0, 0)
+    turn_keys(0, 0)
+    kv_sum[1].start()
+    attend(1, 3)
+    attend(1, 2)
+    turn_keys(1, 1)
+    kv_sum[2].start()
+    attend(1, 1)
+    attend(1, 0)
+    turn_keys(1, 0)
+    kv_sum[3].start()
+    kv_sum[0].step()
+    kv_sum[1].step()
+
+    def unrope(s):
+        x = od[pl.ds(s * 32, 32)].reshape(512, 128)
+        od[pl.ds(s * 32, 32)] = (x * cosine[...].reshape(512, 128) - swap(x) * sine[...].reshape(512, 128)).reshape(32, 16, 128)
+
+    unrope(0)
+    unrope(1)
+
+    def place(i):
+        dpre[pl.ds(aligned(i * 16, 16), 16), 384:512] = od[there[2, i]].astype(BF16)
+
+    repeat(64, 8, place)
+
+    def dln_tile(start, cs):
+        r = pl.ds(start, 256)
+        return dot(dpre[r, 0:448], w[0:448, cs])
+
+    def branch_tile(start, cs):
+        r = pl.ds(start, 256)
+        return dot(hb[r, :], wm[0:256, cs]) + dot(dpre[r, 384:512], wmo[:, cs])
+
+    branch = WideScatter(net, branch_tile, out_1, got_1, acc_1, r1_1, r2_1, y, z, c, n)
+    dln = WideScatter(net, dln_tile, out_2, got_2, acc_2, r1_2, r2_2, y, z, c, n)
     d_ring.finish()
+    branch.exchange()
+    kv_sum[2].step()
 
     def grad_units(i, _):
         r = pl.ds(aligned(i * 512, 512), 512)
         dpre[r, 0:256] = (nt(g[r, :], wm[0:256, :]) * slope[r, :]).astype(BF16)
         return 0
 
-    def unrope(i):
-        tab = pl.ds(aligned((i % 32) * 16, 16), 16)
-        x = od[i]
-        od[i] = x * cosine[tab, :] - swap(x) * sine[tab, :]
-
-    repeat(64, 8, unrope)
-
-    def place(i):
-        dpre[pl.ds(aligned(i * 16, 16), 16), 384:512] = od[there[2, i]].astype(BF16)
-
-    repeat(64, 8, place)
-
-    def dln_tile(start, cs):
-        r = pl.ds(start, 256)
-        return dot(dpre[r, 0:448], w[0:448, cs])
-
-    def branch_tile(start, cs):
-        r = pl.ds(start, 256)
-        return dot(hb[r, :], wm[0:256, cs]) + dot(dpre[r, 384:512], wmo[:, cs])
-
-    branch = WideScatter(net, branch_tile, out_1, got_1, acc_1, r1_1, r2_1, y, z, c, n)
-    dln = WideScatter(net, dln_tile, out_2, got_2, acc_2, r1_2, r2_2, y, z, c, n)
-    branch.exchange()
-    kv_sum[1].step()
     lax.fori_loop(0, 2, grad_units, 0)
 
-    def unrope_keys(i):
-        tab = pl.ds(aligned((i % 32) * 16, 16), 16)
-        r = pl.ds(aligned(i * 16, 16), 16)
+    kv_sum[3].step()
+    trans[...] = dpre[:, 0:256].T
+
+    def weight_u(i, _):
+        cs = pl.ds(aligned(i * 1024, 1024), 1024)
+        sum_u[:, cs] = dot(trans[...], ln[:, cs]).astype(BF16)
+        return 0
+
+    lax.fori_loop(0, 2, weight_u, 0)
+    u_sum.start()
+    def unrope_keys(s):
+        r = pl.ds(s * 512, 512)
         x = dkv[n, r, :].astype(F32) + (rdkv[1, r, :].astype(F32) + rdkv[2, r, :].astype(F32))
-        dkvp[i] = x * cosine[tab, :] - swap(x) * sine[tab, :]
+        dkvp[pl.ds(s * 32, 32)] = (x * cosine[...].reshape(512, 128) - swap(x) * sine[...].reshape(512, 128)).reshape(32, 16, 128)
 
     kv_sum[0].finish()
-    repeat(32, 8, unrope_keys)
+    kv_sum[1].finish()
+    unrope_keys(0)
     branch.start()
-    kv_sum[1].finish()
-    repeat(32, 8, lambda i: unrope_keys(i + 32))
+    kv_sum[2].finish()
+    kv_sum[3].finish()
+    unrope_keys(1)
 
     def place_keys(i):
         dpre[pl.ds(aligned(i * 16, 16), 16), 256:384] = dkvp[there[2, i]].astype(BF16)
 
     repeat(64, 8, place_keys)
     dln.exchange()
-    lax.fori_loop(0, 4, weight_f, 0)
-    f_sum.start()
+    trans[...] = dpre[:, 256:512].T
+
+    def weight_l(i, _):
+        cs = pl.ds(aligned(i * 1024, 1024), 1024)
+        sum_l[0:192, cs] = dot(trans[0:192, :], ln[:, cs]).astype(BF16)
+        sum_l[192:256, cs] = dot(trans[192:256, :], g[:, cs]).astype(BF16)
+        return 0
+
+    lax.fori_loop(0, 2, weight_l, 0)
+    l_sum.start()
     branch.step(2)
     branch.step(1)
     dln.start()
     branch.step(3)
     branch.step(0)
-    trans[...] = dpre[:, 0:256].T
-
-    def weight_u(i, _):
-        cs = pl.ds(aligned(i * COLS, COLS), COLS)
-        sum_u[:, cs] = dot(trans[...], ln[:, cs]).astype(BF16)
-        return 0
-
-    lax.fori_loop(0, 4, weight_u, 0)
-    u_sum.start()
-    dln.step(2)
-    dln.step(1)
-    branch.hand_on(2)
-    branch.hand_on(1)
-    dln.step(3)
-    dln.step(0)
     f_sum.step()
-    trans[...] = dpre[:, 256:512].T
-
-    def weight_l(i, _):
-        cs = pl.ds(aligned(i * COLS, COLS), COLS)
-        sum_l[0:192, cs] = dot(trans[0:192, :], ln[:, cs]).astype(BF16)
-        sum_l[192:256, cs] = dot(trans[192:256, :], g[:, cs]).astype(BF16)
-        return 0
-
-    lax.fori_loop(0, 4, weight_l, 0)
-    l_sum.start()
-    dln.hand_on(2)
-    dln.hand_on(1)
-    dln.hand_on(3)
-    dln.second_step()
-    dln.hand_on(0)
-    branch.hand_on(3)
-    branch.second_step()
-    branch.hand_on(0)
+    for j in (2, 1, 3, 0):
+        dln.step(j)
+    for j in (2, 1, 3, 0):
+        branch.hand_on(j)
     u_sum.step()
+
+    def norm_sums(p, i, cs, v):
+        column[0:1, cs] += jnp.sum(v * hats[4 * p + i, :, cs], 0, keepdims=True)
+        column[1:2, cs] += jnp.sum(v, 0, keepdims=True)
+
+    column[...] = jnp.zeros((8, D), F32)
+    net.arrived(hats.at[pl.ds(0, 6)], hats_in)
+    for j in (2, 1, 3, 0):
+        dln.hand_on(j, norm_sums)
+    norm_out, norm_in, final_out, final_in, all_out, all_in = net.group(), net.slot(), net.group(), net.slot(), net.group(), net.slot()
+    for m in range(4):
+        for k in range(2):
+            for i in range(4):
+                ssend[m, 4 * k + i : 4 * k + i + 1, :] = column[k : k + 1, m * COLS + i * 128 : m * COLS + i * 128 + 128]
+    chip = y * 4 + z
+    wrecv[chip] = ssend[...]
+    for p in other_chips(y, z, c):
+        net.copy(ssend, wrecv.at[chip], (p, n), norm_out, norm_in)
     sums = jnp.sum(dpre[...].astype(F32), 0, keepdims=True)
     for i in range(4):
         brecv[n, i : i + 1, :] = sums[:, i * 128 : i * 128 + 128]
     small_out, small_in, branch_out, branch_in = net.group(), net.slot(), net.group(), net.slot()
     for j in (1, 3, 2):
         net.copy(brecv.at[n], brecv.at[n], to((n + j) % 4), small_out, small_in)
-    dln.finish()
-
+    l_sum.step()
+    branch.finish()
     for i in range(2):
         for h in range(2):
-            csend[i * 16 : (i + 1) * 16, h * 1024 : (h + 1) * 1024] = dln.result(i, h)
-    grad = csend[...]
-    sums = (jnp.sum(grad * xhat[...], 0, keepdims=True), jnp.sum(grad, 0, keepdims=True))
-    for m in range(4):
-        for k in range(2):
-            for i in range(4):
-                ssend[m, 4 * k + i : 4 * k + i + 1, :] = sums[k][:, m * COLS + i * 128 : m * COLS + i * 128 + 128]
-    srecv[n] = ssend[n]
-    norm_out, norm_in, final_out, final_in, all_out, all_in = net.group(), net.slot(), net.group(), net.slot(), net.group(), net.slot()
+            cs = slice(h * 1024, (h + 1) * 1024)
+            bsend[i * 16 : (i + 1) * 16, cs] = branch.result(i, cs).astype(BF16)
+    bfin[share(n), :] = bsend[:, my_cols]
     for j in (1, 3, 2):
         m = (n + j) % 4
-        net.copy(ssend.at[m], srecv.at[n], to(m), norm_out, norm_in)
+        net.copy(bsend.at[:, w_cols(m)], bfin.at[share(n)], to(m), branch_out, branch_in)
+    dln.finish()
+
+    for i in range(2):
+        for h in range(2):
+            cs = slice(h * 1024, (h + 1) * 1024)
+            csend[i * 16 : (i + 1) * 16, cs] = dln.result(i, cs)
     for i in range(16):
         cs = slice(i * 128, (i + 1) * 128)
         csend[:, cs] = csend[:, cs] * gbs[i // 4, i % 4 : i % 4 + 1, :]
@@ -824,35 +876,40 @@
     x = xs[...].astype(F32)
     mean = jnp.sum(x, 1, keepdims=True) / D
     var = jnp.sum(x * x, 1, keepdims=True) / D - mean * mean
-    csend[...] = lax.rsqrt(var + EPS) * (grad - first - xhat[...] * second)
-    cfin[share(n), :] = csend[:, my_cols]
+    clow[...] = (lax.rsqrt(var + EPS) * (grad - first - xhat[...] * second)).astype(BF16)
+    cfin[share(n), :] = clow[:, my_cols]
     for j in (1, 3, 2):
         m = (n + j) % 4
-        net.copy(csend.at[:, w_cols(m)], cfin.at[share(n)], to(m), final_out, final_in)
-    net.arrived(srecv.at[pl.ds(0, 3)], norm_in)
-    wrecv[me] = (srecv[0] + srecv[1]) + (srecv[2] + srecv[3])
-    for p in wide_peers(y, z, c):
-        net.copy(wrecv.at[me], wrecv.at[me], (p, n), all_out, all_in)
-    l_sum.step()
-    branch.finish()
-    for i in range(2):
-        for h in range(2):
-            bsend[i * 16 : (i + 1) * 16, h * 1024 : (h + 1) * 1024] = branch.result(i, h).astype(BF16)
-    bfin[share(n), :] = bsend[:, my_cols]
-    for j in (1, 3, 2):
+        net.copy(clow.at[:, w_cols(m)], cfin.at[share(n)], to(m), final_out, final_in)
+    net.arrived(wrecv.at[pl.ds(0, 15)], norm_in)
+    nsum[...] = jnp.sum(wrecv[...], 0)
+    srecv[n * 2 + c] = nsum[n]
+    for j in (1, 3, 2, 0):
         m = (n + j) % 4
-        net.copy(bsend.at[:, w_cols(m)], bfin.at[share(n)], to(m), branch_out, branch_in)
+        for d in (0, 1) if j else (1,):
+            net.copy(nsum.at[m], srecv.at[n * 2 + c], (wide_of(y, z, (c + d) % 2), m), all_out, all_in)
+    outs = []
+
+    def give(x, to):
+        outs.append(pltpu.make_async_copy(x, to, local.at[1 + len(outs)]))
+        outs[-1].start()
+
     f_sum.finish()
     for h in range(2):
         grad_f[h * 144 : (h + 1) * 144, :] = f_sum.half(h)
+    v_512[2] = grad_f[256:257, :]
+    give(grad_f.at[pl.ds(0, 256)], o_f)
+    give(v_512.at[2], o_bo)
     u_sum.finish()
     for h in range(2):
-        grad_u[h * 128 : (h + 1) * 128, :] = u_sum.half(h)
+        grad_u[:, h * 128 : (h + 1) * 128] = u_sum.half(h).T
+    give(grad_u, o_u)
     l_sum.finish()
     for h in range(2):
         grad_l[h * 128 : (h + 1) * 128, :] = l_sum.half(h)
+    for i, x in enumerate((o_k, o_v, o_q, o_o)):
+        give(grad_l.at[pl.ds(64 * i, 64)], x)
     net.arrived(dpre.at[pl.ds(0, 96)], branch_in)
-    net.arrived(srecv.at[pl.ds(0, 3)], small_in)
     block = dealing[me]
     valid = block % (MAXLEN // BLOCK) * BLOCK + row < jnp.where(block < MAXLEN // BLOCK, lengths[0], lengths[1])
     valid = valid[:, 0:128]
@@ -860,11 +917,27 @@
         cs = slice(i * 128, i * 128 + 128)
         base = bfin[:, cs].astype(F32) + (b_o[i : i + 1, :].astype(F32) + b_d[i : i + 1, :].astype(F32))
         res[:, cs] = (tok[:, cs].astype(F32) + jnp.where(valid, base, 0.0)).astype(BF16)
-    small[...] = (brecv[0] + brecv[1]) + (brecv[2] + brecv[3])
+    give(res, o_res)
+    net.arrived(srecv.at[pl.ds(0, 3)], small_in)
+    sums = (brecv[0] + brecv[1]) + (brecv[2] + brecv[3])
+    v_256[:, 0:128] = sums[0:1]
+    v_256[:, 128:256] = sums[1:2]
+    v_64[0] = sums[2:3, 0:64]
+    v_64[1] = sums[2:3, 64:128]
+    v_64[2] = sums[3:4, 0:64]
+    give(v_256, o_bu)
+    for i, x in enumerate((o_bk, o_bv, o_bq)):
+        give(v_64.at[i], x)
     net.arrived(cfin.at[pl.ds(0, 96)], final_in)
-    ig[...] = cot[...].astype(F32) + cfin[...]
-    net.arrived(wrecv.at[pl.ds(0, 31)], all_in)
-    norm[...] = jnp.sum(wrecv[...], 0)
+    ig[...] = cot[...].astype(F32) + cfin[...].astype(F32)
+    give(ig, o_ig)
+    net.arrived(srecv.at[pl.ds(0, 7)], all_in)
+    sums = jnp.sum(srecv[...], 0)
+    for i in range(4):
+        v_512[0, :, i * 128 : i * 128 + 128] = sums[i : i + 1]
+        v_512[1, :, i * 128 : i * 128 + 128] = sums[4 + i : 5 + i]
+    give(v_512.at[0], o_gain)
+    give(v_512.at[1], o_bias)
 
     lg.drain()
     gg.drain()
@@ -879,14 +952,23 @@
     net.sent(srecv.at[pl.ds(0, 3)], gains_out)
     net.sent(srecv.at[pl.ds(0, 3)], small_out)
     net.sent(dpre.at[pl.ds(0, 96)], branch_out)
-    net.sent(srecv.at[pl.ds(0, 3)], norm_out)
+    net.sent(wrecv.at[pl.ds(0, 15)], norm_out)
     net.sent(cfin.at[pl.ds(0, 96)], final_out)
-    net.sent(wrecv.at[pl.ds(0, 31)], all_out)
+    net.sent(srecv.at[pl.ds(0, 7)], all_out)
+    net.sent(hats.at[pl.ds(0, 6)], hats_out)
+    for x in outs:
+        x.wait()
     assert (net.groups, net.slots) == (SENDS, ARRIVALS), (net.groups, net.slots)
 
 
+RESULTS = (
+    (BLOCK, COLS), (1, COLS), (1, COLS), (64, COLS), (1, 64), (64, COLS), (1, 64), (64, COLS), (1, 64), (64, COLS), (1, COLS),
+    (COLS, UNITS), (1, UNITS), (UNITS, COLS),
+)
+
+
 def call_block(*args):
-    vmem, anywhere = pl.BlockSpec(memory_space=pltpu.VMEM), pl.BlockSpec(memory_space=pl.ANY)
+    anywhere = pl.BlockSpec(memory_space=pl.ANY)
     shape = jax.ShapeDtypeStruct
 
     def buf(dtype, *size):
@@ -895,18 +977,29 @@
     wide = [buf(BF16, 512, D), buf(BF16, 512, D), buf(BF16, 512, D), buf(BF16, 2, 192, D), buf(BF16, 96, D)]
     return pl.pallas_call(
         block_kernel,
-        out_shape=(
-            shape((BLOCK, COLS), BF16),
-            shape((BLOCK, COLS), F32),
-            shape((256, COLS), F32),
-            shape((256, COLS), F32),
-            shape((288, COLS), F32),
-            shape((8, 128), F32),
-            shape((8, 128), F32),
-        ),
-        in_specs=[pl.BlockSpec(memory_space=pltpu.SMEM)] * 2 + [vmem] * 16 + [anywhere] * 2,
-        out_specs=(vmem,) * 7,
+        out_shape=(shape((BLOCK, COLS), BF16), *(shape(x, F32) for x in RESULTS)),
+        in_specs=[pl.BlockSpec(memory_space=pltpu.SMEM)] * 2 + [anywhere] * 18,
+        out_specs=(anywhere,) * 15,
         scratch_shapes=[
+            buf(BF16, BLOCK, COLS),
+            buf(BF16, BLOCK, COLS),
+            buf(BF16, COLS, UNITS),
+            buf(F32, 1, COLS),
+            buf(F32, 1, COLS),
+            buf(BF16, 1, 64),
+            buf(BF16, 1, 64),
+            buf(BF16, 1, 64),
+            buf(BF16, 4, 128),
+            buf(BF16, 2, 128),
+            buf(BF16, 4, 128),
+            buf(BF16, BLOCK, COLS),
+            buf(F32, BLOCK, COLS),
+            buf(F32, 256, COLS),
+            buf(F32, COLS, UNITS),
+            buf(F32, 288, COLS),
+            buf(F32, 3, 1, COLS),
+            buf(F32, 3, 1, 64),
+            buf(F32, 1, UNITS),
             buf(BF16, ROWS, D),
             buf(BF16, ROWS, D),
             buf(BF16, 704, D),
@@ -915,16 +1008,17 @@
             buf(BF16, PART, D),
             buf(F32, 4, 8, 128),
             buf(F32, PART, D),
-            buf(F32, 512, 128),
-            buf(F32, 512, 128),
-            buf(F32, 64, 16, 256),
+            buf(F32, 32, 16, 128),
+            buf(F32, 32, 16, 128),
+            buf(F32, 64, 16, 128),
+            buf(F32, 64, 16, 128),
             buf(F32, ROWS, UNITS),
             buf(BF16, ROWS, UNITS),
             buf(BF16, ROWS, 512),
-            buf(BF16, 4, ROWS, 128),
+            buf(BF16, 4, 64, 16, 128),
             buf(BF16, 2 * MAXLEN, 128),
-            buf(BF16, ROWS, 128),
-            buf(BF16, ROWS, 128),
+            buf(BF16, 64, 16, 128),
+            buf(BF16, 64, 16, 128),
             buf(F32, 64, 16, 128),
             buf(F32, 2, 128, MAXLEN),
             buf(BF16, 4, ROWS, 128),
@@ -944,61 +1038,56 @@
             buf(BF16, PART, D),
             buf(BF16, BLOCK, COLS),
             buf(F32, PART, D),
-            buf(F32, BLOCK, COLS),
+            buf(BF16, PART, D),
+            buf(BF16, BLOCK, COLS),
             buf(F32, 4, 8, 128),
+            buf(F32, 8, 8, 128),
             buf(F32, 4, 8, 128),
+            buf(F32, 16, 4, 8, 128),
             buf(F32, 4, 8, 128),
-            buf(F32, 32, 8, 128),
+            buf(F32, 8, 16, D),
+            buf(F32, 8, D),
             buf(F32, 1, COLS),
             buf(jnp.int32, 8, 128),
             pltpu.SMEM((8, 128), jnp.int32),
             buf(jnp.int32, 2, 8, MAXLEN),
             pltpu.SemaphoreType.DMA((SENDS,)),
             pltpu.SemaphoreType.DMA((ARRIVALS,)),
-            pltpu.SemaphoreType.DMA((3,)),
+            pltpu.SemaphoreType.DMA((18,)),
+            pltpu.SemaphoreType.DMA((18,)),
         ],
         compiler_params=pltpu.CompilerParams(collective_id=0, has_side_effects=True, vmem_limit_bytes=63 * 2**20),
     )(*args)
 
 
-def split_kernel(
-    res, ig, grad_l, grad_u, grad_f, small, norm,
-    res_o, ig_o, gain_o, bias_o, q_o, bq_o, k_o, bk_o, v_o, bv_o, o_o, bo_o, u_o, bu_o, f_o, bf_o,
-):
-    res_o[...] = res[...]
-    ig_o[...] = ig[...]
-    k_o[...] = grad_l[0:64, :]
-    v_o[...] = grad_l[64:128, :]
-    q_o[...] = grad_l[128:192, :]
-    o_o[...] = grad_l[192:256, :]
-    u_o[...] = grad_u[...].T
-    f_o[...] = grad_f[0:256, :]
-    for i in range(4):
-        gain_o[:, i * 128 : i * 128 + 128] = norm[i : i + 1, :]
-        bias_o[:, i * 128 : i * 128 + 128] = norm[4 + i : 5 + i, :]
-    bu_o[:, 0:128] = small[0:1, :]
-    bu_o[:, 128:256] = small[1:2, :]
-    bk_o[...] = small[2:3, 0:64]
-    bv_o[...] = small[2:3, 64:128]
-    bq_o[...] = small[3:4, 0:64]
-    bo_o[...] = grad_f[256:257, :]
-    bf_o[...] = grad_f[256:257, :]
-
-
-def call_split(*args):
-    vmem = pl.BlockSpec(memory_space=pltpu.VMEM)
-    head, vector = (64, COLS), (1, COLS)
-    sizes = [
-        (BLOCK, COLS), vector, vector, head, (1, 64), head, (1, 64), head, (1, 64), head, vector,
-        (COLS, UNITS), (1, UNITS), (UNITS, COLS), vector,
-    ]
+def relay_kernel(*refs):
+    given, taken, held, here, there = refs[:15], refs[15:31], refs[31:46], refs[46], refs[47]
+    order = sorted(range(15), key=lambda i: -given[i].size)
+    come = [pltpu.make_async_copy(given[i], held[i], here.at[i]) for i in range(15)]
+    go = [pltpu.make_async_copy(held[i], taken[i], there.at[i]) for i in range(15)]
+    go.append(pltpu.make_async_copy(held[11], taken[15], there.at[15]))
+    for i in order:
+        come[i].start()
+    for i in order:
+        come[i].wait()
+        go[i].start()
+        if i == 11:
+            go[15].start()
+    for x in go:
+        x.wait()
+
+
+def relay(arrays):
+    anywhere = pl.BlockSpec(memory_space=pl.ANY)
     return pl.pallas_call(
-        split_kernel,
-        out_shape=(jax.ShapeDtypeStruct((BLOCK, COLS), BF16), *(jax.ShapeDtypeStruct(s, F32) for s in sizes)),
-        in_specs=[vmem] * 7,
-        out_specs=(vmem,) * 16,
+        relay_kernel,
+        out_shape=tuple(jax.ShapeDtypeStruct(x.shape, x.dtype) for x in (*arrays, arrays[11])),
+        in_specs=[anywhere] * 15,
+        out_specs=(anywhere,) * 16,
+        scratch_shapes=[pltpu.VMEM(x.shape, x.dtype) for x in arrays]
+        + [pltpu.SemaphoreType.DMA((15,)), pltpu.SemaphoreType.DMA((16,))],
         compiler_params=pltpu.CompilerParams(vmem_limit_bytes=62 * 2**20),
-    )(*args)
+    )(*arrays)
 
 
 def on_device(
@@ -1006,7 +1095,7 @@
     w_fc1, b_fc1, w_fc2, b_fc2, cotangent, lengths, dealing,
 ):
     cosine, sine = (
-        np.ascontiguousarray(t.reshape(MAXLEN // BLOCK, 4, PART, 128).transpose(1, 0, 2, 3)).reshape(4, -1, 128)
+        np.ascontiguousarray(t.reshape(MAXLEN // BLOCK, 4, PART, 128).transpose(1, 0, 2, 3)).reshape(4, -1, 16, 128)
         for t in rope_tables()
     )
     out = call_block(
@@ -1015,7 +1104,7 @@
         b_fc1.reshape(-1, 128), b_fc2.reshape(-1, 128),
         jnp.asarray(cosine), jnp.asarray(sine),
     )
-    out = list(call_split(*out))
+    out = list(relay(out))
     for i in (4, 6, 8):
         out[i] = out[i].T
     for i in (2, 3, 5, 7, 9, 11, 13, 15):

time: 106 us -> 102 us (0.962)
  Pallas kernels: 106 us -> 101 us
    pallas_call x2, Pallas kernels: 106 us -> 101 us  [the longest x1 98.6 us: call_block(): pl.pallas_call(block_kernel, out_shape=(shape((BLOCK, COLS), BF16), *(sha...]
where the time goes in v5:
time: 102 us
  Pallas kernels  101 us (99%)
    pallas_call x1, Pallas kernels, call_block(): pl.pallas_call(block_kernel, out_shape=(shape((BLOCK, COLS), BF16), *(sha...  98.6 us
    pallas_call x1, Pallas kernels, relay(): pl.pallas_call(relay_kernel, out_shape=tuple((jax.ShapeDtypeStruct(x.shap...  2.61 us

profile of v5, /device:TPU:1, one launch (start us, length us, event | category | flops | bytes accessed | tf_op | source)
XLA Modules:
  0.0 102.0 jit_solution(9180900943405117916)
XLA Ops:
  0.7 98.6 %shard_map.315 = (bf16[128,512]{1,0:T(8,128)(2,1)}, f32[128,512]{1,0:T(8,128)}, f32[1,512]{1,0:T(1,128)}, f32[1,512]{1,0:T(1,128)}, f32[64,512]{1,0:T(8,128)}, /...) custom-call(s32[32]{0:T(128)} %dealing.1, ...), custom_call_target="tpu_custom_call" | custom-call | tf_op jit(solution)/shard_map/pallas_call | solution.py:978
  99.3 2.6 %shard_map.316 = (bf16[128,512]{1,0:T(8,128)(2,1)}, f32[128,512]{1,0:T(8,128)}, f32[1,512]{1,0:T(1,128)}, f32[1,512]{1,0:T(1,128)}, f32[64,512]{1,0:T(8,128)}, /...) custom-call(bf16[128,512]{1,0:T(8,128)(2,1)} %get-tuple-element.47.r, ...), custom_call_target="tpu_custom_call" | custom-call | tf_op jit(solution)/shard_map/pallas_call | solution.py:1082

commit v6 on v5

--- a/solution.py
+++ b/solution.py
@@ -649,12 +649,12 @@
         return 0
 
     kv_ring[0].forward()
-    d_ring.forward()
     o_ring.finish()
     wmo[64:128, :] = wm[256:320, :]
     for j in (0, 3, 1, 2):
         gg.far_two(j)
     kv_ring[1].forward()
+    d_ring.forward()
 
     gg.finish()
     hats_out, hats_in = net.group(), net.slot()
@@ -664,7 +664,6 @@
         net.copy(xhat.at[pl.ds(0, 16)], hats.at[y], (wide_of((y + d) % 4, z, c), n), hats_out, hats_in)
         net.copy(xhat.at[pl.ds(16, 16)], hats.at[4 + z], (wide_of(y, (z + d) % 4, c), n), hats_out, hats_in)
     lax.fori_loop(0, 2, weight_f, 0)
-    f_sum.start()
 
     def grad_o(i, _):
         r = pl.ds(aligned(i * 512, 512), 512)
@@ -725,6 +724,7 @@
     kv_sum = [key_sum(0, 1), key_sum(0, 0), key_sum(1, 1), key_sum(1, 0)]
     kv_ring[0].finish()
     kv_ring[1].finish()
+    f_sum.start()
     repeat(32, 4, gather_keys)
     attend(0, 3)
     attend(0, 2)
@@ -742,8 +742,6 @@
     attend(1, 0)
     turn_keys(1, 0)
     kv_sum[3].start()
-    kv_sum[0].step()
-    kv_sum[1].step()
 
     def unrope(s):
         x = od[pl.ds(s * 32, 32)].reshape(512, 128)
@@ -769,7 +767,8 @@
     dln = WideScatter(net, dln_tile, out_2, got_2, acc_2, r1_2, r2_2, y, z, c, n)
     d_ring.finish()
     branch.exchange()
-    kv_sum[2].step()
+    kv_sum[0].step()
+    kv_sum[1].step()
 
     def grad_units(i, _):
         r = pl.ds(aligned(i * 512, 512), 512)
@@ -778,7 +777,9 @@
 
     lax.fori_loop(0, 2, grad_units, 0)
 
+    kv_sum[2].step()
     kv_sum[3].step()
+    branch.start()
     trans[...] = dpre[:, 0:256].T
 
     def weight_u(i, _):
@@ -796,7 +797,6 @@
     kv_sum[0].finish()
     kv_sum[1].finish()
     unrope_keys(0)
-    branch.start()
     kv_sum[2].finish()
     kv_sum[3].finish()
     unrope_keys(1)
@@ -806,6 +806,8 @@
 
     repeat(64, 8, place_keys)
     dln.exchange()
+    for j in (2, 1, 3, 0):
+        branch.step(j)
     trans[...] = dpre[:, 256:512].T
 
     def weight_l(i, _):
@@ -816,11 +818,7 @@
 
     lax.fori_loop(0, 2, weight_l, 0)
     l_sum.start()
-    branch.step(2)
-    branch.step(1)
     dln.start()
-    branch.step(3)
-    branch.step(0)
     f_sum.step()
     for j in (2, 1, 3, 0):
         dln.step(j)

time: 102 us -> 101 us (level)
    pallas_call x1, Pallas kernels: 98.6 us -> 97.4 us  [call_block(): pl.pallas_call(block_kernel, out_shape=(shape((BLOCK, COLS), BF16), *(sha...]
where the time goes in v6:
time: 101 us
  Pallas kernels  100 us (99%)
    pallas_call x1, Pallas kernels, call_block(): pl.pallas_call(block_kernel, out_shape=(shape((BLOCK, COLS), BF16), *(sha...  97.4 us
    pallas_call x1, Pallas kernels, relay(): pl.pallas_call(relay_kernel, out_shape=tuple((jax.ShapeDtypeStruct(x.shap...  2.61 us

profile of v6, /device:TPU:1, one launch (start us, length us, event | category | flops | bytes accessed | tf_op | source)
XLA Modules:
  0.0 100.8 jit_solution(12696574351514314089)
XLA Ops:
  0.7 97.4 %shard_map.315 = (bf16[128,512]{1,0:T(8,128)(2,1)}, f32[128,512]{1,0:T(8,128)}, f32[1,512]{1,0:T(1,128)}, f32[1,512]{1,0:T(1,128)}, f32[64,512]{1,0:T(8,128)}, /...) custom-call(s32[32]{0:T(128)} %dealing.1, ...), custom_call_target="tpu_custom_call" | custom-call | tf_op jit(solution)/shard_map/pallas_call | solution.py:976
  98.0 2.6 %shard_map.316 = (bf16[128,512]{1,0:T(8,128)(2,1)}, f32[128,512]{1,0:T(8,128)}, f32[1,512]{1,0:T(1,128)}, f32[1,512]{1,0:T(1,128)}, f32[64,512]{1,0:T(8,128)}, /...) custom-call(bf16[128,512]{1,0:T(8,128)(2,1)} %get-tuple-element.47.r, ...), custom_call_target="tpu_custom_call" | custom-call | tf_op jit(solution)/shard_map/pallas_call | solution.py:1080

commit v7 on v6

--- a/solution.py
+++ b/solution.py
@@ -808,6 +808,7 @@
     dln.exchange()
     for j in (2, 1, 3, 0):
         branch.step(j)
+    dln.start()
     trans[...] = dpre[:, 256:512].T
 
     def weight_l(i, _):
@@ -818,7 +819,6 @@
 
     lax.fori_loop(0, 2, weight_l, 0)
     l_sum.start()
-    dln.start()
     f_sum.step()
     for j in (2, 1, 3, 0):
         dln.step(j)

time: 101 us -> 100 us (0.990)
  no operation moved by 1% of the time
where the time goes in v7:
time: 100 us
  Pallas kernels  99.4 us (99%)
    pallas_call x1, Pallas kernels, call_block(): pl.pallas_call(block_kernel, out_shape=(shape((BLOCK, COLS), BF16), *(sha...  96.8 us
    pallas_call x1, Pallas kernels, relay(): pl.pallas_call(relay_kernel, out_shape=tuple((jax.ShapeDtypeStruct(x.shap...  2.61 us

profile of v7, /device:TPU:1, one launch (start us, length us, event | category | flops | bytes accessed | tf_op | source)
XLA Modules:
  0.0 100.2 jit_solution(12537011487635970278)
XLA Ops:
  0.7 96.8 %shard_map.315 = (bf16[128,512]{1,0:T(8,128)(2,1)}, f32[128,512]{1,0:T(8,128)}, f32[1,512]{1,0:T(1,128)}, f32[1,512]{1,0:T(1,128)}, f32[64,512]{1,0:T(8,128)}, /...) custom-call(s32[32]{0:T(128)} %dealing.1, ...), custom_call_target="tpu_custom_call" | custom-call | tf_op jit(solution)/shard_map/pallas_call | solution.py:976
  97.5 2.6 %shard_map.316 = (bf16[128,512]{1,0:T(8,128)(2,1)}, f32[128,512]{1,0:T(8,128)}, f32[1,512]{1,0:T(1,128)}, f32[1,512]{1,0:T(1,128)}, f32[64,512]{1,0:T(8,128)}, /...) custom-call(bf16[128,512]{1,0:T(8,128)(2,1)} %get-tuple-element.47.r, ...), custom_call_target="tpu_custom_call" | custom-call | tf_op jit(solution)/shard_map/pallas_call | solution.py:1080
